TPU v7x, 128 devices: a whole 4x4x4 slice. The times are simulated.
128 devices in a mesh: dp: 8 (over x, z_hi), vocab: 16 (over z_lo, y, core).
Axes of the slice: x: 4, y: 4, z: 4 (z_hi: 2, z_lo: 2; z = z_hi * 2 + z_lo), core: 2. Of those that a mesh axis runs over, the one named last changes fastest.
Arguments:
- query_hidden: bfloat16 [16, 128, 4096], P('dp', None, 'vocab'), may hold values from -144 to 144
- passage_hidden: bfloat16 [16, 256, 4096], P('dp', None, 'vocab'), may hold values from -144 to 144
- head_weight: bfloat16 [4096, 32768], P(None, 'vocab'), may hold values from -6 to 6
- query_mask: int32 [16, 128], P('dp'), may hold values from 0 to 1, as said below
- passage_mask: int32 [16, 256], P('dp'), may hold values from 0 to 1, as said below
- positive: int32 [16], replicated, may hold values from 0 to 15
Outputs:
- grad_query_hidden: bfloat16 [16, 128, 4096], P('dp', None, 'vocab')
- grad_passage_hidden: bfloat16 [16, 256, 4096], P('dp', None, 'vocab')
- query_loss: float32 [16], P('dp')
Inputs may be any that keep to these rules, and one draw needn't show every extreme that they name: `query_mask`: the live tokens of each query are a prefix of 32 to 128 positions. `passage_mask`: the live tokens of each passage are a prefix of 64 to 256 positions.
All inputs are finite; a program needn't handle non-finite values.
Results may differ from a plain program's by a relative error of at most 0.0095.
Values may be sent and summed in bfloat16 or wider, within the bound.
No kernel may reach another device: no remote copies, remote signals or barrier semaphores. Data moves between devices by JAX's collectives and lax.ppermute only.
A program may use at most 128 MiB of HBM per device.

v0:
```python
import jax
import jax.numpy as jnp
from jax import lax
from jax.sharding import PartitionSpec as P

normalizer_sharpness = 0.2
score_div = 16.0
loss_scale = 65536.0


def pooling_row_block(lexicon_projection_lines, live):
    divided_similarity_matrix = lexicon_projection_lines / normalizer_sharpness
    live_rows = live[:, :, None] > 0
    largest_element = jnp.max(jnp.where(live_rows, divided_similarity_matrix, -1e30), axis=1)
    expo = jnp.where(
        live_rows, jnp.exp(divided_similarity_matrix - largest_element[:, None, :]), 0.0
    )
    cumulative_accumulator = jnp.sum(expo, axis=1)
    softened_rectifier_output = normalizer_sharpness * (
        largest_element + jnp.log(cumulative_accumulator)
    )
    return (softened_rectifier_output, expo / cumulative_accumulator[:, None, :])


def exact_dot(left, right):
    return jnp.dot(left, right, precision=lax.Precision.HIGHEST, preferred_element_type=jnp.float32)


def loss_and_grad(scores, targets, total_queries):
    largest_element = jnp.max(scores, axis=1)
    lse = largest_element + jnp.log(jnp.sum(jnp.exp(scores - largest_element[:, None]), axis=1))
    picked = (targets[:, None] == jnp.arange(scores.shape[1], dtype=jnp.int32)[None, :]).astype(
        jnp.float32
    )
    losses = lse - jnp.sum(scores * picked, axis=1)
    probs = jnp.exp(scores - lse[:, None])
    return (losses, (probs - picked) * (loss_scale / total_queries))


def token_grads(dpooled, softened_rectifier_output, share):
    dsmooth = dpooled * jnp.where(
        softened_rectifier_output > 0,
        1.0 / (1.0 + jnp.maximum(softened_rectifier_output, 0.0)),
        0.0,
    )
    dlogits = (share * dsmooth[:, None, :]).astype(jnp.bfloat16)
    return dlogits.reshape(dlogits.shape[0] * dlogits.shape[1], dlogits.shape[2])


def on_device(query_hidden, passage_hidden, head_weight, query_mask, passage_mask, positive):
    q_count, q_len, width_part = query_hidden.shape
    p_count, p_len, _ = passage_hidden.shape
    columns = head_weight.shape[1]
    split = q_count * q_len
    tokens = jnp.concatenate(
        [
            query_hidden.reshape(split, width_part),
            passage_hidden.reshape(p_count * p_len, width_part),
        ],
        axis=0,
    )
    w_rows = head_weight
    lexicon_projection_lines = jnp.dot(
        lax.all_gather(tokens, "vocab", axis=1, tiled=True),
        w_rows,
        preferred_element_type=jnp.float32,
    )
    q_smooth, q_share = pooling_row_block(
        lexicon_projection_lines[:split].reshape(q_count, q_len, columns), query_mask
    )
    p_smooth, p_share = pooling_row_block(
        lexicon_projection_lines[split:].reshape(p_count, p_len, columns), passage_mask
    )
    q_pooled = jnp.log1p(jnp.maximum(q_smooth, 0.0))
    p_pooled = jnp.log1p(jnp.maximum(p_smooth, 0.0))
    group = lax.axis_index("dp")
    total_queries = positive.shape[0]
    p_every = lax.all_gather(p_pooled, "dp", axis=0, tiled=True)
    scores = lax.psum(exact_dot(q_pooled, p_every.T), "vocab") / score_div
    targets = lax.dynamic_slice_in_dim(positive, group * q_count, q_count, 0)
    query_loss, dscores = loss_and_grad(scores, targets, total_queries)
    dq_pooled = exact_dot(dscores, p_every) / score_div
    grad_passage_summary = lax.psum_scatter(
        exact_dot(dscores.T, q_pooled) / score_div, "dp", scatter_dimension=0, tiled=True
    )
    dlogits = jnp.concatenate(
        [
            token_grads(dq_pooled, q_smooth, q_share),
            token_grads(grad_passage_summary, p_smooth, p_share),
        ],
        axis=0,
    )
    w_rows = head_weight
    own_grad = lax.psum_scatter(
        lax.dot_general(
            w_rows, dlogits, (((1,), (1,)), ((), ())), preferred_element_type=jnp.float32
        ),
        "vocab",
        scatter_dimension=0,
        tiled=True,
    ).T
    own_grad = own_grad.astype(jnp.bfloat16)
    grad_query_hidden = own_grad[:split].reshape(q_count, q_len, width_part)
    grad_passage_hidden = own_grad[split:].reshape(p_count, p_len, width_part)
    return (grad_query_hidden, grad_passage_hidden, query_loss)


def solution(mesh):
    return jax.shard_map(
        on_device,
        mesh=mesh,
        in_specs=(
            P("dp", None, "vocab"),
            P("dp", None, "vocab"),
            P(None, "vocab"),
            P("dp", None),
            P("dp", None),
            P(),
        ),
        out_specs=(P("dp", None, "vocab"), P("dp", None, "vocab"), P("dp")),
        check_vma=False,
    )
```

profile of v0, /device:TPU:0, one launch (start us, length us, event | category | flops | bytes accessed | tf_op | source)
XLA Modules:
  0.0 344.2 jit_solution(16631525663870407592)
XLA Ops:
  7.2 0.0 all-gather.3.cloned.1.call-start
  7.2 1.8 pad_maximum_fusion
  9.0 0.0 all-gather.3.cloned.1.call-update
  9.0 0.0 all-reduce.3.cloned.1.call-start
  9.1 0.7 broadcast_compare_fusion
  9.8 1.2 dynamic-slice
  11.7 0.7 dynamic_slice.3
  12.4 0.7 broadcast_compare_fusion.1
  13.1 0.7 fusion.29
  13.8 50.4 %all-gather.3.cloned.1.call-done = bf16[768,4096]{1,0:T(8,128)(2,1)} async-done(((bf16[768,256]{1,0:T(8,128)(2,1)}), bf16[768,4096]{1,0:T(8,128)(2,1)}) %all-gather.3.cloned.1.call-update) | async-done | bytes 6291472 | tf_op jit(solution)/shard_map/all_gather | solution.py:64
  64.2 17.7 %fusion.23 = f32[768,2048]{1,0:T(8,128)S(1)} fusion(bf16[768,4096]{1,0:T(8,128)(2,1)} %all-gather.3.cloned.1.call-done, bf16[4096,2048]{1,0:T(8,128)(2,1)} %param.8), kind=kOutput, calls=%fused_computation.53 | convolution fusion | flops 12884901888 | bytes 29360128 | tf_op jit(solution)/shard_map/dot_general | solution.py:63
  81.9 0.0 copy-start
  81.9 0.6 select_reduce_fusion.1
  82.5 0.3 select_reduce_fusion.3
  82.9 0.5 select_reduce_fusion.2
  83.3 1.2 copy-done
  84.6 0.9 select_reduce_fusion
  85.6 34.2 %all-gather = f32[8,2,2048]{2,1,0:T(2,128)S(1)} all-gather(f32[1,2,2048]{2,1,0:T(2,128)S(1)} %log-plus-one_bitcast_fusion), channel_id=1, replica_groups=mesh['dp'=8,'vocab'=16] {'dp'}, dimensions={0}, use_global_device_ids=true | all-gather | bytes 147456 | tf_op jit(solution)/shard_map/all_gather | solution.py:78
  119.8 0.1 reshape.58
  119.9 0.2 fusion.12
  120.1 27.2 %psum.7 = f32[2,16]{1,0:T(2,128)S(1)} all-reduce(f32[2,16]{1,0:T(2,128)S(1)} %fusion.12), channel_id=1, replica_groups=mesh['dp'=8,'vocab'=16] {'vocab'}, use_global_device_ids=true, to_apply=%region_4.5 | all-reduce | flops 32 | bytes 256 | tf_op jit(solution)/shard_map/psum | solution.py:79
  147.3 0.1 fusion.18
  147.4 0.2 select_reduce_fusion.4
  147.7 0.5 fusion.22
  148.2 1.1 convolution_multiply_fusion
  149.3 0.0 all-reduce.3.cloned.1.call-update
  149.3 0.2 reduce-scatter.2.cloned.1.call-start
  149.5 0.3 fusion.6
  149.8 2.2 fusion.7
  152.0 79.7 %all-reduce.3.cloned.1.call-done = f32[16,2048]{1,0:T(8,128)} async-done(((f32[16,2048]{1,0:T(8,128)}), f32[16,2048]{1,0:T(8,128)}) %all-reduce.3.cloned.1.call-update) | async-done | bytes 131088
  231.6 0.9 fusion.10
  232.5 3.0 fusion
  235.5 19.4 %convolution_bitcast_fusion = f32[4096,768]{0,1:T(8,128)} fusion(bf16[4096,2048]{1,0:T(8,128)(2,1)} %param.8, bf16[512,2048]{1,0:T(8,128)(2,1)S(1)} %fusion, bf16[256,2048]{1,0:T(8,128)(2,1)S(1)} %fusion.7), kind=kOutput, calls=%fused_computation | convolution fusion | flops 12891193344 | bytes 32505856 | tf_op jit(solution)/shard_map/dot_general | solution.py:95
  254.9 0.0 reduce-scatter.2.cloned.1.call-update
  254.9 80.2 %reduce-scatter.2.cloned.1.call-done = f32[256,768]{0,1:T(8,128)} async-done(((f32[4096,768]{0,1:T(8,128)}), f32[256,768]{0,1:T(8,128)}) %reduce-scatter.2.cloned.1.call-update) | async-done | bytes 786448 | tf_op jit(solution)/shard_map/reduce_scatter | solution.py:94
  335.1 1.2 convert_bitcast_fusion
  336.3 0.7 slice.18
  337.0 0.7 slice.19
  (2 shorter events, 0.1 us)
Async XLA Ops:
  7.2 57.0 %all-gather.3.cloned.1.call-start = ((), (), s32[]{:S(2)}) async-start(), calls=%async_computation.1 | async-start | bytes 6684672 | tf_op jit(solution)/shard_map/all_gather | solution.py:64
  9.0 222.6 %all-reduce.3.cloned.1.call-start = ((), (), s32[]{:S(2)}) async-start(), calls=%async_computation.3 | async-start | bytes 262144
  81.9 2.7 copy-start
  149.3 185.8 %reduce-scatter.2.cloned.1.call-start = ((), (), s32[]{:S(2)}) async-start(), calls=%async_computation.2 | async-start | bytes 13369344 | tf_op jit(solution)/shard_map/reduce_scatter | solution.py:94
Sparse Core Ops, SparseCore 0:
  9.6 54.5 all-gather.2
  149.4 82.1 all-reduce.2
  255.0 80.0 reduce-scatter.1
where the time goes:
time: 345 us; the launch traced here: 344 us
  waiting for transfers between devices  210 us (61%)
  blocking collectives  61.4 us (18%)
  matrix products  38.7 us (11%)
  between operations  14.5 us (4%)
  other arithmetic  14.3 us (4%)
  local copies, waits for them, and re-layouts  4.7 us (1%)
    reduce_scatter x1, waiting for transfers between devices, on_device(): lax.psum_scatter(lax.dot_general(w_rows, dlogits, (((1,), (1,)), ((), ())...  80.2 us
    unnamed x4, waiting for transfers between devices  79.7 us
    all_gather x1, waiting for transfers between devices, on_device(): lax.all_gather(tokens, 'vocab', axis=1, tiled=True)  50.4 us
    all_gather x1, blocking collectives, on_device(): p_every = lax.all_gather(p_pooled, 'dp', axis=0, tiled=True)  34.2 us
    psum x1, blocking collectives, on_device(): scores = lax.psum(exact_dot(q_pooled, p_every.T), 'vocab') / score_div  27.2 us
    dot_general x1, matrix products, on_device(): lax.dot_general(w_rows, dlogits, (((1,), (1,)), ((), ())), preferred_elem...  19.4 us
    dot_general x1, matrix products, on_device(): jnp.dot(lax.all_gather(tokens, 'vocab', axis=1, tiled=True), w_rows, pref...  17.7 us
  transfers between devices with their start and end apart: 3, of which 3 were waited for; matrix products, arithmetic and copies ran while one was open for 2% of the time, Pallas kernels for 0%

commit v1 on v0

v1 whole, which is shorter than its diff:
```python
import functools

import jax
import jax.numpy as jnp
from jax import lax
from jax.experimental import pallas as pl
from jax.experimental.pallas import tpu as pltpu
from jax.sharding import PartitionSpec as P

SHARP = 0.2
DIV = 16.0
LOSS_SCALE = 65536.0
BF = jnp.bfloat16
F32 = jnp.float32
VLIM = 56 * 1024 * 1024
BLK = 256


def y_perm(k):
    return [(z * 8 + y * 2 + c, z * 8 + ((y + k) % 4) * 2 + c) for z in range(2) for y in range(4) for c in range(2)]


Z_SWAP = [(v, v ^ 8) for v in range(16)]
CORE_SWAP = [(v, v ^ 1) for v in range(16)]


def to_y(x, k):
    return lax.ppermute(x, "vocab", y_perm(k % 4))


def to_z(x):
    return lax.ppermute(x, "vocab", Z_SWAP)


def to_core(x):
    return lax.ppermute(x, "vocab", CORE_SWAP)


def to_x(x, k):
    return lax.ppermute(x, "dp", [(g, ((g // 2 + k) % 4) * 2 + g % 2) for g in range(8)])


def to_zhi(x):
    return lax.ppermute(x, "dp", [(g, g ^ 1) for g in range(8)])


def load_operands(copies, nk, bn, steps, idx, xrefs, w, xs, ws, xsem, wsem):
    j = pl.program_id(0)

    def x_copy(i):
        a, k, src, dst, n = copies[i]
        return pltpu.make_async_copy(
            xrefs[a].at[pl.ds(src, n), :], xs.at[pl.ds(dst, n), pl.ds(k * BLK, BLK)], xsem.at[i]
        )

    def w_copy(step, slot, k):
        row = pl.multiple_of(idx[k] * BLK, BLK)
        col = pl.multiple_of(step * bn, bn)
        return pltpu.make_async_copy(
            w.at[pl.ds(row, BLK), pl.ds(col, bn)], ws.at[slot, pl.ds(k * BLK, BLK), :], wsem.at[slot, k]
        )

    slot = lax.rem(j, 2)

    @pl.when(j == 0)
    def _():
        for k in range(nk):
            w_copy(0, 0, k).start()
        for i in range(len(copies)):
            x_copy(i).start()

    @pl.when(j + 1 < steps)
    def _():
        for k in range(nk):
            w_copy(j + 1, 1 - slot, k).start()

    @pl.when(j == 0)
    def _():
        for i in range(len(copies)):
            x_copy(i).wait()

    for k in range(nk):
        w_copy(j, slot, k).wait()
    return slot


def logits_kernel(copies, nk, nx, bn, steps, has_acc, idx, *refs):
    xrefs = refs[:nx]
    w = refs[nx]
    pos = nx + 1
    acc = None
    if has_acc:
        acc = refs[pos]
        pos += 1
    out, xs, ws, xsem, wsem = refs[pos:]
    slot = load_operands(copies, nk, bn, steps, idx, xrefs, w, xs, ws, xsem, wsem)
    res = jnp.dot(xs[...], ws[slot], preferred_element_type=F32)
    if has_acc:
        res = res + acc[...]
    out[...] = res


def logits_part(arrays, copies, idx, w, acc):
    rows = 768
    cols = w.shape[1]
    nk = idx.shape[0]
    bn = 512
    steps = cols // bn
    any_spec = pl.BlockSpec(memory_space=pl.ANY)
    blk = pl.BlockSpec((rows, bn), lambda j, *_: (0, j))
    ins = list(arrays) + [w] + ([acc] if acc is not None else [])
    return pl.pallas_call(
        functools.partial(logits_kernel, copies, nk, len(arrays), bn, steps, acc is not None),
        grid_spec=pltpu.PrefetchScalarGridSpec(
            num_scalar_prefetch=1,
            grid=(steps,),
            in_specs=[any_spec] * (len(arrays) + 1) + ([blk] if acc is not None else []),
            out_specs=blk,
            scratch_shapes=[
                pltpu.VMEM((rows, nk * BLK), BF),
                pltpu.VMEM((2, nk * BLK, bn), BF),
                pltpu.SemaphoreType.DMA((len(copies),)),
                pltpu.SemaphoreType.DMA((2, nk)),
            ],
        ),
        out_shape=jax.ShapeDtypeStruct((rows, cols), F32),
        compiler_params=pltpu.CompilerParams(vmem_limit_bytes=VLIM),
        name="logits_part",
    )(idx, *ins)


def pool_kernel(copies, nk, nx, bn, steps, seqs, idx, lens, *refs):
    xrefs = refs[:nx]
    w, acc, expo, stats, xs, ws, xsem, wsem = refs[nx:]
    slot = load_operands(copies, nk, bn, steps, idx, xrefs, w, xs, ws, xsem, wsem)
    logits = jnp.dot(xs[...], ws[slot], preferred_element_type=F32) + acc[...]
    smooth, sums = [], []
    for s, (start, n) in enumerate(seqs):
        part = logits[start : start + n] * (1.0 / SHARP)
        live = lax.broadcasted_iota(jnp.int32, (n, 1), 0) < lens[s]
        top = jnp.max(jnp.where(live, part, -1e30), axis=0, keepdims=True)
        e = jnp.where(live, jnp.exp(part - top), 0.0)
        total = jnp.sum(e, axis=0, keepdims=True)
        expo[pl.ds(start, n), :] = e
        smooth.append(SHARP * (top + jnp.log(total)))
        sums.append(total)
    stats[...] = jnp.concatenate(smooth + sums, axis=0)


def logits_pool(arrays, copies, idx, lens, w, acc, seqs):
    rows = 768
    cols = w.shape[1]
    nk = idx.shape[0]
    bn = 512
    steps = cols // bn
    any_spec = pl.BlockSpec(memory_space=pl.ANY)
    blk = pl.BlockSpec((rows, bn), lambda j, *_: (0, j))
    return pl.pallas_call(
        functools.partial(pool_kernel, copies, nk, len(arrays), bn, steps, seqs),
        grid_spec=pltpu.PrefetchScalarGridSpec(
            num_scalar_prefetch=2,
            grid=(steps,),
            in_specs=[any_spec] * (len(arrays) + 1) + [blk],
            out_specs=[blk, pl.BlockSpec((8, bn), lambda j, *_: (0, j))],
            scratch_shapes=[
                pltpu.VMEM((rows, nk * BLK), BF),
                pltpu.VMEM((2, nk * BLK, bn), BF),
                pltpu.SemaphoreType.DMA((len(copies),)),
                pltpu.SemaphoreType.DMA((2, nk)),
            ],
        ),
        out_shape=[jax.ShapeDtypeStruct((rows, cols), F32), jax.ShapeDtypeStruct((8, cols), F32)],
        compiler_params=pltpu.CompilerParams(vmem_limit_bytes=VLIM),
        name="logits_pool",
    )(idx, lens, *arrays, w, acc)


def exact_dot(a, b, dims):
    return lax.dot_general(a, b, (dims, ((), ())), precision=lax.Precision.HIGHEST, preferred_element_type=F32)


def gram_kernel(a, b, out):
    every = jnp.concatenate([a[...], b[...]], axis=0)
    out[...] = exact_dot(every, every, ((1,), (1,)))


def gram(a, b):
    n = a.shape[0] + b.shape[0]
    return pl.pallas_call(
        gram_kernel,
        out_shape=jax.ShapeDtypeStruct((n, n), F32),
        compiler_params=pltpu.CompilerParams(vmem_limit_bytes=VLIM),
        name="gram",
    )(a, b)


def nt_dot(a, b):
    return lax.dot_general(a, b, (((1,), (1,)), ((), ())), preferred_element_type=F32)


def first_grad_kernel(seqs, nk, total_queries, idx, parts, pa, pb, stats, picked, expo, w, dl, loss, *refs):
    outs = refs[:nk]
    es, ws, esem, wsem = refs[nk:]

    def e_copy(s):
        start, n = seqs[s]
        return pltpu.make_async_copy(expo.at[pl.ds(start, n), :], es.at[pl.ds(start, n), :], esem.at[s])

    def w_copy(k):
        row = pl.multiple_of(idx[k] * BLK, BLK)
        return pltpu.make_async_copy(w.at[pl.ds(row, BLK), :], ws.at[k], wsem.at[k])

    for s in range(len(seqs)):
        e_copy(s).start()
    for k in range(nk):
        w_copy(k).start()

    scores = parts[0]
    for i in range(1, parts.shape[0]):
        scores = scores + parts[i]
    scores = scores / DIV
    n = scores.shape[0]
    row = lax.broadcasted_iota(jnp.int32, (n, n), 0)
    col = lax.broadcasted_iota(jnp.int32, (n, n), 1)
    is_q = (row % 4) < 2
    is_p = (col % 4) >= 2
    masked = jnp.where(is_p, scores, -1e30)
    top = jnp.max(masked, axis=1, keepdims=True)
    lse = top + jnp.log(jnp.sum(jnp.where(is_p, jnp.exp(masked - top), 0.0), axis=1, keepdims=True))
    pick = picked[...]
    losses = lse - jnp.sum(scores * pick, axis=1, keepdims=True)
    loss[...] = jnp.broadcast_to(losses[:8], loss.shape)
    probs = jnp.where(is_p, jnp.exp(masked - lse), 0.0)
    dscores = jnp.where(is_q, (probs - pick) * (LOSS_SCALE / total_queries), 0.0)
    both = dscores + dscores.T
    every = jnp.concatenate([pa[...], pb[...]], axis=0)
    dpooled = exact_dot(both[:8], every, ((1,), (0,))) / DIV
    smooth = stats[0:4, :]
    gate = jnp.where(smooth > 0, 1.0 / (1.0 + jnp.maximum(smooth, 0.0)), 0.0)
    g = dpooled[:4] * gate / stats[4:8, :]
    for s, (start, n) in enumerate(seqs):
        e_copy(s).wait()
        dl[pl.ds(start, n), :] = (es[pl.ds(start, n), :] * g[s : s + 1, :]).astype(BF)
    for k in range(nk):
        w_copy(k).wait()
        outs[k][...] = nt_dot(dl[...], ws[k]).astype(outs[k].dtype)


def first_grad(idx, parts, pa, pb, stats, picked, expo, w, seqs, dtypes, total_queries):
    rows, cols = expo.shape
    nk = len(dtypes)
    vm = pl.BlockSpec(memory_space=pltpu.VMEM)
    any_spec = pl.BlockSpec(memory_space=pl.ANY)
    return pl.pallas_call(
        functools.partial(first_grad_kernel, seqs, nk, total_queries),
        in_specs=[pl.BlockSpec(memory_space=pltpu.SMEM)] + [vm] * 5 + [any_spec] * 2,
        out_specs=[vm] * (2 + nk),
        scratch_shapes=[
            pltpu.VMEM((rows, cols), F32),
            pltpu.VMEM((nk, BLK, cols), BF),
            pltpu.SemaphoreType.DMA((len(seqs),)),
            pltpu.SemaphoreType.DMA((nk,)),
        ],
        out_shape=[jax.ShapeDtypeStruct((rows, cols), BF), jax.ShapeDtypeStruct((8, 128), F32)]
        + [jax.ShapeDtypeStruct((rows, BLK), t) for t in dtypes],
        compiler_params=pltpu.CompilerParams(vmem_limit_bytes=VLIM),
        name="first_grad",
    )(idx, parts, pa, pb, stats, picked, expo, w)


def grad_kernel(nk, idx, dl, w, *refs):
    outs = refs[:nk]
    ws, wsem = refs[nk:]

    def w_copy(k):
        row = pl.multiple_of(idx[k] * BLK, BLK)
        return pltpu.make_async_copy(w.at[pl.ds(row, BLK), :], ws.at[k], wsem.at[k])

    for k in range(nk):
        w_copy(k).start()
    for k in range(nk):
        w_copy(k).wait()
        outs[k][...] = nt_dot(dl[...], ws[k]).astype(outs[k].dtype)


def grad_part(idx, dl, w, dtypes):
    rows, cols = dl.shape
    nk = len(dtypes)
    vm = pl.BlockSpec(memory_space=pltpu.VMEM)
    return pl.pallas_call(
        functools.partial(grad_kernel, nk),
        in_specs=[pl.BlockSpec(memory_space=pltpu.SMEM), vm, pl.BlockSpec(memory_space=pl.ANY)],
        out_specs=[vm] * nk,
        scratch_shapes=[pltpu.VMEM((nk, BLK, cols), BF), pltpu.SemaphoreType.DMA((nk,))],
        out_shape=[jax.ShapeDtypeStruct((rows, BLK), t) for t in dtypes],
        compiler_params=pltpu.CompilerParams(vmem_limit_bytes=VLIM),
        name="grad_part",
    )(idx, dl, w)


def on_device(query_hidden, passage_hidden, head_weight, query_mask, passage_mask, positive):
    q_count, q_len, width = query_hidden.shape
    p_count, p_len, _ = passage_hidden.shape
    w = head_weight
    split = q_count * q_len
    seqs = tuple((i * q_len, q_len) for i in range(q_count)) + tuple(
        (split + i * p_len, p_len) for i in range(p_count)
    )
    own = jnp.concatenate([query_hidden.reshape(split, width), passage_hidden.reshape(p_count * p_len, width)], axis=0)

    vocab = lax.axis_index("vocab")
    z, y, core = vocab // 8, (vocab // 2) % 4, vocab % 2

    def block(dy, dz):
        base = ((z + dz) % 2) * 8 + ((y + dy) % 4) * 2
        return [base + core, base + 1 - core]

    def index(*places):
        return jnp.stack([b for p in places for b in block(*p)]).astype(jnp.int32)

    x10, xm0, x01 = to_y(own, -1), to_y(own, 1), to_z(own)
    own_s = to_core(own)
    h = 384
    f1 = to_y(jnp.concatenate([x10[:h], x01[h:]], axis=0), -1)
    f2 = to_y(jnp.concatenate([x01[h:], xm0[h:]], axis=0), 1)
    f3 = to_z(jnp.concatenate([x10[:h], xm0[:h]], axis=0))
    near = [own, own_s] + [t for p in (x10, xm0, x01) for t in (p, to_core(p))]
    whole = tuple((i, i, 0, 0, 768) for i in range(8))
    acc = logits_part(near, whole, index((0, 0), (1, 0), (-1, 0), (0, 1)), w, None)
    g1 = to_y(f3[:256], -1)
    g2 = to_z(jnp.concatenate([f1[256:384], f2[384:512]], axis=0))
    g3 = to_y(f2[128:384], 1)
    mid = [t for p in (f1, f2, f3) for t in (p, to_core(p))]
    mid_copies = []
    for c in range(2):
        mid_copies += [
            (0 + c, 0 + c, 0, 0, h),
            (2 + c, 0 + c, h, h, h),
            (4 + c, 2 + c, 0, 0, h),
            (0 + c, 2 + c, h, h, h),
            (4 + c, 4 + c, h, 0, h),
            (2 + c, 4 + c, 0, h, h),
        ]
    acc = logits_part(mid, tuple(mid_copies), index((2, 0), (1, 1), (-1, 1)), w, acc)
    last = [t for p in (g1, g2, g3) for t in (p, to_core(p))]
    last_copies = tuple((2 * i + c, c, 0, 256 * i, 256) for i in range(3) for c in range(2))
    lens = jnp.concatenate([jnp.sum(query_mask > 0, axis=1), jnp.sum(passage_mask > 0, axis=1)]).astype(jnp.int32)
    expo, stats = logits_pool(last, last_copies, index((2, 1)), lens, w, acc, seqs)

    pooled = jnp.log1p(jnp.maximum(stats[:4], 0.0))
    pa = jnp.concatenate([pooled] + [to_x(pooled, -k) for k in (1, 2, 3)], axis=0)
    pb = to_zhi(pa)
    part = gram(pa, pb)
    parts = lax.all_to_all(jnp.broadcast_to(part, (16,) + part.shape), "vocab", 0, 0)

    group = lax.axis_index("dp")
    slot = jnp.arange(32, dtype=jnp.int32)
    place = slot // 4
    gx = (group // 2 + place % 4) % 4
    gz = (group % 2 + place // 4) % 2
    seq = (gx * 2 + gz) * 2 + slot % 2
    target = positive[seq]
    picked = ((target[:, None] == seq[None, :]) & (slot[:, None] % 4 < 2) & (slot[None, :] % 4 >= 2)).astype(F32)

    dl, loss, m21, s21 = first_grad(
        index((2, 1)), parts, pa, pb, stats, picked, expo, w, seqs, (F32, BF), positive.shape[0]
    )
    t21 = (m21 + to_core(s21)).astype(BF)
    r1, r2, r3 = to_y(t21[:256], 1), to_z(t21[256:512]), to_y(t21[512:], -1)
    m20, s20, m11, s11, mm1, sm1 = grad_part(index((2, 0), (1, 1), (-1, 1)), dl, w, (F32, BF) * 3)

    def pad(part, start):
        return jnp.pad(part.astype(F32), ((start, 768 - start - part.shape[0]), (0, 0)))

    t20 = (m20 + to_core(s20) + pad(r2, 256)).astype(BF)
    t11 = (m11 + to_core(s11) + pad(r1, 0)).astype(BF)
    tm1 = (mm1 + to_core(sm1) + pad(r3, 512)).astype(BF)
    u1 = to_y(jnp.concatenate([t20[:h], t11[h:]], axis=0), 1)
    u2 = to_y(jnp.concatenate([tm1[h:], t20[h:]], axis=0), -1)
    u3 = to_z(jnp.concatenate([t11[:h], tm1[:h]], axis=0))
    m10, s10, mm0, sm0, m01, s01, m00, s00 = grad_part(index((1, 0), (-1, 0), (0, 1), (0, 0)), dl, w, (F32, BF) * 4)
    t10 = (m10 + to_core(s10) + pad(u1[:h], 0) + pad(u3[:h], 0)).astype(BF)
    tm0 = (mm0 + to_core(sm0) + pad(u3[h:], 0) + pad(u2[h:], h)).astype(BF)
    t01 = (m01 + to_core(s01) + pad(u1[h:], h) + pad(u2[:h], h)).astype(BF)
    v1, v2, v3 = to_y(t10, 1), to_y(tm0, -1), to_z(t01)
    out = m00 + to_core(s00) + v1.astype(F32) + v2.astype(F32) + v3.astype(F32)
    out = out.astype(BF)
    return (
        out[:split].reshape(q_count, q_len, width),
        out[split:].reshape(p_count, p_len, width),
        loss[:q_count, 0],
    )


def solution(mesh):
    return jax.shard_map(
        on_device,
        mesh=mesh,
        in_specs=(
            P("dp", None, "vocab"),
            P("dp", None, "vocab"),
            P(None, "vocab"),
            P("dp", None),
            P("dp", None),
            P(),
        ),
        out_specs=(P("dp", None, "vocab"), P("dp", None, "vocab"), P("dp")),
        check_vma=False,
    )
```

time: 345 us -> 193 us (0.56)
  waiting for transfers between devices: 210 us -> 48.9 us
  Pallas kernels: 0 us -> 80.1 us
  blocking collectives: 61.4 us -> 0 us
  starting transfers between devices: 0.3 us -> 44.4 us
  matrix products: 38.7 us -> 0 us
  between operations: 14.5 us -> 1.29 us
  other arithmetic: 14.3 us -> 8.29 us
  local copies, waits for them, and re-layouts: 4.7 us -> 9.86 us
    reduce_scatter x1 -> x0, waiting for transfers between devices: 80.2 us -> none  [on_device(): lax.psum_scatter(lax.dot_general(w_rows, dlogits, (((1,), (1,)), ((), ())...]
    pallas_call x0 -> x7, Pallas kernels: none -> 80.1 us  [the longest x2 33.2 us: grad_part(): pl.pallas_call(functools.partial(grad_kernel, nk), in_specs=[pl.BlockSpec...]
    unnamed x4 -> x0, waiting for transfers between devices: 79.7 us -> none
    all_gather x1 -> x0, waiting for transfers between devices: 50.4 us -> none  [on_device(): lax.all_gather(tokens, 'vocab', axis=1, tiled=True)]
    ppermute x0 -> x40, waiting for transfers between devices: none -> 43.4 us  [the longest x12 26.4 us: to_y(): return lax.ppermute(x, 'vocab', y_perm(k % 4))]
    ppermute x0 -> x40, starting transfers between devices: none -> 39.9 us  [the longest x12 19.8 us: to_y(): return lax.ppermute(x, 'vocab', y_perm(k % 4))]
    dot_general x5 -> x0, matrix products: 38.7 us -> none  [the longest x1 19.4 us: on_device(): lax.dot_general(w_rows, dlogits, (((1,), (1,)), ((), ())), preferred_elem...]
    all_gather x1 -> x0, blocking collectives: 34.2 us -> none  [on_device(): p_every = lax.all_gather(p_pooled, 'dp', axis=0, tiled=True)]
  transfers between devices with their start and end apart: 3 -> 41, of which waited for: 3 -> 15; matrix products, arithmetic and copies ran while one was open for 2% -> 5% of each run, Pallas kernels for 0% -> 31%
where the time goes in v1:
time: 193 us
  Pallas kernels  80.1 us (42%)
  waiting for transfers between devices  48.9 us (25%)
  starting transfers between devices  44.4 us (23%)
  local copies, waits for them, and re-layouts  9.86 us (5%)
  other arithmetic  8.29 us (4%)
    pallas_call x2, Pallas kernels, grad_part(): pl.pallas_call(functools.partial(grad_kernel, nk), in_specs=[pl.BlockSpec...  33.2 us
    ppermute x12, waiting for transfers between devices, to_y(): return lax.ppermute(x, 'vocab', y_perm(k % 4))  26.4 us
    pallas_call x2, Pallas kernels, logits_part(): pl.pallas_call(functools.partial(logits_kernel, copies, nk, len(arrays),...  25.7 us
    ppermute x12, starting transfers between devices, to_y(): return lax.ppermute(x, 'vocab', y_perm(k % 4))  19.8 us
    ppermute x6, waiting for transfers between devices, to_z(): return lax.ppermute(x, 'vocab', Z_SWAP)  10.5 us
    pallas_call x1, Pallas kernels, logits_pool(): pl.pallas_call(functools.partial(pool_kernel, copies, nk, len(arrays), bn...  10.4 us
    pallas_call x1, Pallas kernels, first_grad(): pl.pallas_call(functools.partial(first_grad_kernel, seqs, nk, total_queri...  8.78 us
    ppermute x6, starting transfers between devices, to_z(): return lax.ppermute(x, 'vocab', Z_SWAP)  7.98 us
  transfers between devices with their start and end apart: 41, of which 15 were waited for; matrix products, arithmetic and copies ran while one was open for 5% of the time, Pallas kernels for 31%

profile of v1, /device:TPU:0, one launch (start us, length us, event | category | flops | bytes accessed | tf_op | source)
XLA Modules:
  0.0 192.8 jit_solution(4795831648391206348)
XLA Ops:
  0.6 1.0 pad_maximum_fusion.2.refs_0_
  1.7 3.2 %collective-permute-start = (bf16[768,256]{1,0:T(8,128)(2,1)S(1)}, bf16[768,256]{1,0:T(8,128)(2,1)S(1)}, u32[]{:S(2)}, u32[]{:S(2)}) collective-permute-start(bf16[768,256]{1,0:T(8,128)(2,1)S(1)} %pad_maximum_fusion.2.refs_0_), channel_id=1, source_target_pairs={{0,6},{1,7},{2,0},{3,1},{4,2},{5,3},{6,4},{7,5},{8,14},{9,15},{10,... | collective-permute-start | bytes 1179656 | tf_op jit(solution)/shard_map/ppermute | solution.py:28
  4.8 1.9 collective-permute-start.5
  6.8 6.5 %collective-permute-done.refs_2_ = bf16[768,256]{1,0:T(8,128)(2,1)S(1)} collective-permute-done((bf16[768,256]{1,0:T(8,128)(2,1)S(1)}, bf16[768,256]{1,0:T(8,128)(2,1)S(1)}, u32[]{:S(2)}, u32[]{:S(2)}) %collective-permute-start) | collective-permute-done | bytes 393248 | tf_op jit(solution)/shard_map/ppermute | solution.py:28
  13.2 3.4 %collective-permute-done.1.refs_4_ = bf16[768,256]{1,0:T(8,128)(2,1)S(1)} collective-permute-done((bf16[768,256]{1,0:T(8,128)(2,1)S(1)}, bf16[768,256]{1,0:T(8,128)(2,1)S(1)}, u32[]{:S(2)}, u32[]{:S(2)}) %collective-permute-start.1) | collective-permute-done | bytes 393248 | tf_op jit(solution)/shard_map/ppermute | solution.py:28
  16.9 3.2 %collective-permute-start.6 = (bf16[768,256]{1,0:T(8,128)(2,1)S(1)}, bf16[768,256]{1,0:T(8,128)(2,1)S(1)}, u32[]{:S(2)}, u32[]{:S(2)}) collective-permute-start(bf16[768,256]{1,0:T(8,128)(2,1)S(1)} %get-tuple-element.56), channel_id=1, source_target_pairs={{0,6},{1,7},{2,0},{3,1},{4,2},{5,3},{6,4},{7,5},{8,14},{9,15},{10,... | collective-permute-start | bytes 1179656 | tf_op jit(solution)/shard_map/ppermute | solution.py:28
  20.1 1.9 collective-permute-start.2
  22.2 5.5 %collective-permute-done.7.refs_2_ = bf16[768,256]{1,0:T(8,128)(2,1)S(1)} collective-permute-done((bf16[768,256]{1,0:T(8,128)(2,1)S(1)}, bf16[768,256]{1,0:T(8,128)(2,1)S(1)}, u32[]{:S(2)}, u32[]{:S(2)}) %collective-permute-start.7) | collective-permute-done | bytes 393248 | tf_op jit(solution)/shard_map/ppermute | solution.py:28
  28.5 0.7 pad_maximum_fusion.7
  29.1 2.7 %collective-permute-done.2.refs_4_ = bf16[768,256]{1,0:T(8,128)(2,1)S(1)} collective-permute-done((bf16[768,256]{1,0:T(8,128)(2,1)S(1)}, bf16[768,256]{1,0:T(8,128)(2,1)S(1)}, u32[]{:S(2)}, u32[]{:S(2)}) %collective-permute-start.2) | collective-permute-done | bytes 393248 | tf_op jit(solution)/shard_map/ppermute | solution.py:32
  31.8 1.7 collective-permute-start.8
  33.6 0.8 fusion.1
  34.5 3.2 %collective-permute-start.3 = (bf16[256,256]{1,0:T(8,128)(2,1)S(1)}, bf16[256,256]{1,0:T(8,128)(2,1)}, u32[]{:S(2)}, u32[]{:S(2)}) collective-permute-start(bf16[256,256]{1,0:T(8,128)(2,1)S(1)} %slice.110), channel_id=1, source_target_pairs={{0,6},{1,7},{2,0},{3,1},{4,2},{5,3},{6,4},{7,5},{8,14},{9,15},{10,... | collective-permute-start | bytes 393224 | tf_op jit(solution)/shard_map/ppermute | solution.py:28
  38.2 0.6 pad_add_fusion.idx
  38.9 0.8 fusion
  39.7 1.1 collective-permute-done.10.refs_4_
  40.8 0.5 collective-permute-start.11
  41.4 0.6 pad_add_fusion.1.lens
  41.9 0.7 stack.96.idx
  42.6 0.6 stack.97.idx
  43.3 12.8 %logits_part.2.refs_7_ = f32[768,2048]{1,0:T(8,128)} custom-call(s32[8]{0:T(128)} %stack.97.idx, bf16[768,256]{1,0:T(8,128)(2,1)} %copy-done.2, bf16[768,256]{1,0:T(8,128)(2,1)} %copy-done.21, bf16[768,256]{1,0:T(8,128)(2,1)} %copy-done.6, bf16[768,256]{1,0:T(8,128)(2,1)} %copy-done.22, bf16[768,256]{1,0:T(8,128)(2,1)} %copy-done.3, ...), custom_call_target="tpu_custom_call" | custom-call | tf_op jit(solution)/shard_map/logits_part/pallas_call | solution.py:112
  56.1 0.7 copy-done.20
  56.9 12.9 %logits_part.3.refs_7_ = f32[768,2048]{1,0:T(8,128)} custom-call(s32[6]{0:T(128)} %stack.96.idx, bf16[768,256]{1,0:T(8,128)(2,1)} %copy-done.17, bf16[768,256]{1,0:T(8,128)(2,1)} %copy-done.20, bf16[768,256]{1,0:T(8,128)(2,1)} %copy-done.5, bf16[768,256]{1,0:T(8,128)(2,1)} %copy-done.19, bf16[768,256]{1,0:T(8,128)(2,1)} %copy-done.16, ...), custom_call_target="tpu_custom_call" | custom-call | tf_op jit(solution)/shard_map/logits_part/pallas_call | solution.py:112
  69.8 10.4 %logits_pool.1 = (f32[768,2048]{1,0:T(8,128)}, f32[8,2048]{1,0:T(8,128)}) custom-call(s32[2]{0:T(128)} %pad_add_fusion.idx, s32[4]{0:T(128)} %pad_add_fusion.1.lens, bf16[256,256]{1,0:T(8,128)(2,1)} %collective-permute-done.3.refs_0_, bf16[256,256]{1,0:T(8,128)(2,1)} %collective-permute-done.4.refs_1_, bf16[256,256]{1,0:T(8,128)(2,1)} %collective-permute-done.8.refs_2_, ...), custom_call_target="tpu_custom_call" | custom-call | tf_op jit(solution)/shard_map/logits_pool/pallas_call | solution.py:158
  80.3 0.9 maximum_log-plus-one_fusion
  81.1 2.8 %collective-permute-start.19 = (f32[4,2048]{1,0:T(4,128)S(1)}, f32[4,2048]{1,0:T(4,128)S(1)}, u32[]{:S(2)}, u32[]{:S(2)}) collective-permute-start(f32[4,2048]{1,0:T(4,128)S(1)} %maximum_log-plus-one_fusion), channel_id=1, source_target_pairs={{0,96},{16,112},{32,0},{48,16},{64,32},{80,48},{96,64},{112,80},{1... | collective-permute-start | bytes 98312 | tf_op jit(solution)/shard_map/ppermute | solution.py:40
  84.0 0.8 collective-permute-start.20
  84.8 0.9 collective-permute-start.21
  85.7 3.7 %collective-permute-done.20 = f32[4,2048]{1,0:T(4,128)S(1)} collective-permute-done((f32[4,2048]{1,0:T(4,128)S(1)}, f32[4,2048]{1,0:T(4,128)S(1)}, u32[]{:S(2)}, u32[]{:S(2)}) %collective-permute-start.20) | collective-permute-done | bytes 32800 | tf_op jit(solution)/shard_map/ppermute | solution.py:40
  89.4 0.5 collective-permute-done.21
  90.0 3.7 %collective-permute-start.22 = (f32[16,2048]{1,0:T(8,128)S(1)}, f32[16,2048]{1,0:T(8,128)S(1)}, u32[]{:S(2)}, u32[]{:S(2)}) collective-permute-start(f32[16,2048]{1,0:T(8,128)S(1)} %pad_maximum_fusion.8.a.pa), channel_id=1, source_target_pairs={{0,16},{16,0},{32,48},{48,32},{64,80},{80,64},{96,112},{112,96},{1... | collective-permute-start | bytes 393224 | tf_op jit(solution)/shard_map/ppermute | solution.py:44
  93.6 0.7 gather_fusion
  94.4 2.2 %collective-permute-done.22.b.pb = f32[16,2048]{1,0:T(8,128)S(1)} collective-permute-done((f32[16,2048]{1,0:T(8,128)S(1)}, f32[16,2048]{1,0:T(8,128)S(1)}, u32[]{:S(2)}, u32[]{:S(2)}) %collective-permute-start.22) | collective-permute-done | bytes 131104 | tf_op jit(solution)/shard_map/ppermute | solution.py:44
  96.6 0.6 copy-done.18
  97.2 1.9 gram.1
  99.1 0.7 broadcast_in_dim.2
  99.9 0.8 reshape.352
  100.7 4.5 %all-to-all-start = ((f32[16,1,1024]{2,1,0:T(1,128)}), f32[16,1,1024]{2,1,0:T(1,128)S(1)}, u32[]{:S(2)}, u32[]{:S(2)}) async-start(f32[16,1,1024]{2,1,0:T(1,128)} %reshape.352), calls=%async_computation | async-start | bytes 131072 | tf_op jit(solution)/shard_map/all_to_all | solution.py:354
  105.2 0.7 and_convert_fusion.picked
  105.9 5.4 %all-to-all-done = f32[16,1,1024]{2,1,0:T(1,128)S(1)} async-done(((f32[16,1,1024]{2,1,0:T(1,128)}), f32[16,1,1024]{2,1,0:T(1,128)S(1)}, u32[]{:S(2)}, u32[]{:S(2)}) %all-to-all-start) | async-done | bytes 65568 | tf_op jit(solution)/shard_map/all_to_all | solution.py:354
  111.3 0.5 broadcast.528
  111.8 0.8 reduce.2
  112.6 0.8 reshape.353.parts
  113.5 8.8 %first_grad.1 = (bf16[768,2048]{1,0:T(8,128)(2,1)}, f32[8,128]{1,0:T(8,128)}, f32[768,256]{1,0:T(8,128)}, bf16[768,256]{1,0:T(8,128)(2,1)}) custom-call(s32[2]{0:T(128)} %pad_add_fusion.idx, f32[16,32,32]{2,1,0:T(8,128)} %reshape.353.parts, f32[16,2048]{1,0:T(8,128)} %copy-done.4, f32[16,2048]{1,0:T(8,128)} %copy-done.18, ...), custom_call_target="tpu_custom_call" | custom-call | tf_op jit(solution)/shard_map/first_grad/pallas_call | solution.py:254
  122.5 14.8 %grad_part.3 = (f32[768,256]{1,0:T(8,128)}, bf16[768,256]{1,0:T(8,128)(2,1)}, f32[768,256]{1,0:T(8,128)}, bf16[768,256]{1,0:T(8,128)(2,1)}, f32[768,256]{1,0:T(8,128)}, /*index=5*/bf16[768,256]{1,0:T(8,128)(2,1)}) custom-call(s32[6]{0:T(128)} %stack.96.idx, bf16[768,2048]{1,0:T(8,128)(2,1)} %get-tuple-element.25.dl, bf16[4096,2048]{1,0:T(8,128)(2,1)} %w.5), custom_call_target="tpu_custom_call" | custom-call | tf_op jit(solution)/shard_map/grad_part/pallas_call | solution.py:290
  137.9 0.6 collective-permute-start.29
  138.5 0.6 stack.86.idx
  139.1 0.5 collective-permute-start.25
  139.6 18.4 %grad_part.2 = (f32[768,256]{1,0:T(8,128)}, bf16[768,256]{1,0:T(8,128)(2,1)}, f32[768,256]{1,0:T(8,128)}, bf16[768,256]{1,0:T(8,128)(2,1)}, f32[768,256]{1,0:T(8...) custom-call(s32[8]{0:T(128)} %stack.86.idx, ...), custom_call_target="tpu_custom_call" | custom-call | tf_op jit(solution)/shard_map/grad_part/pallas_call | solution.py:290
  158.3 2.7 %collective-permute-start.32 = (bf16[256,256]{1,0:T(8,128)(2,1)S(1)}, bf16[256,256]{1,0:T(8,128)(2,1)S(1)}, u32[]{:S(2)}, u32[]{:S(2)}) collective-permute-start(bf16[256,256]{1,0:T(8,128)(2,1)S(1)} %get-tuple-element.52), channel_id=1, source_target_pairs={{0,6},{1,7},{2,0},{3,1},{4,2},{5,3},{6,4},{7,5},{8,14},{9,15},{10,... | collective-permute-start | bytes 393224 | tf_op jit(solution)/shard_map/ppermute | solution.py:28
  161.0 0.7 collective-permute-start.27
  161.8 2.5 %collective-permute-done.32 = bf16[256,256]{1,0:T(8,128)(2,1)S(1)} collective-permute-done((bf16[256,256]{1,0:T(8,128)(2,1)S(1)}, bf16[256,256]{1,0:T(8,128)(2,1)S(1)}, u32[]{:S(2)}, u32[]{:S(2)}) %collective-permute-start.32) | collective-permute-done | bytes 131104 | tf_op jit(solution)/shard_map/ppermute | solution.py:28
  164.5 0.7 collective-permute-start.33
  165.3 1.2 collective-permute-done.27
  166.8 3.3 %collective-permute-start.36 = (bf16[768,256]{1,0:T(8,128)(2,1)S(1)}, bf16[768,256]{1,0:T(8,128)(2,1)S(1)}, u32[]{:S(2)}, u32[]{:S(2)}) collective-permute-start(bf16[768,256]{1,0:T(8,128)(2,1)S(1)} %pad_maximum_fusion.6), channel_id=1, source_target_pairs={{0,6},{1,7},{2,0},{3,1},{4,2},{5,3},{6,4},{7,5},{8,14},{9,15},{10,... | collective-permute-start | bytes 1179656 | tf_op jit(solution)/shard_map/ppermute | solution.py:28
  170.6 4.6 %collective-permute-done.33 = bf16[768,256]{1,0:T(8,128)(2,1)S(1)} collective-permute-done((bf16[768,256]{1,0:T(8,128)(2,1)S(1)}, bf16[768,256]{1,0:T(8,128)(2,1)S(1)}, u32[]{:S(2)}, u32[]{:S(2)}) %collective-permute-start.33) | collective-permute-done | bytes 393248 | tf_op jit(solution)/shard_map/ppermute | solution.py:32
  175.2 3.0 %collective-permute-done.30 = bf16[768,256]{1,0:T(8,128)(2,1)S(1)} collective-permute-done((bf16[768,256]{1,0:T(8,128)(2,1)S(1)}, bf16[768,256]{1,0:T(8,128)(2,1)S(1)}, u32[]{:S(2)}, u32[]{:S(2)}) %collective-permute-start.30) | collective-permute-done | bytes 393248 | tf_op jit(solution)/shard_map/ppermute | solution.py:28
  178.8 3.3 %collective-permute-start.37 = (bf16[768,256]{1,0:T(8,128)(2,1)S(1)}, bf16[768,256]{1,0:T(8,128)(2,1)S(1)}, u32[]{:S(2)}, u32[]{:S(2)}) collective-permute-start(bf16[768,256]{1,0:T(8,128)(2,1)S(1)} %add_convert_fusion.2), channel_id=1, source_target_pairs={{0,6},{1,7},{2,0},{3,1},{4,2},{5,3},{6,4},{7,5},{8,14},{9,15},{10,... | collective-permute-start | bytes 1179656 | tf_op jit(solution)/shard_map/ppermute | solution.py:28
  182.3 1.0 collective-permute-start.39
  183.3 1.3 slice_reduce_fusion
  184.6 4.5 %collective-permute-done.34 = bf16[768,256]{1,0:T(8,128)(2,1)S(1)} collective-permute-done((bf16[768,256]{1,0:T(8,128)(2,1)S(1)}, bf16[768,256]{1,0:T(8,128)(2,1)S(1)}, u32[]{:S(2)}, u32[]{:S(2)}) %collective-permute-start.34) | collective-permute-done | bytes 393248 | tf_op jit(solution)/shard_map/ppermute | solution.py:28
  189.1 2.0 %collective-permute-done.39 = bf16[768,256]{1,0:T(8,128)(2,1)S(1)} collective-permute-done((bf16[768,256]{1,0:T(8,128)(2,1)S(1)}, bf16[768,256]{1,0:T(8,128)(2,1)S(1)}, u32[]{:S(2)}, u32[]{:S(2)}) %collective-permute-start.39) | collective-permute-done | bytes 393248 | tf_op jit(solution)/shard_map/ppermute | solution.py:32
  191.4 0.7 slice.130
  192.1 0.7 slice.129
  (130 shorter events, 5.1 us)
Async XLA Ops:
  0.6 93.0 %copy-start = (s32[16]{0:T(128)S(1)}, s32[16]{0:T(128)}, u32[]{:S(2)}) copy-start(s32[16]{0:T(128)} %param.11) | copy-start | bytes 196
  1.7 41.6 %copy-start.2 = (bf16[768,256]{1,0:T(8,128)(2,1)}, bf16[768,256]{1,0:T(8,128)(2,1)S(1)}, u32[]{:S(2)}) copy-start(bf16[768,256]{1,0:T(8,128)(2,1)S(1)} %pad_maximum_fusion.2.refs_0_) | copy-start | bytes 1179652
  1.7 11.5 %collective-permute-start = (bf16[768,256]{1,0:T(8,128)(2,1)S(1)}, bf16[768,256]{1,0:T(8,128)(2,1)S(1)}, u32[]{:S(2)}, u32[]{:S(2)}) collective-permute-start(bf16[768,256]{1,0:T(8,128)(2,1)S(1)} %pad_maximum_fusion.2.refs_0_), channel_id=1, source_target_pairs={{0,6},{1,7},{2,0},{3,1},{4,2},{5,3},{6,4},{7,5},{8,14},{9,15},{10,... | collective-permute-start | bytes 1179656 | tf_op jit(solution)/shard_map/ppermute | solution.py:28
  4.8 11.8 %collective-permute-start.1 = (bf16[768,256]{1,0:T(8,128)(2,1)S(1)}, bf16[768,256]{1,0:T(8,128)(2,1)S(1)}, u32[]{:S(2)}, u32[]{:S(2)}) collective-permute-start(bf16[768,256]{1,0:T(8,128)(2,1)S(1)} %pad_maximum_fusion.2.refs_0_), channel_id=1, source_target_pairs={{0,2},{1,3},{2,4},{3,5},{4,6},{5,7},{6,0},{7,1},{8,10},{9,11},{10,... | collective-permute-start | bytes 1179656 | tf_op jit(solution)/shard_map/ppermute | solution.py:28
  4.8 11.8 %collective-permute-start.5 = (bf16[768,256]{1,0:T(8,128)(2,1)S(1)}, bf16[768,256]{1,0:T(8,128)(2,1)S(1)}, u32[]{:S(2)}, u32[]{:S(2)}) collective-permute-start(bf16[768,256]{1,0:T(8,128)(2,1)S(1)} %pad_maximum_fusion.2.refs_0_), channel_id=1, source_target_pairs={{0,8},{1,9},{2,10},{3,11},{4,12},{5,13},{6,14},{7,15},{8,0},{9,1},... | collective-permute-start | bytes 1179656 | tf_op jit(solution)/shard_map/ppermute | solution.py:32
  13.2 30.0 %copy-start.6 = (bf16[768,256]{1,0:T(8,128)(2,1)}, bf16[768,256]{1,0:T(8,128)(2,1)S(1)}, u32[]{:S(2)}) copy-start(bf16[768,256]{1,0:T(8,128)(2,1)S(1)} %collective-permute-done.refs_2_) | copy-start | bytes 1179652
  16.6 26.6 %copy-start.3 = (bf16[768,256]{1,0:T(8,128)(2,1)}, bf16[768,256]{1,0:T(8,128)(2,1)S(1)}, u32[]{:S(2)}) copy-start(bf16[768,256]{1,0:T(8,128)(2,1)S(1)} %collective-permute-done.1.refs_4_) | copy-start | bytes 1179652
  16.7 26.6 %copy-start.7 = (bf16[768,256]{1,0:T(8,128)(2,1)}, bf16[768,256]{1,0:T(8,128)(2,1)S(1)}, u32[]{:S(2)}) copy-start(bf16[768,256]{1,0:T(8,128)(2,1)S(1)} %collective-permute-done.5.refs_6_) | copy-start | bytes 1179652
  16.8 10.9 %collective-permute-start.7 = (bf16[768,256]{1,0:T(8,128)(2,1)S(1)}, bf16[768,256]{1,0:T(8,128)(2,1)S(1)}, u32[]{:S(2)}, u32[]{:S(2)}) collective-permute-start(bf16[768,256]{1,0:T(8,128)(2,1)S(1)} %get-tuple-element.57), channel_id=1, source_target_pairs={{0,2},{1,3},{2,4},{3,5},{4,6},{5,7},{6,0},{7,1},{8,10},{9,11},{10,... | collective-permute-start | bytes 1179656 | tf_op jit(solution)/shard_map/ppermute | solution.py:28
  16.9 10.9 %collective-permute-start.6 = (bf16[768,256]{1,0:T(8,128)(2,1)S(1)}, bf16[768,256]{1,0:T(8,128)(2,1)S(1)}, u32[]{:S(2)}, u32[]{:S(2)}) collective-permute-start(bf16[768,256]{1,0:T(8,128)(2,1)S(1)} %get-tuple-element.56), channel_id=1, source_target_pairs={{0,6},{1,7},{2,0},{3,1},{4,2},{5,3},{6,4},{7,5},{8,14},{9,15},{10,... | collective-permute-start | bytes 1179656 | tf_op jit(solution)/shard_map/ppermute | solution.py:28
  20.1 8.2 %collective-permute-start.15 = (bf16[768,256]{1,0:T(8,128)(2,1)S(1)}, bf16[768,256]{1,0:T(8,128)(2,1)S(1)}, u32[]{:S(2)}, u32[]{:S(2)}) collective-permute-start(bf16[768,256]{1,0:T(8,128)(2,1)S(1)} %pad_maximum_fusion.2.refs_0_), channel_id=1, source_target_pairs={{0,1},{1,0},{2,3},{3,2},{4,5},{5,4},{6,7},{7,6},{8,9},{9,8},{10,11... | collective-permute-start | bytes 1179656 | tf_op jit(solution)/shard_map/ppermute | solution.py:36
  20.1 11.7 %collective-permute-start.2 = (bf16[768,256]{1,0:T(8,128)(2,1)S(1)}, bf16[768,256]{1,0:T(8,128)(2,1)S(1)}, u32[]{:S(2)}, u32[]{:S(2)}) collective-permute-start(bf16[768,256]{1,0:T(8,128)(2,1)S(1)} %get-tuple-element.58), channel_id=1, source_target_pairs={{0,8},{1,9},{2,10},{3,11},{4,12},{5,13},{6,14},{7,15},{8,0},{9,1},... | collective-permute-start | bytes 1179656 | tf_op jit(solution)/shard_map/ppermute | solution.py:32
  22.0 12.4 %collective-permute-start.16 = (bf16[768,256]{1,0:T(8,128)(2,1)S(1)}, bf16[768,256]{1,0:T(8,128)(2,1)S(1)}, u32[]{:S(2)}, u32[]{:S(2)}) collective-permute-start(bf16[768,256]{1,0:T(8,128)(2,1)S(1)} %collective-permute-done.refs_2_), channel_id=1, source_target_pairs={{0,1},{1,0},{2,3},{3,2},{4,5},{5,4},{6,7},{7,6},{8,9},{9,8},{10,11... | collective-permute-start | bytes 1179656 | tf_op jit(solution)/shard_map/ppermute | solution.py:36
  27.7 28.3 %copy-start.5 = (bf16[768,256]{1,0:T(8,128)(2,1)}, bf16[768,256]{1,0:T(8,128)(2,1)S(1)}, u32[]{:S(2)}) copy-start(bf16[768,256]{1,0:T(8,128)(2,1)S(1)} %collective-permute-done.7.refs_2_) | copy-start | bytes 1179652
  27.7 6.7 %collective-permute-start.17 = (bf16[768,256]{1,0:T(8,128)(2,1)S(1)}, bf16[768,256]{1,0:T(8,128)(2,1)}, u32[]{:S(2)}, u32[]{:S(2)}) collective-permute-start(bf16[768,256]{1,0:T(8,128)(2,1)S(1)} %collective-permute-done.1.refs_4_), channel_id=1, source_target_pairs={{0,1},{1,0},{2,3},{3,2},{4,5},{5,4},{6,7},{7,6},{8,9},{9,8},{10,11... | collective-permute-start | bytes 1179656 | tf_op jit(solution)/shard_map/ppermute | solution.py:36
  27.7 28.3 %copy-start.17 = (bf16[768,256]{1,0:T(8,128)(2,1)}, bf16[768,256]{1,0:T(8,128)(2,1)S(1)}, u32[]{:S(2)}) copy-start(bf16[768,256]{1,0:T(8,128)(2,1)S(1)} %collective-permute-done.6.refs_0_) | copy-start | bytes 1179652
  27.8 10.0 %collective-permute-start.18 = (bf16[768,256]{1,0:T(8,128)(2,1)S(1)}, bf16[768,256]{1,0:T(8,128)(2,1)}, u32[]{:S(2)}, u32[]{:S(2)}) collective-permute-start(bf16[768,256]{1,0:T(8,128)(2,1)S(1)} %collective-permute-done.5.refs_6_), channel_id=1, source_target_pairs={{0,1},{1,0},{2,3},{3,2},{4,5},{5,4},{6,7},{7,6},{8,9},{9,8},{10,11... | collective-permute-start | bytes 1179656 | tf_op jit(solution)/shard_map/ppermute | solution.py:36
  28.3 13.0 %collective-permute-start.13 = (bf16[768,256]{1,0:T(8,128)(2,1)S(1)}, bf16[768,256]{1,0:T(8,128)(2,1)S(1)}, u32[]{:S(2)}, u32[]{:S(2)}) collective-permute-start(bf16[768,256]{1,0:T(8,128)(2,1)S(1)} %collective-permute-done.7.refs_2_), channel_id=1, source_target_pairs={{0,1},{1,0},{2,3},{3,2},{4,5},{5,4},{6,7},{7,6},{8,9},{9,8},{10,11... | collective-permute-start | bytes 1179656 | tf_op jit(solution)/shard_map/ppermute | solution.py:36
  31.8 24.3 %copy-start.16 = (bf16[768,256]{1,0:T(8,128)(2,1)}, bf16[768,256]{1,0:T(8,128)(2,1)S(1)}, u32[]{:S(2)}) copy-start(bf16[768,256]{1,0:T(8,128)(2,1)S(1)} %collective-permute-done.2.refs_4_) | copy-start | bytes 1179652
  31.8 5.9 %collective-permute-start.8 = (bf16[256,256]{1,0:T(8,128)(2,1)}, bf16[256,256]{1,0:T(8,128)(2,1)}, u32[]{:S(2)}, u32[]{:S(2)}) collective-permute-start(bf16[256,256]{1,0:T(8,128)(2,1)} %pad_maximum_fusion.7), channel_id=1, source_target_pairs={{0,8},{1,9},{2,10},{3,11},{4,12},{5,13},{6,14},{7,15},{8,0},{9,1},... | collective-permute-start | bytes 393224 | tf_op jit(solution)/shard_map/ppermute | solution.py:32
  34.4 6.4 %collective-permute-start.10 = (bf16[256,256]{1,0:T(8,128)(2,1)S(1)}, bf16[256,256]{1,0:T(8,128)(2,1)}, u32[]{:S(2)}, u32[]{:S(2)}) collective-permute-start(bf16[256,256]{1,0:T(8,128)(2,1)S(1)} %slice.115), channel_id=1, source_target_pairs={{0,2},{1,3},{2,4},{3,5},{4,6},{5,7},{6,0},{7,1},{8,10},{9,11},{10,... | collective-permute-start | bytes 393224 | tf_op jit(solution)/shard_map/ppermute | solution.py:28
  34.5 6.3 %collective-permute-start.3 = (bf16[256,256]{1,0:T(8,128)(2,1)S(1)}, bf16[256,256]{1,0:T(8,128)(2,1)}, u32[]{:S(2)}, u32[]{:S(2)}) collective-permute-start(bf16[256,256]{1,0:T(8,128)(2,1)S(1)} %slice.110), channel_id=1, source_target_pairs={{0,6},{1,7},{2,0},{3,1},{4,2},{5,3},{6,4},{7,5},{8,14},{9,15},{10,... | collective-permute-start | bytes 393224 | tf_op jit(solution)/shard_map/ppermute | solution.py:28
  37.7 18.4 %collective-permute-start.12 = (bf16[768,256]{1,0:T(8,128)(2,1)S(1)}, bf16[768,256]{1,0:T(8,128)(2,1)S(1)}, u32[]{:S(2)}, u32[]{:S(2)}) collective-permute-start(bf16[768,256]{1,0:T(8,128)(2,1)S(1)} %collective-permute-done.6.refs_0_), channel_id=1, source_target_pairs={{0,1},{1,0},{2,3},{3,2},{4,5},{5,4},{6,7},{7,6},{8,9},{9,8},{10,11... | collective-permute-start | bytes 1179656 | tf_op jit(solution)/shard_map/ppermute | solution.py:36
  37.7 18.4 %collective-permute-start.14 = (bf16[768,256]{1,0:T(8,128)(2,1)S(1)}, bf16[768,256]{1,0:T(8,128)(2,1)}, u32[]{:S(2)}, u32[]{:S(2)}) collective-permute-start(bf16[768,256]{1,0:T(8,128)(2,1)S(1)} %collective-permute-done.2.refs_4_), channel_id=1, source_target_pairs={{0,1},{1,0},{2,3},{3,2},{4,5},{5,4},{6,7},{7,6},{8,9},{9,8},{10,11... | collective-permute-start | bytes 1179656 | tf_op jit(solution)/shard_map/ppermute | solution.py:36
  40.8 29.1 %collective-permute-start.9 = (bf16[256,256]{1,0:T(8,128)(2,1)}, bf16[256,256]{1,0:T(8,128)(2,1)}, u32[]{:S(2)}, u32[]{:S(2)}) collective-permute-start(bf16[256,256]{1,0:T(8,128)(2,1)} %collective-permute-done.8.refs_2_), channel_id=1, source_target_pairs={{0,1},{1,0},{2,3},{3,2},{4,5},{5,4},{6,7},{7,6},{8,9},{9,8},{10,11... | collective-permute-start | bytes 393224 | tf_op jit(solution)/shard_map/ppermute | solution.py:36
  40.8 29.1 %collective-permute-start.11 = (bf16[256,256]{1,0:T(8,128)(2,1)}, bf16[256,256]{1,0:T(8,128)(2,1)}, u32[]{:S(2)}, u32[]{:S(2)}) collective-permute-start(bf16[256,256]{1,0:T(8,128)(2,1)} %collective-permute-done.10.refs_4_), channel_id=1, source_target_pairs={{0,1},{1,0},{2,3},{3,2},{4,5},{5,4},{6,7},{7,6},{8,9},{9,8},{10,11... | collective-permute-start | bytes 393224 | tf_op jit(solution)/shard_map/ppermute | solution.py:36
  41.3 14.8 %copy-start.19 = (bf16[768,256]{1,0:T(8,128)(2,1)}, bf16[768,256]{1,0:T(8,128)(2,1)S(1)}, u32[]{:S(2)}) copy-start(bf16[768,256]{1,0:T(8,128)(2,1)S(1)} %collective-permute-done.13.refs_3_) | copy-start | bytes 1179652
  41.3 28.6 %collective-permute-start.4 = (bf16[256,256]{1,0:T(8,128)(2,1)}, bf16[256,256]{1,0:T(8,128)(2,1)}, u32[]{:S(2)}, u32[]{:S(2)}) collective-permute-start(bf16[256,256]{1,0:T(8,128)(2,1)} %collective-permute-done.3.refs_0_), channel_id=1, source_target_pairs={{0,1},{1,0},{2,3},{3,2},{4,5},{5,4},{6,7},{7,6},{8,9},{9,8},{10,11... | collective-permute-start | bytes 393224 | tf_op jit(solution)/shard_map/ppermute | solution.py:36
  81.1 4.5 %collective-permute-start.19 = (f32[4,2048]{1,0:T(4,128)S(1)}, f32[4,2048]{1,0:T(4,128)S(1)}, u32[]{:S(2)}, u32[]{:S(2)}) collective-permute-start(f32[4,2048]{1,0:T(4,128)S(1)} %maximum_log-plus-one_fusion), channel_id=1, source_target_pairs={{0,96},{16,112},{32,0},{48,16},{64,32},{80,48},{96,64},{112,80},{1... | collective-permute-start | bytes 98312 | tf_op jit(solution)/shard_map/ppermute | solution.py:40
  84.0 5.4 %collective-permute-start.20 = (f32[4,2048]{1,0:T(4,128)S(1)}, f32[4,2048]{1,0:T(4,128)S(1)}, u32[]{:S(2)}, u32[]{:S(2)}) collective-permute-start(f32[4,2048]{1,0:T(4,128)S(1)} %maximum_log-plus-one_fusion), channel_id=1, source_target_pairs={{0,64},{16,80},{32,96},{48,112},{64,0},{80,16},{96,32},{112,48},{1... | collective-permute-start | bytes 98312 | tf_op jit(solution)/shard_map/ppermute | solution.py:40
  84.8 5.1 %collective-permute-start.21 = (f32[4,2048]{1,0:T(4,128)S(1)}, f32[4,2048]{1,0:T(4,128)S(1)}, u32[]{:S(2)}, u32[]{:S(2)}) collective-permute-start(f32[4,2048]{1,0:T(4,128)S(1)} %maximum_log-plus-one_fusion), channel_id=1, source_target_pairs={{0,32},{16,48},{32,64},{48,80},{64,96},{80,112},{96,0},{112,16},{1... | collective-permute-start | bytes 98312 | tf_op jit(solution)/shard_map/ppermute | solution.py:40
  89.9 6.6 %copy-start.4 = (f32[16,2048]{1,0:T(8,128)}, f32[16,2048]{1,0:T(8,128)S(1)}, u32[]{:S(2)}) copy-start(f32[16,2048]{1,0:T(8,128)S(1)} %pad_maximum_fusion.8.a.pa) | copy-start | bytes 393220
  90.0 6.6 %collective-permute-start.22 = (f32[16,2048]{1,0:T(8,128)S(1)}, f32[16,2048]{1,0:T(8,128)S(1)}, u32[]{:S(2)}, u32[]{:S(2)}) collective-permute-start(f32[16,2048]{1,0:T(8,128)S(1)} %pad_maximum_fusion.8.a.pa), channel_id=1, source_target_pairs={{0,16},{16,0},{32,48},{48,32},{64,80},{80,64},{96,112},{112,96},{1... | collective-permute-start | bytes 393224 | tf_op jit(solution)/shard_map/ppermute | solution.py:44
  100.7 10.7 %all-to-all-start = ((f32[16,1,1024]{2,1,0:T(1,128)}), f32[16,1,1024]{2,1,0:T(1,128)S(1)}, u32[]{:S(2)}, u32[]{:S(2)}) async-start(f32[16,1,1024]{2,1,0:T(1,128)} %reshape.352), calls=%async_computation | async-start | bytes 131072 | tf_op jit(solution)/shard_map/all_to_all | solution.py:354
  122.3 15.5 %collective-permute-start.26 = (bf16[768,256]{1,0:T(8,128)(2,1)}, bf16[768,256]{1,0:T(8,128)(2,1)S(1)}, u32[]{:S(2)}, u32[]{:S(2)}) collective-permute-start(bf16[768,256]{1,0:T(8,128)(2,1)} %get-tuple-element.33), channel_id=1, source_target_pairs={{0,1},{1,0},{2,3},{3,2},{4,5},{5,4},{6,7},{7,6},{8,9},{9,8},{10,11... | collective-permute-start | bytes 1179656 | tf_op jit(solution)/shard_map/ppermute | solution.py:36
  122.5 15.3 %copy-start.8 = (f32[768,256]{1,0:T(8,128)S(1)}, f32[768,256]{1,0:T(8,128)}, u32[]{:S(2)}) copy-start(f32[768,256]{1,0:T(8,128)} %get-tuple-element.32) | copy-start | bytes 2359300
  137.3 21.0 %collective-permute-start.28 = (bf16[768,256]{1,0:T(8,128)(2,1)}, bf16[768,256]{1,0:T(8,128)(2,1)S(1)}, u32[]{:S(2)}, u32[]{:S(2)}) collective-permute-start(bf16[768,256]{1,0:T(8,128)(2,1)} %get-tuple-element.35), channel_id=1, source_target_pairs={{0,1},{1,0},{2,3},{3,2},{4,5},{5,4},{6,7},{7,6},{8,9},{9,8},{10,11... | collective-permute-start | bytes 1179656 | tf_op jit(solution)/shard_map/ppermute | solution.py:36
  137.9 23.1 %collective-permute-start.29 = (bf16[256,256]{1,0:T(8,128)(2,1)S(1)}, bf16[256,256]{1,0:T(8,128)(2,1)S(1)}, u32[]{:S(2)}, u32[]{:S(2)}) collective-permute-start(bf16[256,256]{1,0:T(8,128)(2,1)S(1)} %get-tuple-element.51), channel_id=1, source_target_pairs={{0,2},{1,3},{2,4},{3,5},{4,6},{5,7},{6,0},{7,1},{8,10},{9,11},{10,... | collective-permute-start | bytes 393224 | tf_op jit(solution)/shard_map/ppermute | solution.py:28
  138.5 23.3 %collective-permute-start.31 = (bf16[768,256]{1,0:T(8,128)(2,1)}, bf16[768,256]{1,0:T(8,128)(2,1)S(1)}, u32[]{:S(2)}, u32[]{:S(2)}) collective-permute-start(bf16[768,256]{1,0:T(8,128)(2,1)} %get-tuple-element.37), channel_id=1, source_target_pairs={{0,1},{1,0},{2,3},{3,2},{4,5},{5,4},{6,7},{7,6},{8,9},{9,8},{10,11... | collective-permute-start | bytes 1179656 | tf_op jit(solution)/shard_map/ppermute | solution.py:36
  139.1 22.5 %copy-start.15 = (f32[768,256]{1,0:T(8,128)S(1)}, f32[768,256]{1,0:T(8,128)}, u32[]{:S(2)}) copy-start(f32[768,256]{1,0:T(8,128)} %get-tuple-element.34) | copy-start | bytes 2359300
  139.1 25.2 %copy-start.14 = (f32[768,256]{1,0:T(8,128)S(1)}, f32[768,256]{1,0:T(8,128)}, u32[]{:S(2)}) copy-start(f32[768,256]{1,0:T(8,128)} %get-tuple-element.36) | copy-start | bytes 2359300
  139.1 26.1 %collective-permute-start.25 = (bf16[768,256]{1,0:T(8,128)(2,1)}, bf16[768,256]{1,0:T(8,128)(2,1)S(1)}, u32[]{:S(2)}, u32[]{:S(2)}) collective-permute-start(bf16[768,256]{1,0:T(8,128)(2,1)} %get-tuple-element.31), channel_id=1, source_target_pairs={{0,1},{1,0},{2,3},{3,2},{4,5},{5,4},{6,7},{7,6},{8,9},{9,8},{10,11... | collective-permute-start | bytes 1179656 | tf_op jit(solution)/shard_map/ppermute | solution.py:36
  158.0 8.5 %copy-start.13 = (f32[768,256]{1,0:T(8,128)S(1)}, f32[768,256]{1,0:T(8,128)}, u32[]{:S(2)}) copy-start(f32[768,256]{1,0:T(8,128)} %get-tuple-element.30) | copy-start | bytes 2359300
  158.0 12.0 %copy-start.26 = (bf16[768,256]{1,0:T(8,128)(2,1)S(1)}, bf16[768,256]{1,0:T(8,128)(2,1)}, u32[]{:S(2)}) copy-start(bf16[768,256]{1,0:T(8,128)(2,1)} %get-tuple-element.39) | copy-start | bytes 1179652
  158.1 12.0 %copy-start.25 = (bf16[768,256]{1,0:T(8,128)(2,1)S(1)}, bf16[768,256]{1,0:T(8,128)(2,1)}, u32[]{:S(2)}) copy-start(bf16[768,256]{1,0:T(8,128)(2,1)} %get-tuple-element.41) | copy-start | bytes 1179652
  158.1 17.1 %copy-start.24 = (bf16[768,256]{1,0:T(8,128)(2,1)S(1)}, bf16[768,256]{1,0:T(8,128)(2,1)}, u32[]{:S(2)}) copy-start(bf16[768,256]{1,0:T(8,128)(2,1)} %get-tuple-element.27) | copy-start | bytes 1179652
  158.1 20.1 %copy-start.12 = (f32[768,256]{1,0:T(8,128)S(1)}, f32[768,256]{1,0:T(8,128)}, u32[]{:S(2)}) copy-start(f32[768,256]{1,0:T(8,128)} %get-tuple-element.28) | copy-start | bytes 2359300
  158.1 20.1 %copy-start.23 = (pred[768]{0:T(1024)(128)(4,1)S(1)}, pred[768]{0:T(1024)(128)(4,1)}, u32[]{:S(2)}) copy-start(pred[768]{0:T(1024)(128)(4,1)} %constant.230.clone.1) | copy-start | bytes 2308
  158.1 12.0 %collective-permute-start.24 = (bf16[768,256]{1,0:T(8,128)(2,1)}, bf16[768,256]{1,0:T(8,128)(2,1)S(1)}, u32[]{:S(2)}, u32[]{:S(2)}) collective-permute-start(bf16[768,256]{1,0:T(8,128)(2,1)} %get-tuple-element.29), channel_id=1, source_target_pairs={{0,1},{1,0},{2,3},{3,2},{4,5},{5,4},{6,7},{7,6},{8,9},{9,8},{10,11... | collective-permute-start | bytes 1179656 | tf_op jit(solution)/shard_map/ppermute | solution.py:36
  158.3 6.0 %collective-permute-start.32 = (bf16[256,256]{1,0:T(8,128)(2,1)S(1)}, bf16[256,256]{1,0:T(8,128)(2,1)S(1)}, u32[]{:S(2)}, u32[]{:S(2)}) collective-permute-start(bf16[256,256]{1,0:T(8,128)(2,1)S(1)} %get-tuple-element.52), channel_id=1, source_target_pairs={{0,6},{1,7},{2,0},{3,1},{4,2},{5,3},{6,4},{7,5},{8,14},{9,15},{10,... | collective-permute-start | bytes 393224 | tf_op jit(solution)/shard_map/ppermute | solution.py:28
  161.0 5.5 %collective-permute-start.27 = (bf16[256,256]{1,0:T(8,128)(2,1)S(1)}, bf16[256,256]{1,0:T(8,128)(2,1)S(1)}, u32[]{:S(2)}, u32[]{:S(2)}) collective-permute-start(bf16[256,256]{1,0:T(8,128)(2,1)S(1)} %get-tuple-element.53), channel_id=1, source_target_pairs={{0,8},{1,9},{2,10},{3,11},{4,12},{5,13},{6,14},{7,15},{8,0},{9,1},... | collective-permute-start | bytes 393224 | tf_op jit(solution)/shard_map/ppermute | solution.py:32
  161.7 17.0 %copy-start.11 = (f32[768,256]{1,0:T(8,128)S(1)}, f32[768,256]{1,0:T(8,128)}, u32[]{:S(2)}) copy-start(f32[768,256]{1,0:T(8,128)} %get-tuple-element.38) | copy-start | bytes 2359300
  164.4 17.7 %copy-start.10 = (f32[768,256]{1,0:T(8,128)S(1)}, f32[768,256]{1,0:T(8,128)}, u32[]{:S(2)}) copy-start(f32[768,256]{1,0:T(8,128)} %get-tuple-element.40) | copy-start | bytes 2359300
  164.5 26.7 %copy-start.9 = (f32[768,256]{1,0:T(8,128)S(1)}, f32[768,256]{1,0:T(8,128)}, u32[]{:S(2)}) copy-start(f32[768,256]{1,0:T(8,128)} %get-tuple-element.26) | copy-start | bytes 2359300
  164.5 10.7 %collective-permute-start.33 = (bf16[768,256]{1,0:T(8,128)(2,1)S(1)}, bf16[768,256]{1,0:T(8,128)(2,1)S(1)}, u32[]{:S(2)}, u32[]{:S(2)}) collective-permute-start(bf16[768,256]{1,0:T(8,128)(2,1)S(1)} %pad_maximum_fusion.5), channel_id=1, source_target_pairs={{0,8},{1,9},{2,10},{3,11},{4,12},{5,13},{6,14},{7,15},{8,0},{9,1},... | collective-permute-start | bytes 1179656 | tf_op jit(solution)/shard_map/ppermute | solution.py:32
  166.6 26.1 %copy-start.1 = (s32[16]{0:T(128)S(1)}, s32[16]{0:T(128)}, u32[]{:S(2)}) copy-start(s32[16]{0:T(128)} %param.11) | copy-start | bytes 196
  166.7 11.5 %collective-permute-start.30 = (bf16[768,256]{1,0:T(8,128)(2,1)S(1)}, bf16[768,256]{1,0:T(8,128)(2,1)S(1)}, u32[]{:S(2)}, u32[]{:S(2)}) collective-permute-start(bf16[768,256]{1,0:T(8,128)(2,1)S(1)} %pad_maximum_fusion.4), channel_id=1, source_target_pairs={{0,2},{1,3},{2,4},{3,5},{4,6},{5,7},{6,0},{7,1},{8,10},{9,11},{10,... | collective-permute-start | bytes 1179656 | tf_op jit(solution)/shard_map/ppermute | solution.py:28
  166.8 11.8 %collective-permute-start.36 = (bf16[768,256]{1,0:T(8,128)(2,1)S(1)}, bf16[768,256]{1,0:T(8,128)(2,1)S(1)}, u32[]{:S(2)}, u32[]{:S(2)}) collective-permute-start(bf16[768,256]{1,0:T(8,128)(2,1)S(1)} %pad_maximum_fusion.6), channel_id=1, source_target_pairs={{0,6},{1,7},{2,0},{3,1},{4,2},{5,3},{6,4},{7,5},{8,14},{9,15},{10,... | collective-permute-start | bytes 1179656 | tf_op jit(solution)/shard_map/ppermute | solution.py:28
  170.1 8.6 %collective-permute-start.35 = (bf16[768,256]{1,0:T(8,128)(2,1)S(1)}, bf16[768,256]{1,0:T(8,128)(2,1)S(1)}, u32[]{:S(2)}, u32[]{:S(2)}) collective-permute-start(bf16[768,256]{1,0:T(8,128)(2,1)S(1)} %copy-done.26), channel_id=1, source_target_pairs={{0,1},{1,0},{2,3},{3,2},{4,5},{5,4},{6,7},{7,6},{8,9},{9,8},{10,11... | collective-permute-start | bytes 1179656 | tf_op jit(solution)/shard_map/ppermute | solution.py:36
  170.1 12.0 %collective-permute-start.38 = (bf16[768,256]{1,0:T(8,128)(2,1)S(1)}, bf16[768,256]{1,0:T(8,128)(2,1)S(1)}, u32[]{:S(2)}, u32[]{:S(2)}) collective-permute-start(bf16[768,256]{1,0:T(8,128)(2,1)S(1)} %copy-done.25), channel_id=1, source_target_pairs={{0,1},{1,0},{2,3},{3,2},{4,5},{5,4},{6,7},{7,6},{8,9},{9,8},{10,11... | collective-permute-start | bytes 1179656 | tf_op jit(solution)/shard_map/ppermute | solution.py:36
  175.2 9.4 %collective-permute-start.23 = (bf16[768,256]{1,0:T(8,128)(2,1)S(1)}, bf16[768,256]{1,0:T(8,128)(2,1)S(1)}, u32[]{:S(2)}, u32[]{:S(2)}) collective-permute-start(bf16[768,256]{1,0:T(8,128)(2,1)S(1)} %copy-done.24), channel_id=1, source_target_pairs={{0,1},{1,0},{2,3},{3,2},{4,5},{5,4},{6,7},{7,6},{8,9},{9,8},{10,11... | collective-permute-start | bytes 1179656 | tf_op jit(solution)/shard_map/ppermute | solution.py:36
  178.5 10.6 %collective-permute-start.34 = (bf16[768,256]{1,0:T(8,128)(2,1)S(1)}, bf16[768,256]{1,0:T(8,128)(2,1)S(1)}, u32[]{:S(2)}, u32[]{:S(2)}) collective-permute-start(bf16[768,256]{1,0:T(8,128)(2,1)S(1)} %add_convert_fusion.3), channel_id=1, source_target_pairs={{0,2},{1,3},{2,4},{3,5},{4,6},{5,7},{6,0},{7,1},{8,10},{9,11},{10,... | collective-permute-start | bytes 1179656 | tf_op jit(solution)/shard_map/ppermute | solution.py:28
  178.8 10.3 %collective-permute-start.37 = (bf16[768,256]{1,0:T(8,128)(2,1)S(1)}, bf16[768,256]{1,0:T(8,128)(2,1)S(1)}, u32[]{:S(2)}, u32[]{:S(2)}) collective-permute-start(bf16[768,256]{1,0:T(8,128)(2,1)S(1)} %add_convert_fusion.2), channel_id=1, source_target_pairs={{0,6},{1,7},{2,0},{3,1},{4,2},{5,3},{6,4},{7,5},{8,14},{9,15},{10,... | collective-permute-start | bytes 1179656 | tf_op jit(solution)/shard_map/ppermute | solution.py:28
  182.3 8.9 %collective-permute-start.39 = (bf16[768,256]{1,0:T(8,128)(2,1)S(1)}, bf16[768,256]{1,0:T(8,128)(2,1)S(1)}, u32[]{:S(2)}, u32[]{:S(2)}) collective-permute-start(bf16[768,256]{1,0:T(8,128)(2,1)S(1)} %add_convert_fusion.1), channel_id=1, source_target_pairs={{0,8},{1,9},{2,10},{3,11},{4,12},{5,13},{6,14},{7,15},{8,0},{9,1},... | collective-permute-start | bytes 1179656 | tf_op jit(solution)/shard_map/ppermute | solution.py:32
  (4 other events, 8.3 us)

commit v2 on v1

v2 whole, which is shorter than its diff:
```python
import functools

import jax
import jax.numpy as jnp
import numpy as np
from jax import lax
from jax.experimental import pallas as pl
from jax.experimental.pallas import tpu as pltpu
from jax.sharding import PartitionSpec as P

SHARP = 0.2
DIV = 16.0
LOSS_SCALE = 65536.0
BF = jnp.bfloat16
F32 = jnp.float32
MIB = 1024 * 1024
BLK = 256
HBM_SPEC = pl.BlockSpec(memory_space=pltpu.HBM)


def y_perm(k):
    return [(z * 8 + y * 2 + c, z * 8 + ((y + k) % 4) * 2 + c) for z in range(2) for y in range(4) for c in range(2)]


Z_SWAP = [(v, v ^ 8) for v in range(16)]
CORE_SWAP = [(v, v ^ 1) for v in range(16)]


def to_y(x, k):
    return lax.ppermute(x, "vocab", y_perm(k % 4))


def to_z(x):
    return lax.ppermute(x, "vocab", Z_SWAP)


def to_core(x):
    return lax.ppermute(x, "vocab", CORE_SWAP)


def to_x(x, k):
    return lax.ppermute(x, "dp", [(g, ((g // 2 + k) % 4) * 2 + g % 2) for g in range(8)])


def to_zhi(x):
    return lax.ppermute(x, "dp", [(g, g ^ 1) for g in range(8)])


PLACES = ((0, 0), (1, 0), (-1, 0), (0, 1), (2, 0), (1, 1), (-1, 1), (2, 1))


def place_table():
    rows = []
    for v in range(16):
        z, y, core = v // 8, (v // 2) % 4, v % 2
        rows.append([((z + dz) % 2) * 4 + (y + dy) % 4 for dy, dz in PLACES] + [core] * 8)
    return np.array(rows, np.int32)


def matmul_cost(m, k, n):
    return pl.CostEstimate(flops=2 * m * k * n, bytes_accessed=2 * k * n, transcendentals=0)


def load_operands(copies, places, bn, steps, idx, xrefs, w, xs, ws, xsem, wsem):
    j = pl.program_id(0)
    nk = 2 * len(places)

    def x_copy(i):
        a, k, src, dst, n = copies[i]
        return pltpu.make_async_copy(
            xrefs[a].at[pl.ds(src, n), :], xs.at[pl.ds(dst, n), pl.ds(k * BLK, BLK)], xsem.at[i]
        )

    def w_copy(step, slot, k):
        core = idx[8]
        side = core if k % 2 == 0 else 1 - core
        row = pl.multiple_of((idx[places[k // 2]] * 2 + side) * BLK, BLK)
        col = pl.multiple_of(step * bn, bn)
        return pltpu.make_async_copy(
            w.at[pl.ds(row, BLK), pl.ds(col, bn)], ws.at[slot, pl.ds(k * BLK, BLK), :], wsem.at[slot, k]
        )

    slot = lax.rem(j, 2)

    @pl.when(j == 0)
    def _():
        for k in range(nk):
            w_copy(0, 0, k).start()
        for i in range(len(copies)):
            x_copy(i).start()

    @pl.when(j + 1 < steps)
    def _():
        for k in range(nk):
            w_copy(j + 1, 1 - slot, k).start()

    @pl.when(j == 0)
    def _():
        for i in range(len(copies)):
            x_copy(i).wait()

    for k in range(nk):
        w_copy(j, slot, k).wait()
    return slot


def logits_kernel(copies, places, nx, bn, steps, has_acc, idx, *refs):
    xrefs = refs[:nx]
    w = refs[nx]
    pos = nx + 1
    acc = None
    if has_acc:
        acc = refs[pos]
        pos += 1
    out, xs, ws, xsem, wsem = refs[pos:]
    slot = load_operands(copies, places, bn, steps, idx, xrefs, w, xs, ws, xsem, wsem)
    res = jnp.dot(xs[...], ws[slot], preferred_element_type=F32)
    if has_acc:
        res = res + acc[...]
    out[...] = res


def logits_part(arrays, copies, places, idx, w, acc, out_space=None):
    rows = 768
    cols = w.shape[1]
    nk = 2 * len(places)
    bn = 512
    steps = cols // bn
    any_spec = pl.BlockSpec(memory_space=pl.ANY)
    blk = pl.BlockSpec((rows, bn), lambda j, *_: (0, j))
    ins = list(arrays) + [w] + ([acc] if acc is not None else [])
    return pl.pallas_call(
        functools.partial(logits_kernel, copies, places, len(arrays), bn, steps, acc is not None),
        grid_spec=pltpu.PrefetchScalarGridSpec(
            num_scalar_prefetch=1,
            grid=(steps,),
            in_specs=[any_spec] * len(arrays) + [HBM_SPEC] + ([blk] if acc is not None else []),
            out_specs=blk,
            scratch_shapes=[
                pltpu.VMEM((rows, nk * BLK), BF),
                pltpu.VMEM((2, nk * BLK, bn), BF),
                pltpu.SemaphoreType.DMA((len(copies),)),
                pltpu.SemaphoreType.DMA((2, nk)),
            ],
        ),
        out_shape=jax.ShapeDtypeStruct((rows, cols), F32) if out_space is None else out_space((rows, cols), F32),
        compiler_params=pltpu.CompilerParams(vmem_limit_bytes=18 * MIB),
        name="logits_part",
        cost_estimate=matmul_cost(rows, nk * BLK, cols),
    )(idx, *ins)


def pool_kernel(copies, places, nx, bn, steps, seqs, idx, lens, *refs):
    xrefs = refs[:nx]
    w, acc, expo, stats, pooled, xs, ws, xsem, wsem = refs[nx:]
    slot = load_operands(copies, places, bn, steps, idx, xrefs, w, xs, ws, xsem, wsem)
    logits = jnp.dot(xs[...], ws[slot], preferred_element_type=F32) + acc[...]
    smooth, sums = [], []
    for s, (start, n) in enumerate(seqs):
        part = logits[start : start + n] * (1.0 / SHARP)
        live = lax.broadcasted_iota(jnp.int32, (n, 1), 0) < lens[s]
        part = jnp.where(live, part, -1e30)
        top = jnp.max(part, axis=0, keepdims=True)
        e = jnp.exp(part - top)
        total = jnp.sum(e, axis=0, keepdims=True)
        expo[pl.ds(start, n), :] = e.astype(BF)
        smooth.append(SHARP * (top + jnp.log(total)))
        sums.append(total)
    both = jnp.concatenate(smooth + sums, axis=0)
    stats[...] = both
    pooled[...] = jnp.log1p(jnp.maximum(both[:4], 0.0))


def logits_pool(arrays, copies, places, idx, lens, w, acc, seqs):
    rows = 768
    cols = w.shape[1]
    nk = 2 * len(places)
    bn = 512
    steps = cols // bn
    any_spec = pl.BlockSpec(memory_space=pl.ANY)
    blk = pl.BlockSpec((rows, bn), lambda j, *_: (0, j))
    return pl.pallas_call(
        functools.partial(pool_kernel, copies, places, len(arrays), bn, steps, seqs),
        grid_spec=pltpu.PrefetchScalarGridSpec(
            num_scalar_prefetch=2,
            grid=(steps,),
            in_specs=[any_spec] * len(arrays) + [HBM_SPEC, blk],
            out_specs=[
                blk,
                pl.BlockSpec((8, bn), lambda j, *_: (0, j)),
                pl.BlockSpec((4, bn), lambda j, *_: (0, j)),
            ],
            scratch_shapes=[
                pltpu.VMEM((rows, nk * BLK), BF),
                pltpu.VMEM((2, nk * BLK, bn), BF),
                pltpu.SemaphoreType.DMA((len(copies),)),
                pltpu.SemaphoreType.DMA((2, nk)),
            ],
        ),
        out_shape=[
            pltpu.HBM((rows, cols), BF),
            jax.ShapeDtypeStruct((8, cols), F32),
            jax.ShapeDtypeStruct((4, cols), F32),
        ],
        compiler_params=pltpu.CompilerParams(vmem_limit_bytes=20 * MIB),
        name="logits_pool",
        cost_estimate=matmul_cost(rows, nk * BLK, cols),
    )(idx, lens, *arrays, w, acc)


def exact_dot(a, b, dims):
    return lax.dot_general(a, b, (dims, ((), ())), precision=lax.Precision.HIGHEST, preferred_element_type=F32)


def split_kinds(a, b):
    every = jnp.concatenate([a, b], axis=0)
    q = jnp.concatenate([every[i : i + 2] for i in range(0, every.shape[0], 4)], axis=0)
    p = jnp.concatenate([every[i + 2 : i + 4] for i in range(0, every.shape[0], 4)], axis=0)
    return q, p


def gram_kernel(a, b, out):
    q, p = split_kinds(a[...], b[...])
    res = exact_dot(q, p, ((1,), (1,)))
    res = jnp.concatenate([res[:8], res[8:], jnp.zeros((8, 96), F32)], axis=1)
    for i in range(out.shape[0]):
        out[i] = res


def gram(a, b, copies):
    return pl.pallas_call(
        gram_kernel,
        out_shape=jax.ShapeDtypeStruct((copies, 8, 128), F32),
        compiler_params=pltpu.CompilerParams(vmem_limit_bytes=4 * MIB),
        name="gram",
    )(a, b)


def nt_dot(a, b):
    return lax.dot_general(a, b, (((1,), (1,)), ((), ())), preferred_element_type=F32)


def store_halves(core, res, mine, sib):
    left, right = res[:, :BLK], res[:, BLK:]

    @pl.when(core == 0)
    def _():
        mine[...] = left
        sib[...] = right.astype(BF)

    @pl.when(core != 0)
    def _():
        mine[...] = right
        sib[...] = left.astype(BF)


def first_grad_kernel(
    seqs, place, total_queries, idx, parts, pa, pb, stats, picked, expo, w, dl, loss, mine, sib, es, ws, esem, wsem
):
    e_copies = [
        pltpu.make_async_copy(expo.at[pl.ds(start, n), :], es.at[pl.ds(start, n), :], esem.at[s])
        for s, (start, n) in enumerate(seqs)
    ]
    row0 = pl.multiple_of(idx[place] * (2 * BLK), 2 * BLK)
    w_copy = pltpu.make_async_copy(w.at[pl.ds(row0, 2 * BLK), :], ws, wsem)
    for c in e_copies:
        c.start()
    w_copy.start()
    scores = parts[0]
    for i in range(1, parts.shape[0]):
        scores = scores + parts[i]
    scores = jnp.concatenate([scores[:, :16], scores[:, 16:32]], axis=0) / DIV
    top = jnp.max(scores, axis=1, keepdims=True)
    lse = top + jnp.log(jnp.sum(jnp.exp(scores - top), axis=1, keepdims=True))
    pick = picked[...]
    losses = lse - jnp.sum(scores * pick, axis=1, keepdims=True)
    loss[...] = jnp.broadcast_to(losses[:8], loss.shape)
    dscores = (jnp.exp(scores - lse) - pick) * (LOSS_SCALE / total_queries)
    q, p = split_kinds(pa[...], pb[...])
    dq = exact_dot(dscores[:8], p, ((1,), (0,)))
    dp = exact_dot(dscores.T[:8], q, ((1,), (0,)))
    dpooled = jnp.concatenate([dq[:2], dp[:2]], axis=0) / DIV
    smooth = stats[0:4, :]
    gate = jnp.where(smooth > 0, 1.0 / (1.0 + jnp.maximum(smooth, 0.0)), 0.0)
    g = dpooled * gate / stats[4:8, :]
    for s, (start, n) in enumerate(seqs):
        e_copies[s].wait()
        dl[pl.ds(start, n), :] = (es[pl.ds(start, n), :].astype(F32) * g[s : s + 1, :]).astype(BF)
    w_copy.wait()
    store_halves(idx[8], nt_dot(dl[...], ws[...]), mine, sib)


def first_grad(place, idx, parts, pa, pb, stats, picked, expo, w, seqs, total_queries):
    rows, cols = expo.shape
    vm = pl.BlockSpec(memory_space=pltpu.VMEM)
    return pl.pallas_call(
        functools.partial(first_grad_kernel, seqs, place, total_queries),
        in_specs=[pl.BlockSpec(memory_space=pltpu.SMEM)] + [vm] * 5 + [HBM_SPEC] * 2,
        out_specs=[vm] * 4,
        scratch_shapes=[
            pltpu.VMEM((rows, cols), BF),
            pltpu.VMEM((2 * BLK, cols), BF),
            pltpu.SemaphoreType.DMA((len(seqs),)),
            pltpu.SemaphoreType.DMA,
        ],
        out_shape=[
            jax.ShapeDtypeStruct((rows, cols), BF),
            jax.ShapeDtypeStruct((8, 128), F32),
            jax.ShapeDtypeStruct((rows, BLK), F32),
            jax.ShapeDtypeStruct((rows, BLK), BF),
        ],
        compiler_params=pltpu.CompilerParams(vmem_limit_bytes=22 * MIB),
        name="first_grad",
        cost_estimate=matmul_cost(rows, 2 * BLK, cols),
    )(idx, parts, pa, pb, stats, picked, pltpu.with_memory_space_constraint(expo, pltpu.HBM), w)


def grad_kernel(first, n, idx, dl, w, mine, sib, ws, wsem):
    i = pl.program_id(0)

    def w_copy(step, slot):
        row = pl.multiple_of(idx[first + step] * (2 * BLK), 2 * BLK)
        return pltpu.make_async_copy(w.at[pl.ds(row, 2 * BLK), :], ws.at[slot], wsem.at[slot])

    slot = lax.rem(i, 2)

    @pl.when(i == 0)
    def _():
        w_copy(0, 0).start()

    @pl.when(i + 1 < n)
    def _():
        w_copy(i + 1, 1 - slot).start()

    w_copy(i, slot).wait()
    store_halves(idx[8], nt_dot(dl[...], ws[slot]), mine, sib)


def grad_part(first, n, idx, dl, w):
    rows, cols = dl.shape
    out = pl.BlockSpec((rows, BLK), lambda i, idx: (i, 0))
    return pl.pallas_call(
        functools.partial(grad_kernel, first, n),
        grid_spec=pltpu.PrefetchScalarGridSpec(
            num_scalar_prefetch=1,
            grid=(n,),
            in_specs=[pl.BlockSpec((rows, cols), lambda i, idx: (0, 0)), HBM_SPEC],
            out_specs=[out, out],
            scratch_shapes=[pltpu.VMEM((2, 2 * BLK, cols), BF), pltpu.SemaphoreType.DMA((2,))],
        ),
        out_shape=[jax.ShapeDtypeStruct((n * rows, BLK), F32), jax.ShapeDtypeStruct((n * rows, BLK), BF)],
        compiler_params=pltpu.CompilerParams(vmem_limit_bytes=18 * MIB),
        name="grad_part",
        cost_estimate=matmul_cost(n * rows, 2 * BLK, cols),
    )(idx, dl, w)


def add_kernel(spec, n_mine, *refs):
    outs = refs[len(refs) - n_mine :]
    for i in range(n_mine):
        outs[i][...] = refs[i][...]
    for i, a, src, dst, n in spec:
        outs[i][pl.ds(dst, n), :] = outs[i][pl.ds(dst, n), :] + refs[n_mine + a][pl.ds(src, n), :].astype(F32)


def add_arrived(mine, arrived, spec):
    return pl.pallas_call(
        functools.partial(add_kernel, spec, len(mine)),
        out_shape=[jax.ShapeDtypeStruct(m.shape, F32) for m in mine],
        compiler_params=pltpu.CompilerParams(vmem_limit_bytes=12 * MIB),
        name="add_arrived",
        cost_estimate=matmul_cost(4096, 2048, 2048),
    )(*mine, *arrived)


def after(x, *others):
    return lax.optimization_barrier((x,) + others)[0]


def on_device(query_hidden, passage_hidden, head_weight, query_mask, passage_mask, positive):
    q_count, q_len, width = query_hidden.shape
    p_count, p_len, _ = passage_hidden.shape
    w = pltpu.with_memory_space_constraint(head_weight, pltpu.HBM)
    split = q_count * q_len
    seqs = tuple((i * q_len, q_len) for i in range(q_count)) + tuple(
        (split + i * p_len, p_len) for i in range(p_count)
    )
    own = jnp.concatenate([query_hidden.reshape(split, width), passage_hidden.reshape(p_count * p_len, width)], axis=0)
    idx = lax.dynamic_index_in_dim(jnp.asarray(place_table()), lax.axis_index("vocab"), 0, keepdims=False)
    at = {p: i for i, p in enumerate(PLACES)}
    h = 384

    x10, xm0, x01 = to_y(own, -1), to_y(own, 1), to_z(own)
    own_s = to_core(own)
    acc = logits_part([own, own_s], ((0, 0, 0, 0, 768), (1, 1, 0, 0, 768)), (0,), idx, w, None)
    x10, xm0, x01, acc = lax.optimization_barrier((x10, xm0, x01, acc))
    f1 = to_y(jnp.concatenate([x10[:h], x01[h:]], axis=0), -1)
    f2 = to_y(jnp.concatenate([x01[h:], xm0[h:]], axis=0), 1)
    f3 = to_z(jnp.concatenate([x10[:h], xm0[:h]], axis=0))
    near = [t for p in (x10, xm0, x01) for t in (p, to_core(p))]
    whole = tuple((i, i, 0, 0, 768) for i in range(6))
    acc = logits_part(near, whole, (1, 2, 3), idx, w, acc, pltpu.HBM)
    f1, f2, f3, acc = lax.optimization_barrier((f1, f2, f3, acc))
    g1 = to_y(f3[:256], -1)
    g2 = to_z(jnp.concatenate([f1[256:384], f2[384:512]], axis=0))
    g3 = to_y(f2[128:384], 1)
    mid = [t for p in (f1, f2, f3) for t in (p, to_core(p))]
    mid_copies = []
    for c in range(2):
        mid_copies += [
            (0 + c, 0 + c, 0, 0, h),
            (2 + c, 0 + c, h, h, h),
            (4 + c, 2 + c, 0, 0, h),
            (0 + c, 2 + c, h, h, h),
            (4 + c, 4 + c, h, 0, h),
            (2 + c, 4 + c, 0, h, h),
        ]
    acc = logits_part(mid, tuple(mid_copies), (4, 5, 6), idx, w, pltpu.with_memory_space_constraint(acc, pltpu.HBM))
    g1, g2, g3, acc = lax.optimization_barrier((g1, g2, g3, acc))
    last = [t for p in (g1, g2, g3) for t in (p, to_core(p))]
    last_copies = tuple((2 * i + c, c, 0, 256 * i, 256) for i in range(3) for c in range(2))
    query_mask, passage_mask, positive = lax.optimization_barrier((query_mask, passage_mask, positive, x10))[:3]
    lens = jnp.concatenate([jnp.sum(query_mask > 0, axis=1), jnp.sum(passage_mask > 0, axis=1)]).astype(jnp.int32)
    expo, stats, pooled = logits_pool(last, last_copies, (7,), idx, lens, w, acc, seqs)

    pa = jnp.concatenate([pooled] + [to_x(pooled, -k) for k in (1, 2, 3)], axis=0)
    pb = to_zhi(pa)
    parts = lax.all_to_all(gram(pa, pb, 16), "vocab", 0, 0)

    group = lax.axis_index("dp")
    slot = jnp.arange(16, dtype=jnp.int32)
    place = slot // 2
    gx = (group // 2 + place % 4) % 4
    gz = (group % 2 + place // 4) % 2
    seq = (gx * 2 + gz) * 2 + slot % 2
    target = positive[seq]
    picked = (target[:, None] == seq[None, :]).astype(F32)

    dl, loss, m21, s21 = first_grad(7, idx, parts, pa, pb, stats, picked, expo, w, seqs, positive.shape[0])
    m20, s20 = grad_part(4, 1, idx, dl, w)
    t21 = (m21 + to_core(s21)).astype(BF)
    def rows(x, i):
        return x[768 * i : 768 * (i + 1)]

    r1, r2, r3 = to_y(t21[:256], 1), to_z(t21[256:512]), to_y(t21[512:], -1)
    mb, sb = grad_part(5, 2, idx, after(dl, t21), w)
    sb = to_core(sb)
    mb, m20 = add_arrived((mb, m20), (r1, r2, r3), ((0, 0, 0, 0, 256), (0, 2, 0, 768 + 512, 256), (1, 1, 0, 256, 256)))
    t20 = (m20 + to_core(s20)).astype(BF)
    t11 = (rows(mb, 0) + rows(sb, 0)).astype(BF)
    tm1 = (rows(mb, 1) + rows(sb, 1)).astype(BF)
    c1 = jnp.concatenate([t20[:h], t11[h:]], axis=0)
    c2 = jnp.concatenate([tm1[h:], t20[h:]], axis=0)
    c3 = jnp.concatenate([t11[:h], tm1[:h]], axis=0)
    c1, c2, c3, dl = lax.optimization_barrier((c1, c2, c3, dl))
    u1, u2, u3 = to_y(c1, 1), to_y(c2, -1), to_z(c3)
    mc, sc = grad_part(1, 3, idx, dl, w)
    sc = to_core(sc)
    (mc,) = add_arrived(
        (mc,),
        (u1, u2, u3),
        (
            (0, 0, 0, 0, h),
            (0, 2, 0, 0, h),
            (0, 2, h, 768, h),
            (0, 1, h, 768 + h, h),
            (0, 0, h, 1536 + h, h),
            (0, 1, 0, 1536 + h, h),
        ),
    )
    t10, tm0, t01 = ((rows(mc, i) + rows(sc, i)).astype(BF) for i in range(3))
    t10, tm0, t01, dl = lax.optimization_barrier((t10, tm0, t01, dl))
    v1, v2, v3 = to_y(t10, 1), to_y(tm0, -1), to_z(t01)
    md, sd = grad_part(0, 1, idx, dl, w)
    k00 = lax.optimization_barrier(md + v1.astype(F32) + v2.astype(F32) + v3.astype(F32))
    sd = to_core(sd)

    def total(a, b):
        return (k00[a:b] + sd[a:b].astype(F32)).astype(BF)

    return (
        total(0, split).reshape(q_count, q_len, width),
        total(split, 768).reshape(p_count, p_len, width),
        loss[:q_count, 0],
    )


def solution(mesh):
    return jax.shard_map(
        on_device,
        mesh=mesh,
        in_specs=(
            P("dp", None, "vocab"),
            P("dp", None, "vocab"),
            P(None, "vocab"),
            P("dp", None),
            P("dp", None),
            P(),
        ),
        out_specs=(P("dp", None, "vocab"), P("dp", None, "vocab"), P("dp")),
        check_vma=False,
    )
```

time: 193 us -> 139 us (0.72)
  waiting for transfers between devices: 48.9 us -> 28.8 us
  Pallas kernels: 80.1 us -> 60.7 us
  local copies, waits for them, and re-layouts: 9.86 us -> 2.2 us
  other arithmetic: 8.29 us -> 4.09 us
  starting transfers between devices: 44.4 us -> 41.3 us
    pallas_call x7 -> x12, Pallas kernels: 80.1 us -> 60.7 us  [the longest x3 24.7 us: logits_part(): pl.pallas_call(functools.partial(logits_kernel, copies, places, len(array...]
    ppermute x12, waiting for transfers between devices: 26.4 us -> 9.28 us  [to_y(): return lax.ppermute(x, 'vocab', y_perm(k % 4))]
    ppermute x6, waiting for transfers between devices: 10.5 us -> 2.58 us  [to_z(): return lax.ppermute(x, 'vocab', Z_SWAP)]
    ppermute x18 -> x15, waiting for transfers between devices: 0.05 us -> 4.4 us  [to_core(): return lax.ppermute(x, 'vocab', CORE_SWAP)]
    unnamed x56 -> x8, local copies, waits for them, and re-layouts: 3.12 us -> 0.03 us
    ppermute x12, starting transfers between devices: 19.8 us -> 17.2 us  [to_y(): return lax.ppermute(x, 'vocab', y_perm(k % 4))]
    ppermute x18 -> x15, starting transfers between devices: 3.89 us -> 2.7 us  [to_core(): return lax.ppermute(x, 'vocab', CORE_SWAP)]
  transfers between devices with their start and end apart: 41 -> 38, of which waited for: 15 -> 16; matrix products, arithmetic and copies ran while one was open for 5% -> 2% of each run, Pallas kernels for 31% -> 34%
where the time goes in v2:
time: 139 us; the launch traced here: 138 us
  Pallas kernels  60.7 us (44%)
  starting transfers between devices  41.3 us (30%)
  waiting for transfers between devices  28.8 us (21%)
  other arithmetic  4.09 us (3%)
  local copies, waits for them, and re-layouts  2.2 us (2%)
    pallas_call x3, Pallas kernels, logits_part(): pl.pallas_call(functools.partial(logits_kernel, copies, places, len(array...  24.7 us
    pallas_call x4, Pallas kernels, grad_part(): pl.pallas_call(functools.partial(grad_kernel, first, n), grid_spec=pltpu....  22.2 us
    ppermute x12, starting transfers between devices, to_y(): return lax.ppermute(x, 'vocab', y_perm(k % 4))  17.2 us
    ppermute x12, waiting for transfers between devices, to_y(): return lax.ppermute(x, 'vocab', y_perm(k % 4))  9.28 us
    ppermute x6, starting transfers between devices, to_z(): return lax.ppermute(x, 'vocab', Z_SWAP)  8.33 us
    pallas_call x1, Pallas kernels, logits_pool(): pl.pallas_call(functools.partial(pool_kernel, copies, places, len(arrays)...  7.13 us
    all_to_all x1, waiting for transfers between devices, on_device(): parts = lax.all_to_all(gram(pa, pb, 16), 'vocab', 0, 0)  6.04 us
    pallas_call x1, Pallas kernels, first_grad(): pl.pallas_call(functools.partial(first_grad_kernel, seqs, place, total_qu...  5.12 us
  transfers between devices with their start and end apart: 38, of which 16 were waited for; matrix products, arithmetic and copies ran while one was open for 2% of the time, Pallas kernels for 34%

profile of v2, /device:TPU:0, one launch (start us, length us, event | category | flops | bytes accessed | tf_op | source)
XLA Modules:
  0.0 138.1 jit_solution(1833692913537125112)
XLA Ops:
  0.6 1.0 pad_maximum_fusion.2.refs_0_
  1.8 3.2 %collective-permute-start = (bf16[768,256]{1,0:T(8,128)(2,1)S(1)}, bf16[768,256]{1,0:T(8,128)(2,1)S(1)}, u32[]{:S(2)}, u32[]{:S(2)}) collective-permute-start(bf16[768,256]{1,0:T(8,128)(2,1)S(1)} %pad_maximum_fusion.2.refs_0_), channel_id=1, source_target_pairs={{0,6},{1,7},{2,0},{3,1},{4,2},{5,3},{6,4},{7,5},{8,14},{9,15},{10,... | collective-permute-start | bytes 1179656 | tf_op jit(solution)/shard_map/ppermute | solution.py:30
  4.9 1.9 %collective-permute-start.2 = (bf16[768,256]{1,0:T(8,128)(2,1)S(1)}, bf16[768,256]{1,0:T(8,128)(2,1)S(1)}, u32[]{:S(2)}, u32[]{:S(2)}) collective-permute-start(bf16[768,256]{1,0:T(8,128)(2,1)S(1)} %pad_maximum_fusion.2.refs_0_), channel_id=1, source_target_pairs={{0,8},{1,9},{2,10},{3,11},{4,12},{5,13},{6,14},{7,15},{8,0},{9,1},... | collective-permute-start | bytes 1179656 | tf_op jit(solution)/shard_map/ppermute | solution.py:34
  6.8 0.7 dynamic-slice_bitcast_fusion.idx
  7.5 4.7 %logits_part.3.refs_7_ = f32[768,2048]{1,0:T(8,128)S(1)} custom-call(s32[16]{0:T(128)S(1)} %dynamic-slice_bitcast_fusion.idx, bf16[768,256]{1,0:T(8,128)(2,1)S(1)} %pad_maximum_fusion.2.refs_0_, bf16[768,256]{1,0:T(8,128)(2,1)S(1)} %collective-permute-done.3.refs_1_, bf16[4096,2048]{1,0:T(8,128)(2,1)} %w.9), custom_call_target="tpu_custom_call" | custom-call | flops 1610612736 | bytes 2097152 | tf_op jit(solution)/shard_map/logits_part/pallas_call | solution.py:132
  12.3 1.6 %collective-permute-done.refs_0_ = bf16[768,256]{1,0:T(8,128)(2,1)S(1)} collective-permute-done((bf16[768,256]{1,0:T(8,128)(2,1)S(1)}, bf16[768,256]{1,0:T(8,128)(2,1)S(1)}, u32[]{:S(2)}, u32[]{:S(2)}) %collective-permute-start) | collective-permute-done | bytes 393248 | tf_op jit(solution)/shard_map/ppermute | solution.py:30
  13.9 3.4 %collective-permute-done.1.refs_2_ = bf16[768,256]{1,0:T(8,128)(2,1)S(1)} collective-permute-done((bf16[768,256]{1,0:T(8,128)(2,1)S(1)}, bf16[768,256]{1,0:T(8,128)(2,1)S(1)}, u32[]{:S(2)}, u32[]{:S(2)}) %collective-permute-start.1) | collective-permute-done | bytes 393248 | tf_op jit(solution)/shard_map/ppermute | solution.py:30
  17.3 0.5 collective-permute-start.8
  18.0 2.0 %collective-permute-start.4 = (bf16[768,256]{1,0:T(8,128)(2,1)S(1)}, bf16[768,256]{1,0:T(8,128)(2,1)S(1)}, u32[]{:S(2)}, u32[]{:S(2)}) collective-permute-start(bf16[768,256]{1,0:T(8,128)(2,1)S(1)} %get-tuple-element.102), channel_id=1, source_target_pairs={{0,6},{1,7},{2,0},{3,1},{4,2},{5,3},{6,4},{7,5},{8,14},{9,15},{10,... | collective-permute-start | bytes 1179656 | tf_op jit(solution)/shard_map/ppermute | solution.py:30
  20.0 0.1 collective-permute-start.5
  20.1 1.9 %collective-permute-start.6 = (bf16[768,256]{1,0:T(8,128)(2,1)S(1)}, bf16[768,256]{1,0:T(8,128)(2,1)S(1)}, u32[]{:S(2)}, u32[]{:S(2)}) collective-permute-start(bf16[768,256]{1,0:T(8,128)(2,1)S(1)} %get-tuple-element.101), channel_id=1, source_target_pairs={{0,8},{1,9},{2,10},{3,11},{4,12},{5,13},{6,14},{7,15},{8,0},{9,1},... | collective-permute-start | bytes 1179656 | tf_op jit(solution)/shard_map/ppermute | solution.py:34
  22.0 9.9 %logits_part.4.refs_7_ = f32[768,2048]{1,0:T(8,128)} custom-call(s32[16]{0:T(128)S(1)} %dynamic-slice_bitcast_fusion.idx, bf16[768,256]{1,0:T(8,128)(2,1)S(1)} %collective-permute-done.refs_0_, bf16[768,256]{1,0:T(8,128)(2,1)S(1)} %collective-permute-done.7.refs_1_, bf16[768,256]{1,0:T(8,128)(2,1)S(1)} %collective-permute-done.1.refs_2_, ...), custom_call_target="tpu_custom_call" | custom-call | flops 4831838208 | bytes 6291456 | tf_op jit(solution)/shard_map/logits_part/pallas_call | solution.py:132
  31.9 0.5 collective-permute-done.5.refs_2_
  32.5 0.5 collective-permute-start.14
  33.0 0.1 fusion.5
  33.2 1.8 %collective-permute-start.11 = (bf16[256,256]{1,0:T(8,128)(2,1)S(1)}, bf16[256,256]{1,0:T(8,128)(2,1)S(1)}, u32[]{:S(2)}, u32[]{:S(2)}) collective-permute-start(bf16[256,256]{1,0:T(8,128)(2,1)S(1)} %pad_maximum_fusion.7), channel_id=1, source_target_pairs={{0,8},{1,9},{2,10},{3,11},{4,12},{5,13},{6,14},{7,15},{8,0},{9,1},... | collective-permute-start | bytes 393224 | tf_op jit(solution)/shard_map/ppermute | solution.py:34
  35.0 1.7 %collective-permute-start.10 = (bf16[256,256]{1,0:T(8,128)(2,1)S(1)}, bf16[256,256]{1,0:T(8,128)(2,1)S(1)}, u32[]{:S(2)}, u32[]{:S(2)}) collective-permute-start(bf16[256,256]{1,0:T(8,128)(2,1)S(1)} %slice.102), channel_id=1, source_target_pairs={{0,6},{1,7},{2,0},{3,1},{4,2},{5,3},{6,4},{7,5},{8,14},{9,15},{10,... | collective-permute-start | bytes 393224 | tf_op jit(solution)/shard_map/ppermute | solution.py:30
  36.7 0.3 collective-permute-start.12
  37.0 10.1 %logits_part.5.refs_7_ = f32[768,2048]{1,0:T(8,128)S(1)} custom-call(s32[16]{0:T(128)S(1)} %dynamic-slice_bitcast_fusion.idx, bf16[768,256]{1,0:T(8,128)(2,1)S(1)} %collective-permute-done.4.refs_0_, bf16[768,256]{1,0:T(8,128)(2,1)S(1)} %collective-permute-done.13.refs_1_, bf16[768,256]{1,0:T(8,128)(2,1)S(1)} %collective-permute-done.5.refs_2_, ...), custom_call_target="tpu_custom_call" | custom-call | flops 4831838208 | bytes 6291456 | tf_op jit(solution)/shard_map/logits_part/pallas_call | solution.py:132
  47.2 0.5 collective-permute-start.17
  47.8 0.1 fusion.6
  48.0 0.5 collective-permute-done.16.refs_1_
  48.6 0.2 collective-permute-done.17.refs_3_
  48.8 0.3 collective-permute-done.18.refs_5_
  49.1 7.1 %logits_pool.1 = (bf16[768,2048]{1,0:T(8,128)(2,1)}, f32[8,2048]{1,0:T(8,128)S(1)}, f32[4,2048]{1,0:T(4,128)S(1)}) custom-call(s32[16]{0:T(128)S(1)} %dynamic-slice_bitcast_fusion.idx, s32[4]{0:T(128)S(1)} %pad_add_fusion.lens, bf16[256,256]{1,0:T(8,128)(2,1)S(1)} %collective-permute-done.10.refs_0_, bf16[256,256]{1,0:T(8,128)(2,1)S(1)} %collective-permute-done.16.refs_1_, ...), custom_call_target="tpu_custom_call" | custom-call | flops 1610612736 | bytes 2097152 | tf_op jit(solution)/shard_map/logits_pool/pallas_call | solution.py:182
  56.2 2.8 %collective-permute-start.19 = (f32[4,2048]{1,0:T(4,128)S(1)}, f32[4,2048]{1,0:T(4,128)S(1)}, u32[]{:S(2)}, u32[]{:S(2)}) collective-permute-start(f32[4,2048]{1,0:T(4,128)S(1)} %get-tuple-element.58), channel_id=1, source_target_pairs={{0,96},{16,112},{32,0},{48,16},{64,32},{80,48},{96,64},{112,80},{1... | collective-permute-start | bytes 98312 | tf_op jit(solution)/shard_map/ppermute | solution.py:42
  59.1 0.8 collective-permute-start.20
  59.9 0.9 collective-permute-start.21
  60.9 3.6 %collective-permute-done.20 = f32[4,2048]{1,0:T(4,128)S(1)} collective-permute-done((f32[4,2048]{1,0:T(4,128)S(1)}, f32[4,2048]{1,0:T(4,128)S(1)}, u32[]{:S(2)}, u32[]{:S(2)}) %collective-permute-start.20) | collective-permute-done | bytes 32800 | tf_op jit(solution)/shard_map/ppermute | solution.py:42
  64.5 0.5 collective-permute-done.21
  65.0 3.7 %collective-permute-start.22 = (f32[16,2048]{1,0:T(8,128)S(1)}, f32[16,2048]{1,0:T(8,128)S(1)}, u32[]{:S(2)}, u32[]{:S(2)}) collective-permute-start(f32[16,2048]{1,0:T(8,128)S(1)} %pad_maximum_fusion.8.a.pa), channel_id=1, source_target_pairs={{0,16},{16,0},{32,48},{48,32},{64,80},{80,64},{96,112},{112,96},{1... | collective-permute-start | bytes 393224 | tf_op jit(solution)/shard_map/ppermute | solution.py:46
  68.7 0.7 gather_fusion
  69.4 2.2 %collective-permute-done.22.b.pb = f32[16,2048]{1,0:T(8,128)S(1)} collective-permute-done((f32[16,2048]{1,0:T(8,128)S(1)}, f32[16,2048]{1,0:T(8,128)S(1)}, u32[]{:S(2)}, u32[]{:S(2)}) %collective-permute-start.22) | collective-permute-done | bytes 131104 | tf_op jit(solution)/shard_map/ppermute | solution.py:46
  71.6 1.0 gram.1
  72.6 4.9 %all-to-all-start = ((f32[16,8,128]{2,1,0:T(8,128)}), f32[16,8,128]{2,1,0:T(8,128)S(1)}, u32[]{:S(2)}, u32[]{:S(2)}) async-start(f32[16,8,128]{2,1,0:T(8,128)} %gram.1), calls=%async_computation | async-start | bytes 131072 | tf_op jit(solution)/shard_map/all_to_all | solution.py:428
  77.6 6.0 %all-to-all-done.parts = f32[16,8,128]{2,1,0:T(8,128)S(1)} async-done(((f32[16,8,128]{2,1,0:T(8,128)}), f32[16,8,128]{2,1,0:T(8,128)S(1)}, u32[]{:S(2)}, u32[]{:S(2)}) %all-to-all-start) | async-done | bytes 65568 | tf_op jit(solution)/shard_map/all_to_all | solution.py:428
  83.6 5.1 %first_grad.1 = (bf16[768,2048]{1,0:T(8,128)(2,1)S(1)}, f32[8,128]{1,0:T(8,128)S(1)}, f32[768,256]{1,0:T(8,128)S(1)}, bf16[768,256]{1,0:T(8,128)(2,1)S(1)}) custom-call(s32[16]{0:T(128)S(1)} %dynamic-slice_bitcast_fusion.idx, f32[16,8,128]{2,1,0:T(8,128)S(1)} %all-to-all-done.parts, f32[16,2048]{1,0:T(8,128)S(1)} %pad_maximum_fusion.8.a.pa, ...), custom_call_target="tpu_custom_call" | custom-call | flops 1610612736 | bytes 2097152 | tf_op jit(solution)/shard_map/first_grad/pallas_call | solution.py:296
  88.7 0.2 collective-permute-start.23
  88.9 4.1 %grad_part.5 = (f32[768,256]{1,0:T(8,128)S(1)}, bf16[768,256]{1,0:T(8,128)(2,1)S(1)}) custom-call(s32[16]{0:T(128)S(1)} %dynamic-slice_bitcast_fusion.idx, bf16[768,2048]{1,0:T(8,128)(2,1)S(1)} %get-tuple-element.78.dl, bf16[4096,2048]{1,0:T(8,128)(2,1)} %w.9), custom_call_target="tpu_custom_call" | custom-call | flops 1610612736 | bytes 2097152 | tf_op jit(solution)/shard_map/grad_part/pallas_call | solution.py:342
  93.0 0.5 collective-permute-start.27
  93.5 0.1 add_convert_fusion.3
  93.6 0.6 collective-permute-start.24
  94.3 0.7 collective-permute-start.25
  94.9 2.7 %collective-permute-start.26 = (bf16[256,256]{1,0:T(8,128)(2,1)S(1)}, bf16[256,256]{1,0:T(8,128)(2,1)S(1)}, u32[]{:S(2)}, u32[]{:S(2)}) collective-permute-start(bf16[256,256]{1,0:T(8,128)(2,1)S(1)} %get-tuple-element.96), channel_id=1, source_target_pairs={{0,6},{1,7},{2,0},{3,1},{4,2},{5,3},{6,4},{7,5},{8,14},{9,15},{10,... | collective-permute-start | bytes 393224 | tf_op jit(solution)/shard_map/ppermute | solution.py:30
  97.6 6.0 %grad_part.4 = (f32[1536,256]{1,0:T(8,128)S(1)}, bf16[1536,256]{1,0:T(8,128)(2,1)S(1)}) custom-call(s32[16]{0:T(128)S(1)} %dynamic-slice_bitcast_fusion.idx, bf16[768,2048]{1,0:T(8,128)(2,1)S(1)} %get-tuple-element.78.dl, bf16[4096,2048]{1,0:T(8,128)(2,1)} %w.9), custom_call_target="tpu_custom_call" | custom-call | flops 3221225472 | bytes 2097152 | tf_op jit(solution)/shard_map/grad_part/pallas_call | solution.py:342
  103.8 0.2 add_arrived.2
  104.0 2.0 %collective-permute-done.28 = bf16[1536,256]{1,0:T(8,128)(2,1)S(1)} collective-permute-done((bf16[1536,256]{1,0:T(8,128)(2,1)S(1)}, bf16[1536,256]{1,0:T(8,128)(2,1)S(1)}, u32[]{:S(2)}, u32[]{:S(2)}) %collective-permute-start.28) | collective-permute-done | bytes 786464 | tf_op jit(solution)/shard_map/ppermute | solution.py:38
  106.0 0.4 add_convert_fusion
  106.7 3.2 %collective-permute-start.30 = (bf16[768,256]{1,0:T(8,128)(2,1)S(1)}, bf16[768,256]{1,0:T(8,128)(2,1)S(1)}, u32[]{:S(2)}, u32[]{:S(2)}) collective-permute-start(bf16[768,256]{1,0:T(8,128)(2,1)S(1)} %pad_maximum_fusion.5), channel_id=1, source_target_pairs={{0,6},{1,7},{2,0},{3,1},{4,2},{5,3},{6,4},{7,5},{8,14},{9,15},{10,... | collective-permute-start | bytes 1179656 | tf_op jit(solution)/shard_map/ppermute | solution.py:30
  109.9 1.4 collective-permute-start.31
  111.3 8.0 %grad_part.6 = (f32[2304,256]{1,0:T(8,128)S(1)}, bf16[2304,256]{1,0:T(8,128)(2,1)S(1)}) custom-call(s32[16]{0:T(128)S(1)} %dynamic-slice_bitcast_fusion.idx, bf16[768,2048]{1,0:T(8,128)(2,1)S(1)} %get-tuple-element.78.dl, bf16[4096,2048]{1,0:T(8,128)(2,1)} %w.9), custom_call_target="tpu_custom_call" | custom-call | flops 4831838208 | bytes 2097152 | tf_op jit(solution)/shard_map/grad_part/pallas_call | solution.py:342
  119.4 1.1 collective-permute-done.31.refs_3_
  120.5 0.4 add_arrived.3
  120.9 1.3 collective-permute-done.32
  122.2 0.3 fusion
  122.6 3.2 %collective-permute-start.34 = (bf16[768,256]{1,0:T(8,128)(2,1)S(1)}, bf16[768,256]{1,0:T(8,128)(2,1)S(1)}, u32[]{:S(2)}, u32[]{:S(2)}) collective-permute-start(bf16[768,256]{1,0:T(8,128)(2,1)S(1)} %get-tuple-element.81), channel_id=1, source_target_pairs={{0,6},{1,7},{2,0},{3,1},{4,2},{5,3},{6,4},{7,5},{8,14},{9,15},{10,... | collective-permute-start | bytes 1179656 | tf_op jit(solution)/shard_map/ppermute | solution.py:30
  125.9 0.7 collective-permute-start.35
  126.5 4.1 %grad_part.7 = (f32[768,256]{1,0:T(8,128)S(1)}, bf16[768,256]{1,0:T(8,128)(2,1)S(1)}) custom-call(s32[16]{0:T(128)S(1)} %dynamic-slice_bitcast_fusion.idx, bf16[768,2048]{1,0:T(8,128)(2,1)S(1)} %get-tuple-element.78.dl, bf16[4096,2048]{1,0:T(8,128)(2,1)} %w.9), custom_call_target="tpu_custom_call" | custom-call | flops 1610612736 | bytes 2097152 | tf_op jit(solution)/shard_map/grad_part/pallas_call | solution.py:342
  130.7 0.6 slice_reduce_fusion
  131.3 3.7 %collective-permute-done.33 = bf16[768,256]{1,0:T(8,128)(2,1)S(1)} collective-permute-done((bf16[768,256]{1,0:T(8,128)(2,1)S(1)}, bf16[768,256]{1,0:T(8,128)(2,1)S(1)}, u32[]{:S(2)}, u32[]{:S(2)}) %collective-permute-start.33) | collective-permute-done | bytes 393248 | tf_op jit(solution)/shard_map/ppermute | solution.py:30
  135.0 1.5 %collective-permute-done.35 = bf16[768,256]{1,0:T(8,128)(2,1)S(1)} collective-permute-done((bf16[768,256]{1,0:T(8,128)(2,1)S(1)}, bf16[768,256]{1,0:T(8,128)(2,1)S(1)}, u32[]{:S(2)}, u32[]{:S(2)}) %collective-permute-start.35) | collective-permute-done | bytes 393248 | tf_op jit(solution)/shard_map/ppermute | solution.py:34
  136.5 0.2 convert_add_fusion
  136.6 0.8 fusion.3
  137.4 0.7 fusion.4
  (66 shorter events, 1.5 us)
Async XLA Ops:
  0.6 68.1 %copy-start = (s32[16]{0:T(128)S(1)}, s32[16]{0:T(128)}, u32[]{:S(2)}) copy-start(s32[16]{0:T(128)} %param.12) | copy-start | bytes 196
  1.7 5.9 %collective-permute-start.3 = (bf16[768,256]{1,0:T(8,128)(2,1)S(1)}, bf16[768,256]{1,0:T(8,128)(2,1)S(1)}, u32[]{:S(2)}, u32[]{:S(2)}) collective-permute-start(bf16[768,256]{1,0:T(8,128)(2,1)S(1)} %pad_maximum_fusion.2.refs_0_), channel_id=1, source_target_pairs={{0,1},{1,0},{2,3},{3,2},{4,5},{5,4},{6,7},{7,6},{8,9},{9,8},{10,11... | collective-permute-start | bytes 1179656 | tf_op jit(solution)/shard_map/ppermute | solution.py:38
  1.8 12.1 %collective-permute-start = (bf16[768,256]{1,0:T(8,128)(2,1)S(1)}, bf16[768,256]{1,0:T(8,128)(2,1)S(1)}, u32[]{:S(2)}, u32[]{:S(2)}) collective-permute-start(bf16[768,256]{1,0:T(8,128)(2,1)S(1)} %pad_maximum_fusion.2.refs_0_), channel_id=1, source_target_pairs={{0,6},{1,7},{2,0},{3,1},{4,2},{5,3},{6,4},{7,5},{8,14},{9,15},{10,... | collective-permute-start | bytes 1179656 | tf_op jit(solution)/shard_map/ppermute | solution.py:30
  4.9 12.4 %collective-permute-start.1 = (bf16[768,256]{1,0:T(8,128)(2,1)S(1)}, bf16[768,256]{1,0:T(8,128)(2,1)S(1)}, u32[]{:S(2)}, u32[]{:S(2)}) collective-permute-start(bf16[768,256]{1,0:T(8,128)(2,1)S(1)} %pad_maximum_fusion.2.refs_0_), channel_id=1, source_target_pairs={{0,2},{1,3},{2,4},{3,5},{4,6},{5,7},{6,0},{7,1},{8,10},{9,11},{10,... | collective-permute-start | bytes 1179656 | tf_op jit(solution)/shard_map/ppermute | solution.py:30
  4.9 12.4 %collective-permute-start.2 = (bf16[768,256]{1,0:T(8,128)(2,1)S(1)}, bf16[768,256]{1,0:T(8,128)(2,1)S(1)}, u32[]{:S(2)}, u32[]{:S(2)}) collective-permute-start(bf16[768,256]{1,0:T(8,128)(2,1)S(1)} %pad_maximum_fusion.2.refs_0_), channel_id=1, source_target_pairs={{0,8},{1,9},{2,10},{3,11},{4,12},{5,13},{6,14},{7,15},{8,0},{9,1},... | collective-permute-start | bytes 1179656 | tf_op jit(solution)/shard_map/ppermute | solution.py:34
  17.3 2.8 %collective-permute-start.7 = (bf16[768,256]{1,0:T(8,128)(2,1)S(1)}, bf16[768,256]{1,0:T(8,128)(2,1)S(1)}, u32[]{:S(2)}, u32[]{:S(2)}) collective-permute-start(bf16[768,256]{1,0:T(8,128)(2,1)S(1)} %collective-permute-done.refs_0_), channel_id=1, source_target_pairs={{0,1},{1,0},{2,3},{3,2},{4,5},{5,4},{6,7},{7,6},{8,9},{9,8},{10,11... | collective-permute-start | bytes 1179656 | tf_op jit(solution)/shard_map/ppermute | solution.py:38
  17.3 4.7 %collective-permute-start.8 = (bf16[768,256]{1,0:T(8,128)(2,1)S(1)}, bf16[768,256]{1,0:T(8,128)(2,1)S(1)}, u32[]{:S(2)}, u32[]{:S(2)}) collective-permute-start(bf16[768,256]{1,0:T(8,128)(2,1)S(1)} %collective-permute-done.1.refs_2_), channel_id=1, source_target_pairs={{0,1},{1,0},{2,3},{3,2},{4,5},{5,4},{6,7},{7,6},{8,9},{9,8},{10,11... | collective-permute-start | bytes 1179656 | tf_op jit(solution)/shard_map/ppermute | solution.py:38
  17.8 4.2 %collective-permute-start.9 = (bf16[768,256]{1,0:T(8,128)(2,1)S(1)}, bf16[768,256]{1,0:T(8,128)(2,1)S(1)}, u32[]{:S(2)}, u32[]{:S(2)}) collective-permute-start(bf16[768,256]{1,0:T(8,128)(2,1)S(1)} %collective-permute-done.2.refs_4_), channel_id=1, source_target_pairs={{0,1},{1,0},{2,3},{3,2},{4,5},{5,4},{6,7},{7,6},{8,9},{9,8},{10,11... | collective-permute-start | bytes 1179656 | tf_op jit(solution)/shard_map/ppermute | solution.py:38
  18.0 13.9 %collective-permute-start.4 = (bf16[768,256]{1,0:T(8,128)(2,1)S(1)}, bf16[768,256]{1,0:T(8,128)(2,1)S(1)}, u32[]{:S(2)}, u32[]{:S(2)}) collective-permute-start(bf16[768,256]{1,0:T(8,128)(2,1)S(1)} %get-tuple-element.102), channel_id=1, source_target_pairs={{0,6},{1,7},{2,0},{3,1},{4,2},{5,3},{6,4},{7,5},{8,14},{9,15},{10,... | collective-permute-start | bytes 1179656 | tf_op jit(solution)/shard_map/ppermute | solution.py:30
  20.0 12.5 %collective-permute-start.5 = (bf16[768,256]{1,0:T(8,128)(2,1)S(1)}, bf16[768,256]{1,0:T(8,128)(2,1)S(1)}, u32[]{:S(2)}, u32[]{:S(2)}) collective-permute-start(bf16[768,256]{1,0:T(8,128)(2,1)S(1)} %get-tuple-element.103), channel_id=1, source_target_pairs={{0,2},{1,3},{2,4},{3,5},{4,6},{5,7},{6,0},{7,1},{8,10},{9,11},{10,... | collective-permute-start | bytes 1179656 | tf_op jit(solution)/shard_map/ppermute | solution.py:30
  20.1 12.9 %copy-start.2 = (s32[2,256]{1,0:T(2,128)S(1)}, s32[2,256]{1,0:T(2,128)}, u32[]{:S(2)}) copy-start(s32[2,256]{1,0:T(2,128)} %param.11) | copy-start | bytes 6148
  20.1 12.3 %collective-permute-start.6 = (bf16[768,256]{1,0:T(8,128)(2,1)S(1)}, bf16[768,256]{1,0:T(8,128)(2,1)S(1)}, u32[]{:S(2)}, u32[]{:S(2)}) collective-permute-start(bf16[768,256]{1,0:T(8,128)(2,1)S(1)} %get-tuple-element.101), channel_id=1, source_target_pairs={{0,8},{1,9},{2,10},{3,11},{4,12},{5,13},{6,14},{7,15},{8,0},{9,1},... | collective-permute-start | bytes 1179656 | tf_op jit(solution)/shard_map/ppermute | solution.py:34
  32.4 4.3 %collective-permute-start.13 = (bf16[768,256]{1,0:T(8,128)(2,1)S(1)}, bf16[768,256]{1,0:T(8,128)(2,1)S(1)}, u32[]{:S(2)}, u32[]{:S(2)}) collective-permute-start(bf16[768,256]{1,0:T(8,128)(2,1)S(1)} %collective-permute-done.4.refs_0_), channel_id=1, source_target_pairs={{0,1},{1,0},{2,3},{3,2},{4,5},{5,4},{6,7},{7,6},{8,9},{9,8},{10,11... | collective-permute-start | bytes 1179656 | tf_op jit(solution)/shard_map/ppermute | solution.py:38
  32.5 4.6 %collective-permute-start.14 = (bf16[768,256]{1,0:T(8,128)(2,1)S(1)}, bf16[768,256]{1,0:T(8,128)(2,1)S(1)}, u32[]{:S(2)}, u32[]{:S(2)}) collective-permute-start(bf16[768,256]{1,0:T(8,128)(2,1)S(1)} %collective-permute-done.5.refs_2_), channel_id=1, source_target_pairs={{0,1},{1,0},{2,3},{3,2},{4,5},{5,4},{6,7},{7,6},{8,9},{9,8},{10,11... | collective-permute-start | bytes 1179656 | tf_op jit(solution)/shard_map/ppermute | solution.py:38
  33.0 4.1 %collective-permute-start.15 = (bf16[768,256]{1,0:T(8,128)(2,1)S(1)}, bf16[768,256]{1,0:T(8,128)(2,1)S(1)}, u32[]{:S(2)}, u32[]{:S(2)}) collective-permute-start(bf16[768,256]{1,0:T(8,128)(2,1)S(1)} %collective-permute-done.6.refs_4_), channel_id=1, source_target_pairs={{0,1},{1,0},{2,3},{3,2},{4,5},{5,4},{6,7},{7,6},{8,9},{9,8},{10,11... | collective-permute-start | bytes 1179656 | tf_op jit(solution)/shard_map/ppermute | solution.py:38
  33.2 14.7 %copy-start.3 = (s32[2,128]{1,0:T(2,128)S(1)}, s32[2,128]{1,0:T(2,128)}, u32[]{:S(2)}) copy-start(s32[2,128]{1,0:T(2,128)} %param.10) | copy-start | bytes 3076
  33.2 14.0 %collective-permute-start.11 = (bf16[256,256]{1,0:T(8,128)(2,1)S(1)}, bf16[256,256]{1,0:T(8,128)(2,1)S(1)}, u32[]{:S(2)}, u32[]{:S(2)}) collective-permute-start(bf16[256,256]{1,0:T(8,128)(2,1)S(1)} %pad_maximum_fusion.7), channel_id=1, source_target_pairs={{0,8},{1,9},{2,10},{3,11},{4,12},{5,13},{6,14},{7,15},{8,0},{9,1},... | collective-permute-start | bytes 393224 | tf_op jit(solution)/shard_map/ppermute | solution.py:34
  35.0 12.1 %collective-permute-start.10 = (bf16[256,256]{1,0:T(8,128)(2,1)S(1)}, bf16[256,256]{1,0:T(8,128)(2,1)S(1)}, u32[]{:S(2)}, u32[]{:S(2)}) collective-permute-start(bf16[256,256]{1,0:T(8,128)(2,1)S(1)} %slice.102), channel_id=1, source_target_pairs={{0,6},{1,7},{2,0},{3,1},{4,2},{5,3},{6,4},{7,5},{8,14},{9,15},{10,... | collective-permute-start | bytes 393224 | tf_op jit(solution)/shard_map/ppermute | solution.py:30
  36.7 10.4 %collective-permute-start.12 = (bf16[256,256]{1,0:T(8,128)(2,1)S(1)}, bf16[256,256]{1,0:T(8,128)(2,1)S(1)}, u32[]{:S(2)}, u32[]{:S(2)}) collective-permute-start(bf16[256,256]{1,0:T(8,128)(2,1)S(1)} %slice.105), channel_id=1, source_target_pairs={{0,2},{1,3},{2,4},{3,5},{4,6},{5,7},{6,0},{7,1},{8,10},{9,11},{10,... | collective-permute-start | bytes 393224 | tf_op jit(solution)/shard_map/ppermute | solution.py:30
  47.2 1.4 %collective-permute-start.16 = (bf16[256,256]{1,0:T(8,128)(2,1)S(1)}, bf16[256,256]{1,0:T(8,128)(2,1)S(1)}, u32[]{:S(2)}, u32[]{:S(2)}) collective-permute-start(bf16[256,256]{1,0:T(8,128)(2,1)S(1)} %collective-permute-done.10.refs_0_), channel_id=1, source_target_pairs={{0,1},{1,0},{2,3},{3,2},{4,5},{5,4},{6,7},{7,6},{8,9},{9,8},{10,11... | collective-permute-start | bytes 393224 | tf_op jit(solution)/shard_map/ppermute | solution.py:38
  47.2 1.5 %collective-permute-start.17 = (bf16[256,256]{1,0:T(8,128)(2,1)S(1)}, bf16[256,256]{1,0:T(8,128)(2,1)S(1)}, u32[]{:S(2)}, u32[]{:S(2)}) collective-permute-start(bf16[256,256]{1,0:T(8,128)(2,1)S(1)} %collective-permute-done.11.refs_2_), channel_id=1, source_target_pairs={{0,1},{1,0},{2,3},{3,2},{4,5},{5,4},{6,7},{7,6},{8,9},{9,8},{10,11... | collective-permute-start | bytes 393224 | tf_op jit(solution)/shard_map/ppermute | solution.py:38
  47.7 1.3 collective-permute-start.18
  56.2 4.6 %collective-permute-start.19 = (f32[4,2048]{1,0:T(4,128)S(1)}, f32[4,2048]{1,0:T(4,128)S(1)}, u32[]{:S(2)}, u32[]{:S(2)}) collective-permute-start(f32[4,2048]{1,0:T(4,128)S(1)} %get-tuple-element.58), channel_id=1, source_target_pairs={{0,96},{16,112},{32,0},{48,16},{64,32},{80,48},{96,64},{112,80},{1... | collective-permute-start | bytes 98312 | tf_op jit(solution)/shard_map/ppermute | solution.py:42
  59.1 5.4 %collective-permute-start.20 = (f32[4,2048]{1,0:T(4,128)S(1)}, f32[4,2048]{1,0:T(4,128)S(1)}, u32[]{:S(2)}, u32[]{:S(2)}) collective-permute-start(f32[4,2048]{1,0:T(4,128)S(1)} %get-tuple-element.58), channel_id=1, source_target_pairs={{0,64},{16,80},{32,96},{48,112},{64,0},{80,16},{96,32},{112,48},{1... | collective-permute-start | bytes 98312 | tf_op jit(solution)/shard_map/ppermute | solution.py:42
  59.9 5.1 %collective-permute-start.21 = (f32[4,2048]{1,0:T(4,128)S(1)}, f32[4,2048]{1,0:T(4,128)S(1)}, u32[]{:S(2)}, u32[]{:S(2)}) collective-permute-start(f32[4,2048]{1,0:T(4,128)S(1)} %get-tuple-element.58), channel_id=1, source_target_pairs={{0,32},{16,48},{32,64},{48,80},{64,96},{80,112},{96,0},{112,16},{1... | collective-permute-start | bytes 98312 | tf_op jit(solution)/shard_map/ppermute | solution.py:42
  65.0 6.6 %collective-permute-start.22 = (f32[16,2048]{1,0:T(8,128)S(1)}, f32[16,2048]{1,0:T(8,128)S(1)}, u32[]{:S(2)}, u32[]{:S(2)}) collective-permute-start(f32[16,2048]{1,0:T(8,128)S(1)} %pad_maximum_fusion.8.a.pa), channel_id=1, source_target_pairs={{0,16},{16,0},{32,48},{48,32},{64,80},{80,64},{96,112},{112,96},{1... | collective-permute-start | bytes 393224 | tf_op jit(solution)/shard_map/ppermute | solution.py:46
  72.6 11.0 %all-to-all-start = ((f32[16,8,128]{2,1,0:T(8,128)}), f32[16,8,128]{2,1,0:T(8,128)S(1)}, u32[]{:S(2)}, u32[]{:S(2)}) async-start(f32[16,8,128]{2,1,0:T(8,128)} %gram.1), calls=%async_computation | async-start | bytes 131072 | tf_op jit(solution)/shard_map/all_to_all | solution.py:428
  88.7 4.7 %collective-permute-start.23 = (bf16[768,256]{1,0:T(8,128)(2,1)S(1)}, bf16[768,256]{1,0:T(8,128)(2,1)S(1)}, u32[]{:S(2)}, u32[]{:S(2)}) collective-permute-start(bf16[768,256]{1,0:T(8,128)(2,1)S(1)} %get-tuple-element.64), channel_id=1, source_target_pairs={{0,1},{1,0},{2,3},{3,2},{4,5},{5,4},{6,7},{7,6},{8,9},{9,8},{10,11... | collective-permute-start | bytes 1179656 | tf_op jit(solution)/shard_map/ppermute | solution.py:38
  93.0 11.0 %collective-permute-start.27 = (bf16[768,256]{1,0:T(8,128)(2,1)S(1)}, bf16[768,256]{1,0:T(8,128)(2,1)S(1)}, u32[]{:S(2)}, u32[]{:S(2)}) collective-permute-start(bf16[768,256]{1,0:T(8,128)(2,1)S(1)} %get-tuple-element.69), channel_id=1, source_target_pairs={{0,1},{1,0},{2,3},{3,2},{4,5},{5,4},{6,7},{7,6},{8,9},{9,8},{10,11... | collective-permute-start | bytes 1179656 | tf_op jit(solution)/shard_map/ppermute | solution.py:38
  93.6 10.1 %collective-permute-start.24 = (bf16[256,256]{1,0:T(8,128)(2,1)S(1)}, bf16[256,256]{1,0:T(8,128)(2,1)S(1)}, u32[]{:S(2)}, u32[]{:S(2)}) collective-permute-start(bf16[256,256]{1,0:T(8,128)(2,1)S(1)} %get-tuple-element.98), channel_id=1, source_target_pairs={{0,2},{1,3},{2,4},{3,5},{4,6},{5,7},{6,0},{7,1},{8,10},{9,11},{10,... | collective-permute-start | bytes 393224 | tf_op jit(solution)/shard_map/ppermute | solution.py:30
  94.3 9.5 %collective-permute-start.25 = (bf16[256,256]{1,0:T(8,128)(2,1)S(1)}, bf16[256,256]{1,0:T(8,128)(2,1)S(1)}, u32[]{:S(2)}, u32[]{:S(2)}) collective-permute-start(bf16[256,256]{1,0:T(8,128)(2,1)S(1)} %get-tuple-element.97), channel_id=1, source_target_pairs={{0,8},{1,9},{2,10},{3,11},{4,12},{5,13},{6,14},{7,15},{8,0},{9,1},... | collective-permute-start | bytes 393224 | tf_op jit(solution)/shard_map/ppermute | solution.py:34
  94.9 8.8 %collective-permute-start.26 = (bf16[256,256]{1,0:T(8,128)(2,1)S(1)}, bf16[256,256]{1,0:T(8,128)(2,1)S(1)}, u32[]{:S(2)}, u32[]{:S(2)}) collective-permute-start(bf16[256,256]{1,0:T(8,128)(2,1)S(1)} %get-tuple-element.96), channel_id=1, source_target_pairs={{0,6},{1,7},{2,0},{3,1},{4,2},{5,3},{6,4},{7,5},{8,14},{9,15},{10,... | collective-permute-start | bytes 393224 | tf_op jit(solution)/shard_map/ppermute | solution.py:30
  103.6 2.4 %collective-permute-start.28 = (bf16[1536,256]{1,0:T(8,128)(2,1)S(1)}, bf16[1536,256]{1,0:T(8,128)(2,1)S(1)}, u32[]{:S(2)}, u32[]{:S(2)}) collective-permute-start(bf16[1536,256]{1,0:T(8,128)(2,1)S(1)} %get-tuple-element.71), channel_id=1, source_target_pairs={{0,1},{1,0},{2,3},{3,2},{4,5},{5,4},{6,7},{7,6},{8,9},{9,8},{10,11... | collective-permute-start | bytes 2359304 | tf_op jit(solution)/shard_map/ppermute | solution.py:38
  106.6 12.8 %collective-permute-start.29 = (bf16[768,256]{1,0:T(8,128)(2,1)S(1)}, bf16[768,256]{1,0:T(8,128)(2,1)S(1)}, u32[]{:S(2)}, u32[]{:S(2)}) collective-permute-start(bf16[768,256]{1,0:T(8,128)(2,1)S(1)} %pad_maximum_fusion.4), channel_id=1, source_target_pairs={{0,2},{1,3},{2,4},{3,5},{4,6},{5,7},{6,0},{7,1},{8,10},{9,11},{10,... | collective-permute-start | bytes 1179656 | tf_op jit(solution)/shard_map/ppermute | solution.py:30
  106.7 12.7 %collective-permute-start.30 = (bf16[768,256]{1,0:T(8,128)(2,1)S(1)}, bf16[768,256]{1,0:T(8,128)(2,1)S(1)}, u32[]{:S(2)}, u32[]{:S(2)}) collective-permute-start(bf16[768,256]{1,0:T(8,128)(2,1)S(1)} %pad_maximum_fusion.5), channel_id=1, source_target_pairs={{0,6},{1,7},{2,0},{3,1},{4,2},{5,3},{6,4},{7,5},{8,14},{9,15},{10,... | collective-permute-start | bytes 1179656 | tf_op jit(solution)/shard_map/ppermute | solution.py:30
  109.9 10.6 %collective-permute-start.31 = (bf16[768,256]{1,0:T(8,128)(2,1)S(1)}, bf16[768,256]{1,0:T(8,128)(2,1)S(1)}, u32[]{:S(2)}, u32[]{:S(2)}) collective-permute-start(bf16[768,256]{1,0:T(8,128)(2,1)S(1)} %pad_maximum_fusion.6), channel_id=1, source_target_pairs={{0,8},{1,9},{2,10},{3,11},{4,12},{5,13},{6,14},{7,15},{8,0},{9,1},... | collective-permute-start | bytes 1179656 | tf_op jit(solution)/shard_map/ppermute | solution.py:34
  119.3 2.9 %collective-permute-start.32 = (bf16[2304,256]{1,0:T(8,128)(2,1)S(1)}, bf16[2304,256]{1,0:T(8,128)(2,1)S(1)}, u32[]{:S(2)}, u32[]{:S(2)}) collective-permute-start(bf16[2304,256]{1,0:T(8,128)(2,1)S(1)} %get-tuple-element.77), channel_id=1, source_target_pairs={{0,1},{1,0},{2,3},{3,2},{4,5},{5,4},{6,7},{7,6},{8,9},{9,8},{10,11... | collective-permute-start | bytes 3538952 | tf_op jit(solution)/shard_map/ppermute | solution.py:38
  122.6 12.4 %collective-permute-start.33 = (bf16[768,256]{1,0:T(8,128)(2,1)S(1)}, bf16[768,256]{1,0:T(8,128)(2,1)S(1)}, u32[]{:S(2)}, u32[]{:S(2)}) collective-permute-start(bf16[768,256]{1,0:T(8,128)(2,1)S(1)} %get-tuple-element.80), channel_id=1, source_target_pairs={{0,2},{1,3},{2,4},{3,5},{4,6},{5,7},{6,0},{7,1},{8,10},{9,11},{10,... | collective-permute-start | bytes 1179656 | tf_op jit(solution)/shard_map/ppermute | solution.py:30
  122.6 12.4 %collective-permute-start.34 = (bf16[768,256]{1,0:T(8,128)(2,1)S(1)}, bf16[768,256]{1,0:T(8,128)(2,1)S(1)}, u32[]{:S(2)}, u32[]{:S(2)}) collective-permute-start(bf16[768,256]{1,0:T(8,128)(2,1)S(1)} %get-tuple-element.81), channel_id=1, source_target_pairs={{0,6},{1,7},{2,0},{3,1},{4,2},{5,3},{6,4},{7,5},{8,14},{9,15},{10,... | collective-permute-start | bytes 1179656 | tf_op jit(solution)/shard_map/ppermute | solution.py:30
  125.9 10.6 %collective-permute-start.35 = (bf16[768,256]{1,0:T(8,128)(2,1)S(1)}, bf16[768,256]{1,0:T(8,128)(2,1)S(1)}, u32[]{:S(2)}, u32[]{:S(2)}) collective-permute-start(bf16[768,256]{1,0:T(8,128)(2,1)S(1)} %get-tuple-element.82), channel_id=1, source_target_pairs={{0,8},{1,9},{2,10},{3,11},{4,12},{5,13},{6,14},{7,15},{8,0},{9,1},... | collective-permute-start | bytes 1179656 | tf_op jit(solution)/shard_map/ppermute | solution.py:34
  126.5 11.6 %copy-start.1 = (s32[16]{0:T(128)S(1)}, s32[16]{0:T(128)}, u32[]{:S(2)}) copy-start(s32[16]{0:T(128)} %param.12) | copy-start | bytes 196
  130.6 6.0 %collective-permute-start.36 = (bf16[768,256]{1,0:T(8,128)(2,1)S(1)}, bf16[768,256]{1,0:T(8,128)(2,1)S(1)}, u32[]{:S(2)}, u32[]{:S(2)}) collective-permute-start(bf16[768,256]{1,0:T(8,128)(2,1)S(1)} %get-tuple-element.83), channel_id=1, source_target_pairs={{0,1},{1,0},{2,3},{3,2},{4,5},{5,4},{6,7},{7,6},{8,9},{9,8},{10,11... | collective-permute-start | bytes 1179656 | tf_op jit(solution)/shard_map/ppermute | solution.py:38

commit v3 on v2

--- a/solution.py
+++ b/solution.py
@@ -51,9 +51,12 @@
 
 def place_table():
     rows = []
-    for v in range(16):
-        z, y, core = v // 8, (v // 2) % 4, v % 2
-        rows.append([((z + dz) % 2) * 4 + (y + dy) % 4 for dy, dz in PLACES] + [core] * 8)
+    for g in range(8):
+        gx, gz = g // 2, g % 2
+        seqs = [(((gx + i % 4) % 4) * 2 + (gz + i // 4) % 2) * 2 + k for i in range(8) for k in range(2)]
+        for v in range(16):
+            z, y, core = v // 8, (v // 2) % 4, v % 2
+            rows.append([((z + dz) % 2) * 4 + (y + dy) % 4 for dy, dz in PLACES] + [core] * 8 + seqs)
     return np.array(rows, np.int32)
 
 
@@ -89,19 +92,24 @@
         for i in range(len(copies)):
             x_copy(i).start()
 
+    @pl.when(j == 0)
+    def _():
+        for i in range(len(copies)):
+            x_copy(i).wait()
+
+    for k in range(nk):
+        w_copy(j, slot, k).wait()
+
     @pl.when(j + 1 < steps)
     def _():
         for k in range(nk):
             w_copy(j + 1, 1 - slot, k).start()
 
-    @pl.when(j == 0)
-    def _():
-        for i in range(len(copies)):
-            x_copy(i).wait()
-
-    for k in range(nk):
-        w_copy(j, slot, k).wait()
     return slot
+
+
+def columns_of(bn):
+    return pl.ds(pl.multiple_of(pl.program_id(0) * bn, bn), bn)
 
 
 def logits_kernel(copies, places, nx, bn, steps, has_acc, idx, *refs):
@@ -115,27 +123,28 @@
     out, xs, ws, xsem, wsem = refs[pos:]
     slot = load_operands(copies, places, bn, steps, idx, xrefs, w, xs, ws, xsem, wsem)
     res = jnp.dot(xs[...], ws[slot], preferred_element_type=F32)
+    cols = columns_of(bn)
     if has_acc:
-        res = res + acc[...]
-    out[...] = res
-
-
-def logits_part(arrays, copies, places, idx, w, acc, out_space=None):
+        res = res + acc[:, cols]
+    out[:, cols] = res
+
+
+def logits_part(arrays, copies, places, idx, w, acc):
     rows = 768
     cols = w.shape[1]
     nk = 2 * len(places)
     bn = 512
     steps = cols // bn
     any_spec = pl.BlockSpec(memory_space=pl.ANY)
-    blk = pl.BlockSpec((rows, bn), lambda j, *_: (0, j))
+    vm = pl.BlockSpec(memory_space=pltpu.VMEM)
     ins = list(arrays) + [w] + ([acc] if acc is not None else [])
     return pl.pallas_call(
         functools.partial(logits_kernel, copies, places, len(arrays), bn, steps, acc is not None),
         grid_spec=pltpu.PrefetchScalarGridSpec(
             num_scalar_prefetch=1,
             grid=(steps,),
-            in_specs=[any_spec] * len(arrays) + [HBM_SPEC] + ([blk] if acc is not None else []),
-            out_specs=blk,
+            in_specs=[any_spec] * len(arrays) + [HBM_SPEC] + ([vm] if acc is not None else []),
+            out_specs=vm,
             scratch_shapes=[
                 pltpu.VMEM((rows, nk * BLK), BF),
                 pltpu.VMEM((2, nk * BLK, bn), BF),
@@ -143,10 +152,10 @@
                 pltpu.SemaphoreType.DMA((2, nk)),
             ],
         ),
-        out_shape=jax.ShapeDtypeStruct((rows, cols), F32) if out_space is None else out_space((rows, cols), F32),
-        compiler_params=pltpu.CompilerParams(vmem_limit_bytes=18 * MIB),
+        out_shape=jax.ShapeDtypeStruct((rows, cols), F32),
+        input_output_aliases={len(arrays) + 2: 0} if acc is not None else {},
+        compiler_params=pltpu.CompilerParams(vmem_limit_bytes=(14 if nk > 2 else 12) * MIB),
         name="logits_part",
-        cost_estimate=matmul_cost(rows, nk * BLK, cols),
     )(idx, *ins)
 
 
@@ -154,7 +163,7 @@
     xrefs = refs[:nx]
     w, acc, expo, stats, pooled, xs, ws, xsem, wsem = refs[nx:]
     slot = load_operands(copies, places, bn, steps, idx, xrefs, w, xs, ws, xsem, wsem)
-    logits = jnp.dot(xs[...], ws[slot], preferred_element_type=F32) + acc[...]
+    logits = jnp.dot(xs[...], ws[slot], preferred_element_type=F32) + acc[:, columns_of(bn)]
     smooth, sums = [], []
     for s, (start, n) in enumerate(seqs):
         part = logits[start : start + n] * (1.0 / SHARP)
@@ -184,7 +193,7 @@
         grid_spec=pltpu.PrefetchScalarGridSpec(
             num_scalar_prefetch=2,
             grid=(steps,),
-            in_specs=[any_spec] * len(arrays) + [HBM_SPEC, blk],
+            in_specs=[any_spec] * len(arrays) + [HBM_SPEC, pl.BlockSpec(memory_space=pltpu.VMEM)],
             out_specs=[
                 blk,
                 pl.BlockSpec((8, bn), lambda j, *_: (0, j)),
@@ -202,9 +211,8 @@
             jax.ShapeDtypeStruct((8, cols), F32),
             jax.ShapeDtypeStruct((4, cols), F32),
         ],
-        compiler_params=pltpu.CompilerParams(vmem_limit_bytes=20 * MIB),
+        compiler_params=pltpu.CompilerParams(vmem_limit_bytes=16 * MIB),
         name="logits_pool",
-        cost_estimate=matmul_cost(rows, nk * BLK, cols),
     )(idx, lens, *arrays, w, acc)
 
 
@@ -309,9 +317,8 @@
             jax.ShapeDtypeStruct((rows, BLK), F32),
             jax.ShapeDtypeStruct((rows, BLK), BF),
         ],
-        compiler_params=pltpu.CompilerParams(vmem_limit_bytes=22 * MIB),
+        compiler_params=pltpu.CompilerParams(vmem_limit_bytes=18 * MIB),
         name="first_grad",
-        cost_estimate=matmul_cost(rows, 2 * BLK, cols),
     )(idx, parts, pa, pb, stats, picked, pltpu.with_memory_space_constraint(expo, pltpu.HBM), w)
 
 
@@ -344,14 +351,13 @@
         grid_spec=pltpu.PrefetchScalarGridSpec(
             num_scalar_prefetch=1,
             grid=(n,),
-            in_specs=[pl.BlockSpec((rows, cols), lambda i, idx: (0, 0)), HBM_SPEC],
+            in_specs=[pl.BlockSpec(memory_space=pltpu.VMEM), HBM_SPEC],
             out_specs=[out, out],
             scratch_shapes=[pltpu.VMEM((2, 2 * BLK, cols), BF), pltpu.SemaphoreType.DMA((2,))],
         ),
         out_shape=[jax.ShapeDtypeStruct((n * rows, BLK), F32), jax.ShapeDtypeStruct((n * rows, BLK), BF)],
-        compiler_params=pltpu.CompilerParams(vmem_limit_bytes=18 * MIB),
+        compiler_params=pltpu.CompilerParams(vmem_limit_bytes=12 * MIB),
         name="grad_part",
-        cost_estimate=matmul_cost(n * rows, 2 * BLK, cols),
     )(idx, dl, w)
 
 
@@ -371,6 +377,26 @@
         name="add_arrived",
         cost_estimate=matmul_cost(4096, 2048, 2048),
     )(*mine, *arrived)
+
+
+def add_last_kernel(split, *refs):
+    parts, (out_q, out_p) = refs[:-2], refs[-2:]
+    res = parts[0][...]
+    for p in parts[1:]:
+        res = res + p[...].astype(F32)
+    res = res.astype(BF)
+    out_q[...] = res[:split]
+    out_p[...] = res[split:]
+
+
+def add_last(mine, others, split):
+    rows, cols = mine.shape
+    return pl.pallas_call(
+        functools.partial(add_last_kernel, split),
+        out_shape=[jax.ShapeDtypeStruct((split, cols), BF), jax.ShapeDtypeStruct((rows - split, cols), BF)],
+        compiler_params=pltpu.CompilerParams(vmem_limit_bytes=12 * MIB),
+        name="add_last",
+    )(mine, *others)
 
 
 def after(x, *others):
@@ -386,7 +412,8 @@
         (split + i * p_len, p_len) for i in range(p_count)
     )
     own = jnp.concatenate([query_hidden.reshape(split, width), passage_hidden.reshape(p_count * p_len, width)], axis=0)
-    idx = lax.dynamic_index_in_dim(jnp.asarray(place_table()), lax.axis_index("vocab"), 0, keepdims=False)
+    me = lax.axis_index(("dp", "vocab"))
+    idx = lax.dynamic_index_in_dim(jnp.asarray(place_table()), me, 0, keepdims=False)
     at = {p: i for i, p in enumerate(PLACES)}
     h = 384
 
@@ -399,11 +426,10 @@
     f3 = to_z(jnp.concatenate([x10[:h], xm0[:h]], axis=0))
     near = [t for p in (x10, xm0, x01) for t in (p, to_core(p))]
     whole = tuple((i, i, 0, 0, 768) for i in range(6))
-    acc = logits_part(near, whole, (1, 2, 3), idx, w, acc, pltpu.HBM)
+    acc = logits_part(near, whole, (1, 2, 3), idx, w, acc)
     f1, f2, f3, acc = lax.optimization_barrier((f1, f2, f3, acc))
-    g1 = to_y(f3[:256], -1)
-    g2 = to_z(jnp.concatenate([f1[256:384], f2[384:512]], axis=0))
-    g3 = to_y(f2[128:384], 1)
+    g1 = to_y(f3[:h], -1)
+    g2 = to_z(f2[h:])
     mid = [t for p in (f1, f2, f3) for t in (p, to_core(p))]
     mid_copies = []
     for c in range(2):
@@ -415,10 +441,10 @@
             (4 + c, 4 + c, h, 0, h),
             (2 + c, 4 + c, 0, h, h),
         ]
-    acc = logits_part(mid, tuple(mid_copies), (4, 5, 6), idx, w, pltpu.with_memory_space_constraint(acc, pltpu.HBM))
-    g1, g2, g3, acc = lax.optimization_barrier((g1, g2, g3, acc))
-    last = [t for p in (g1, g2, g3) for t in (p, to_core(p))]
-    last_copies = tuple((2 * i + c, c, 0, 256 * i, 256) for i in range(3) for c in range(2))
+    acc = logits_part(mid, tuple(mid_copies), (4, 5, 6), idx, w, acc)
+    g1, g2, acc = lax.optimization_barrier((g1, g2, acc))
+    last = [t for p in (g1, g2) for t in (p, to_core(p))]
+    last_copies = tuple((2 * i + c, c, 0, h * i, h) for i in range(2) for c in range(2))
     query_mask, passage_mask, positive = lax.optimization_barrier((query_mask, passage_mask, positive, x10))[:3]
     lens = jnp.concatenate([jnp.sum(query_mask > 0, axis=1), jnp.sum(passage_mask > 0, axis=1)]).astype(jnp.int32)
     expo, stats, pooled = logits_pool(last, last_copies, (7,), idx, lens, w, acc, seqs)
@@ -427,28 +453,20 @@
     pb = to_zhi(pa)
     parts = lax.all_to_all(gram(pa, pb, 16), "vocab", 0, 0)
 
-    group = lax.axis_index("dp")
-    slot = jnp.arange(16, dtype=jnp.int32)
-    place = slot // 2
-    gx = (group // 2 + place % 4) % 4
-    gz = (group % 2 + place // 4) % 2
-    seq = (gx * 2 + gz) * 2 + slot % 2
+    seq = idx[16:]
     target = positive[seq]
     picked = (target[:, None] == seq[None, :]).astype(F32)
 
     dl, loss, m21, s21 = first_grad(7, idx, parts, pa, pb, stats, picked, expo, w, seqs, positive.shape[0])
-    m20, s20 = grad_part(4, 1, idx, dl, w)
     t21 = (m21 + to_core(s21)).astype(BF)
     def rows(x, i):
         return x[768 * i : 768 * (i + 1)]
 
-    r1, r2, r3 = to_y(t21[:256], 1), to_z(t21[256:512]), to_y(t21[512:], -1)
-    mb, sb = grad_part(5, 2, idx, after(dl, t21), w)
+    r1, r2 = to_y(t21[:h], 1), to_z(t21[h:])
+    mb, sb = grad_part(4, 3, idx, after(dl, t21), w)
     sb = to_core(sb)
-    mb, m20 = add_arrived((mb, m20), (r1, r2, r3), ((0, 0, 0, 0, 256), (0, 2, 0, 768 + 512, 256), (1, 1, 0, 256, 256)))
-    t20 = (m20 + to_core(s20)).astype(BF)
-    t11 = (rows(mb, 0) + rows(sb, 0)).astype(BF)
-    tm1 = (rows(mb, 1) + rows(sb, 1)).astype(BF)
+    (mb,) = add_arrived((mb,), (r1, r2), ((0, 0, 0, 768, h), (0, 1, 0, h, h)))
+    t20, t11, tm1 = ((rows(mb, i) + rows(sb, i)).astype(BF) for i in range(3))
     c1 = jnp.concatenate([t20[:h], t11[h:]], axis=0)
     c2 = jnp.concatenate([tm1[h:], t20[h:]], axis=0)
     c3 = jnp.concatenate([t11[:h], tm1[:h]], axis=0)
@@ -472,15 +490,11 @@
     t10, tm0, t01, dl = lax.optimization_barrier((t10, tm0, t01, dl))
     v1, v2, v3 = to_y(t10, 1), to_y(tm0, -1), to_z(t01)
     md, sd = grad_part(0, 1, idx, dl, w)
-    k00 = lax.optimization_barrier(md + v1.astype(F32) + v2.astype(F32) + v3.astype(F32))
-    sd = to_core(sd)
-
-    def total(a, b):
-        return (k00[a:b] + sd[a:b].astype(F32)).astype(BF)
-
+    (md,) = add_arrived((md,), (v1, v2, v3), tuple((0, i, 0, 0, 768) for i in range(3)))
+    out_q, out_p = add_last(md, (to_core(sd),), split)
     return (
-        total(0, split).reshape(q_count, q_len, width),
-        total(split, 768).reshape(p_count, p_len, width),
+        out_q.reshape(q_count, q_len, width),
+        out_p.reshape(p_count, p_len, width),
         loss[:q_count, 0],
     )
 

time: 139 us -> 131 us (0.942)
  starting transfers between devices: 41.3 us -> 36.7 us
  Pallas kernels: 60.7 us -> 56.3 us
  waiting for transfers between devices: 28.8 us -> 31.8 us
  other arithmetic: 4.09 us -> 2.6 us
    pallas_call x3, Pallas kernels: 24.7 us -> 21.7 us  [logits_part(): pl.pallas_call(functools.partial(logits_kernel, copies, places, len(array...]
    ppermute x12 -> x10, starting transfers between devices: 17.2 us -> 14.3 us  [to_y(): return lax.ppermute(x, 'vocab', y_perm(k % 4))]
    ppermute x15 -> x13, waiting for transfers between devices: 4.4 us -> 6.58 us  [to_core(): return lax.ppermute(x, 'vocab', CORE_SWAP)]
    pallas_call x4 -> x3, Pallas kernels: 22.2 us -> 20 us  [grad_part(): pl.pallas_call(functools.partial(grad_kernel, first, n), grid_spec=pltpu....]
    convert_element_type x3 -> x1, other arithmetic: 1.81 us -> 0.4 us  [on_device(): t20, t11, tm1 = ((rows(mb, i) + rows(sb, i)).astype(BF) for i in range(3))]
    ppermute x12 -> x10, waiting for transfers between devices: 9.28 us -> 10.4 us  [to_y(): return lax.ppermute(x, 'vocab', y_perm(k % 4))]
  transfers between devices with their start and end apart: 38 -> 34, of which waited for: 16 -> 15; matrix products, arithmetic and copies ran while one was open for 2% -> 2% of each run, Pallas kernels for 34% -> 33%
where the time goes in v3:
time: 131 us
  Pallas kernels  56.3 us (43%)
  starting transfers between devices  36.7 us (28%)
  waiting for transfers between devices  31.8 us (24%)
  other arithmetic  2.6 us (2%)
  local copies, waits for them, and re-layouts  2.25 us (2%)
    pallas_call x3, Pallas kernels, logits_part(): pl.pallas_call(functools.partial(logits_kernel, copies, places, len(array...  21.7 us
    pallas_call x3, Pallas kernels, grad_part(): pl.pallas_call(functools.partial(grad_kernel, first, n), grid_spec=pltpu....  20 us
    ppermute x10, starting transfers between devices, to_y(): return lax.ppermute(x, 'vocab', y_perm(k % 4))  14.3 us
    ppermute x10, waiting for transfers between devices, to_y(): return lax.ppermute(x, 'vocab', y_perm(k % 4))  10.4 us
    ppermute x6, starting transfers between devices, to_z(): return lax.ppermute(x, 'vocab', Z_SWAP)  8.25 us
    pallas_call x1, Pallas kernels, logits_pool(): pl.pallas_call(functools.partial(pool_kernel, copies, places, len(arrays)...  6.85 us
    ppermute x13, waiting for transfers between devices, to_core(): return lax.ppermute(x, 'vocab', CORE_SWAP)  6.58 us
    all_to_all x1, waiting for transfers between devices, on_device(): parts = lax.all_to_all(gram(pa, pb, 16), 'vocab', 0, 0)  5.82 us
  transfers between devices with their start and end apart: 34, of which 15 were waited for; matrix products, arithmetic and copies ran while one was open for 2% of the time, Pallas kernels for 33%

profile of v3, /device:TPU:0, one launch (start us, length us, event | category | flops | bytes accessed | tf_op | source)
XLA Modules:
  0.0 130.7 jit_solution(1235616601805868248)
XLA Ops:
  0.6 1.0 pad_maximum_fusion.2.refs_0_
  1.7 0.1 collective-permute-start.3
  1.8 3.2 %collective-permute-start = (bf16[768,256]{1,0:T(8,128)(2,1)S(1)}, bf16[768,256]{1,0:T(8,128)(2,1)S(1)}, u32[]{:S(2)}, u32[]{:S(2)}) collective-permute-start(bf16[768,256]{1,0:T(8,128)(2,1)S(1)} %pad_maximum_fusion.2.refs_0_), channel_id=1, source_target_pairs={{0,6},{1,7},{2,0},{3,1},{4,2},{5,3},{6,4},{7,5},{8,14},{9,15},{10,... | collective-permute-start | bytes 1179656 | tf_op jit(solution)/shard_map/ppermute | solution.py:30
  4.9 1.9 %collective-permute-start.2 = (bf16[768,256]{1,0:T(8,128)(2,1)S(1)}, bf16[768,256]{1,0:T(8,128)(2,1)S(1)}, u32[]{:S(2)}, u32[]{:S(2)}) collective-permute-start(bf16[768,256]{1,0:T(8,128)(2,1)S(1)} %pad_maximum_fusion.2.refs_0_), channel_id=1, source_target_pairs={{0,8},{1,9},{2,10},{3,11},{4,12},{5,13},{6,14},{7,15},{8,0},{9,1},... | collective-permute-start | bytes 1179656 | tf_op jit(solution)/shard_map/ppermute | solution.py:34
  6.8 0.7 constant_dynamic-slice_fusion
  7.5 5.3 %logits_part.3.refs_7_ = f32[768,2048]{1,0:T(8,128)S(1)} custom-call(s32[32]{0:T(128)S(1)} %get-tuple-element.99.idx, bf16[768,256]{1,0:T(8,128)(2,1)S(1)} %pad_maximum_fusion.2.refs_0_, bf16[768,256]{1,0:T(8,128)(2,1)S(1)} %collective-permute-done.3.refs_1_, bf16[4096,2048]{1,0:T(8,128)(2,1)} %w.7), custom_call_target="tpu_custom_call" | custom-call | tf_op jit(solution)/shard_map/logits_part/pallas_call | solution.py:141
  12.8 1.1 collective-permute-done.refs_0_
  13.9 3.4 %collective-permute-done.1.refs_2_ = bf16[768,256]{1,0:T(8,128)(2,1)S(1)} collective-permute-done((bf16[768,256]{1,0:T(8,128)(2,1)S(1)}, bf16[768,256]{1,0:T(8,128)(2,1)S(1)}, u32[]{:S(2)}, u32[]{:S(2)}) %collective-permute-start.1) | collective-permute-done | bytes 393248 | tf_op jit(solution)/shard_map/ppermute | solution.py:30
  17.3 0.6 collective-permute-start.9
  17.9 0.1 collective-permute-start.8
  18.2 2.0 %collective-permute-start.4 = (bf16[768,256]{1,0:T(8,128)(2,1)S(1)}, bf16[768,256]{1,0:T(8,128)(2,1)S(1)}, u32[]{:S(2)}, u32[]{:S(2)}) collective-permute-start(bf16[768,256]{1,0:T(8,128)(2,1)S(1)} %get-tuple-element.96), channel_id=1, source_target_pairs={{0,6},{1,7},{2,0},{3,1},{4,2},{5,3},{6,4},{7,5},{8,14},{9,15},{10,... | collective-permute-start | bytes 1179656 | tf_op jit(solution)/shard_map/ppermute | solution.py:30
  20.1 0.1 collective-permute-start.5
  20.3 1.9 %collective-permute-start.6 = (bf16[768,256]{1,0:T(8,128)(2,1)S(1)}, bf16[768,256]{1,0:T(8,128)(2,1)S(1)}, u32[]{:S(2)}, u32[]{:S(2)}) collective-permute-start(bf16[768,256]{1,0:T(8,128)(2,1)S(1)} %get-tuple-element.95), channel_id=1, source_target_pairs={{0,8},{1,9},{2,10},{3,11},{4,12},{5,13},{6,14},{7,15},{8,0},{9,1},... | collective-permute-start | bytes 1179656 | tf_op jit(solution)/shard_map/ppermute | solution.py:34
  22.2 8.2 %logits_part.4.refs_7_ = f32[768,2048]{1,0:T(8,128)S(1)} custom-call(s32[32]{0:T(128)S(1)} %get-tuple-element.99.idx, bf16[768,256]{1,0:T(8,128)(2,1)S(1)} %collective-permute-done.refs_0_, bf16[768,256]{1,0:T(8,128)(2,1)S(1)} %collective-permute-done.7.refs_1_, bf16[768,256]{1,0:T(8,128)(2,1)S(1)} %collective-permute-done.1.refs_2_, ...), custom_call_target="tpu_custom_call", output_to_operand_aliasing={{}: (8, {})} | custom-call | tf_op jit(solution)/shard_map/logits_part/pallas_call | solution.py:141
  30.4 2.2 %collective-permute-done.5.refs_2_ = bf16[768,256]{1,0:T(8,128)(2,1)S(1)} collective-permute-done((bf16[768,256]{1,0:T(8,128)(2,1)S(1)}, bf16[768,256]{1,0:T(8,128)(2,1)S(1)}, u32[]{:S(2)}, u32[]{:S(2)}) %collective-permute-start.5) | collective-permute-done | bytes 393248 | tf_op jit(solution)/shard_map/ppermute | solution.py:30
  32.6 0.5 collective-permute-start.13
  33.1 1.8 %collective-permute-start.10 = (bf16[384,256]{1,0:T(8,128)(2,1)S(1)}, bf16[384,256]{1,0:T(8,128)(2,1)S(1)}, u32[]{:S(2)}, u32[]{:S(2)}) collective-permute-start(bf16[384,256]{1,0:T(8,128)(2,1)S(1)} %slice.93), channel_id=1, source_target_pairs={{0,6},{1,7},{2,0},{3,1},{4,2},{5,3},{6,4},{7,5},{8,14},{9,15},{10,... | collective-permute-start | bytes 589832 | tf_op jit(solution)/shard_map/ppermute | solution.py:30
  35.0 1.7 %collective-permute-start.11 = (bf16[384,256]{1,0:T(8,128)(2,1)S(1)}, bf16[384,256]{1,0:T(8,128)(2,1)S(1)}, u32[]{:S(2)}, u32[]{:S(2)}) collective-permute-start(bf16[384,256]{1,0:T(8,128)(2,1)S(1)} %slice.94), channel_id=1, source_target_pairs={{0,8},{1,9},{2,10},{3,11},{4,12},{5,13},{6,14},{7,15},{8,0},{9,1},... | collective-permute-start | bytes 589832 | tf_op jit(solution)/shard_map/ppermute | solution.py:34
  36.7 0.1 fusion.6
  36.9 8.2 %logits_part.5.refs_5_ = f32[768,2048]{1,0:T(8,128)S(1)} custom-call(s32[32]{0:T(128)S(1)} %get-tuple-element.99.idx, bf16[768,256]{1,0:T(8,128)(2,1)S(1)} %collective-permute-done.4.refs_0_, bf16[768,256]{1,0:T(8,128)(2,1)S(1)} %collective-permute-done.12.refs_1_, ...), custom_call_target="tpu_custom_call", output_to_operand_aliasing={{}: (8, {})} | custom-call | tf_op jit(solution)/shard_map/logits_part/pallas_call | solution.py:141
  45.1 0.1 collective-permute-start.15
  45.2 0.5 collective-permute-start.16
  45.7 0.1 fusion.7
  45.9 0.7 collective-permute-done.15.refs_1_
  46.6 0.3 collective-permute-done.16.refs_3_
  46.9 6.9 %logits_pool.1 = (bf16[768,2048]{1,0:T(8,128)(2,1)}, f32[8,2048]{1,0:T(8,128)S(1)}, f32[4,2048]{1,0:T(4,128)S(1)}) custom-call(s32[32]{0:T(128)S(1)} %get-tuple-element.99.idx, s32[4]{0:T(128)S(1)} %pad_add_fusion.lens, bf16[384,256]{1,0:T(8,128)(2,1)S(1)} %collective-permute-done.10.refs_0_, bf16[384,256]{1,0:T(8,128)(2,1)S(1)} %collective-permute-done.15.refs_1_, ...), custom_call_target="tpu_custom_call" | custom-call | tf_op jit(solution)/shard_map/logits_pool/pallas_call | solution.py:191
  53.8 2.8 %collective-permute-start.17 = (f32[4,2048]{1,0:T(4,128)S(1)}, f32[4,2048]{1,0:T(4,128)S(1)}, u32[]{:S(2)}, u32[]{:S(2)}) collective-permute-start(f32[4,2048]{1,0:T(4,128)S(1)} %get-tuple-element.54), channel_id=1, source_target_pairs={{0,96},{16,112},{32,0},{48,16},{64,32},{80,48},{96,64},{112,80},{1... | collective-permute-start | bytes 98312 | tf_op jit(solution)/shard_map/ppermute | solution.py:42
  56.6 0.8 collective-permute-start.18
  57.4 0.9 collective-permute-start.19
  58.4 3.7 %collective-permute-done.18 = f32[4,2048]{1,0:T(4,128)S(1)} collective-permute-done((f32[4,2048]{1,0:T(4,128)S(1)}, f32[4,2048]{1,0:T(4,128)S(1)}, u32[]{:S(2)}, u32[]{:S(2)}) %collective-permute-start.18) | collective-permute-done | bytes 32800 | tf_op jit(solution)/shard_map/ppermute | solution.py:42
  62.0 0.5 collective-permute-done.19
  62.6 3.7 %collective-permute-start.20 = (f32[16,2048]{1,0:T(8,128)S(1)}, f32[16,2048]{1,0:T(8,128)S(1)}, u32[]{:S(2)}, u32[]{:S(2)}) collective-permute-start(f32[16,2048]{1,0:T(8,128)S(1)} %pad_maximum_fusion.7.a.pa), channel_id=1, source_target_pairs={{0,16},{16,0},{32,48},{48,32},{64,80},{80,64},{96,112},{112,96},{1... | collective-permute-start | bytes 393224 | tf_op jit(solution)/shard_map/ppermute | solution.py:46
  66.3 0.7 gather_fusion
  67.0 2.2 %collective-permute-done.20.b.pb = f32[16,2048]{1,0:T(8,128)S(1)} collective-permute-done((f32[16,2048]{1,0:T(8,128)S(1)}, f32[16,2048]{1,0:T(8,128)S(1)}, u32[]{:S(2)}, u32[]{:S(2)}) %collective-permute-start.20) | collective-permute-done | bytes 131104 | tf_op jit(solution)/shard_map/ppermute | solution.py:46
  69.2 1.0 gram.1
  70.2 3.7 %all-to-all-start = ((f32[16,8,128]{2,1,0:T(8,128)}), f32[16,8,128]{2,1,0:T(8,128)S(1)}, u32[]{:S(2)}, u32[]{:S(2)}) async-start(f32[16,8,128]{2,1,0:T(8,128)} %gram.1), calls=%async_computation | async-start | bytes 131072 | tf_op jit(solution)/shard_map/all_to_all | solution.py:454
  73.9 5.8 %all-to-all-done.parts = f32[16,8,128]{2,1,0:T(8,128)S(1)} async-done(((f32[16,8,128]{2,1,0:T(8,128)}), f32[16,8,128]{2,1,0:T(8,128)S(1)}, u32[]{:S(2)}, u32[]{:S(2)}) %all-to-all-start) | async-done | bytes 65568 | tf_op jit(solution)/shard_map/all_to_all | solution.py:454
  79.8 5.1 %first_grad.1 = (bf16[768,2048]{1,0:T(8,128)(2,1)S(1)}, f32[8,128]{1,0:T(8,128)S(1)}, f32[768,256]{1,0:T(8,128)S(1)}, bf16[768,256]{1,0:T(8,128)(2,1)S(1)}) custom-call(s32[32]{0:T(128)S(1)} %get-tuple-element.99.idx, f32[16,8,128]{2,1,0:T(8,128)S(1)} %all-to-all-done.parts, f32[16,2048]{1,0:T(8,128)S(1)} %pad_maximum_fusion.7.a.pa, ...), custom_call_target="tpu_custom_call" | custom-call | tf_op jit(solution)/shard_map/first_grad/pallas_call | solution.py:304
  84.9 0.2 collective-permute-start.21
  85.1 1.6 %collective-permute-done.21 = bf16[768,256]{1,0:T(8,128)(2,1)S(1)} collective-permute-done((bf16[768,256]{1,0:T(8,128)(2,1)S(1)}, bf16[768,256]{1,0:T(8,128)(2,1)S(1)}, u32[]{:S(2)}, u32[]{:S(2)}) %collective-permute-start.21) | collective-permute-done | bytes 393248 | tf_op jit(solution)/shard_map/ppermute | solution.py:38
  86.7 0.1 add_convert_fusion
  86.9 0.6 collective-permute-start.22
  87.5 0.6 collective-permute-start.23
  88.2 8.0 %grad_part.3 = (f32[2304,256]{1,0:T(8,128)S(1)}, bf16[2304,256]{1,0:T(8,128)(2,1)S(1)}) custom-call(s32[32]{0:T(128)S(1)} %get-tuple-element.99.idx, bf16[768,2048]{1,0:T(8,128)(2,1)S(1)} %get-tuple-element.70.dl, bf16[4096,2048]{1,0:T(8,128)(2,1)} %w.7), custom_call_target="tpu_custom_call" | custom-call | tf_op jit(solution)/shard_map/grad_part/pallas_call | solution.py:349
  96.1 0.1 collective-permute-start.24
  96.3 0.2 add_arrived.3
  96.5 2.6 %collective-permute-done.24 = bf16[2304,256]{1,0:T(8,128)(2,1)S(1)} collective-permute-done((bf16[2304,256]{1,0:T(8,128)(2,1)S(1)}, bf16[2304,256]{1,0:T(8,128)(2,1)S(1)}, u32[]{:S(2)}, u32[]{:S(2)}) %collective-permute-start.24) | collective-permute-done | bytes 1179680 | tf_op jit(solution)/shard_map/ppermute | solution.py:38
  99.1 0.4 fusion.3
  99.7 0.7 collective-permute-start.25
  100.4 2.6 %collective-permute-start.26 = (bf16[768,256]{1,0:T(8,128)(2,1)S(1)}, bf16[768,256]{1,0:T(8,128)(2,1)S(1)}, u32[]{:S(2)}, u32[]{:S(2)}) collective-permute-start(bf16[768,256]{1,0:T(8,128)(2,1)S(1)} %pad_maximum_fusion.5), channel_id=1, source_target_pairs={{0,6},{1,7},{2,0},{3,1},{4,2},{5,3},{6,4},{7,5},{8,14},{9,15},{10,... | collective-permute-start | bytes 1179656 | tf_op jit(solution)/shard_map/ppermute | solution.py:30
  103.0 1.4 %collective-permute-start.27 = (bf16[768,256]{1,0:T(8,128)(2,1)S(1)}, bf16[768,256]{1,0:T(8,128)(2,1)S(1)}, u32[]{:S(2)}, u32[]{:S(2)}) collective-permute-start(bf16[768,256]{1,0:T(8,128)(2,1)S(1)} %pad_maximum_fusion.6), channel_id=1, source_target_pairs={{0,8},{1,9},{2,10},{3,11},{4,12},{5,13},{6,14},{7,15},{8,0},{9,1},... | collective-permute-start | bytes 1179656 | tf_op jit(solution)/shard_map/ppermute | solution.py:34
  104.4 8.0 %grad_part.4 = (f32[2304,256]{1,0:T(8,128)S(1)}, bf16[2304,256]{1,0:T(8,128)(2,1)S(1)}) custom-call(s32[32]{0:T(128)S(1)} %get-tuple-element.99.idx, bf16[768,2048]{1,0:T(8,128)(2,1)S(1)} %get-tuple-element.70.dl, bf16[4096,2048]{1,0:T(8,128)(2,1)} %w.7), custom_call_target="tpu_custom_call" | custom-call | tf_op jit(solution)/shard_map/grad_part/pallas_call | solution.py:349
  112.5 1.1 collective-permute-done.27.refs_3_
  113.6 0.4 add_arrived.4
  114.0 1.3 %collective-permute-done.28 = bf16[2304,256]{1,0:T(8,128)(2,1)S(1)} collective-permute-done((bf16[2304,256]{1,0:T(8,128)(2,1)S(1)}, bf16[2304,256]{1,0:T(8,128)(2,1)S(1)}, u32[]{:S(2)}, u32[]{:S(2)}) %collective-permute-start.28) | collective-permute-done | bytes 1179680 | tf_op jit(solution)/shard_map/ppermute | solution.py:38
  115.3 0.4 fusion
  115.8 3.2 %collective-permute-start.30 = (bf16[768,256]{1,0:T(8,128)(2,1)S(1)}, bf16[768,256]{1,0:T(8,128)(2,1)S(1)}, u32[]{:S(2)}, u32[]{:S(2)}) collective-permute-start(bf16[768,256]{1,0:T(8,128)(2,1)S(1)} %get-tuple-element.73), channel_id=1, source_target_pairs={{0,6},{1,7},{2,0},{3,1},{4,2},{5,3},{6,4},{7,5},{8,14},{9,15},{10,... | collective-permute-start | bytes 1179656 | tf_op jit(solution)/shard_map/ppermute | solution.py:30
  119.0 0.6 collective-permute-start.31
  119.6 0.6 slice_reduce_fusion
  120.3 4.1 %grad_part.5 = (f32[768,256]{1,0:T(8,128)S(1)}, bf16[768,256]{1,0:T(8,128)(2,1)S(1)}) custom-call(s32[32]{0:T(128)S(1)} %get-tuple-element.99.idx, bf16[768,2048]{1,0:T(8,128)(2,1)S(1)} %get-tuple-element.70.dl, bf16[4096,2048]{1,0:T(8,128)(2,1)} %w.7), custom_call_target="tpu_custom_call" | custom-call | tf_op jit(solution)/shard_map/grad_part/pallas_call | solution.py:349
  124.4 3.7 %collective-permute-done.29.refs_1_ = bf16[768,256]{1,0:T(8,128)(2,1)S(1)} collective-permute-done((bf16[768,256]{1,0:T(8,128)(2,1)S(1)}, bf16[768,256]{1,0:T(8,128)(2,1)S(1)}, u32[]{:S(2)}, u32[]{:S(2)}) %collective-permute-start.29) | collective-permute-done | bytes 393248 | tf_op jit(solution)/shard_map/ppermute | solution.py:30
  128.1 1.5 %collective-permute-done.31.refs_3_ = bf16[768,256]{1,0:T(8,128)(2,1)S(1)} collective-permute-done((bf16[768,256]{1,0:T(8,128)(2,1)S(1)}, bf16[768,256]{1,0:T(8,128)(2,1)S(1)}, u32[]{:S(2)}, u32[]{:S(2)}) %collective-permute-start.31) | collective-permute-done | bytes 393248 | tf_op jit(solution)/shard_map/ppermute | solution.py:34
  129.6 0.3 add_arrived.5.refs_0_
  129.9 0.8 add_last.1
  (50 shorter events, 1.0 us)
Async XLA Ops:
  0.6 65.7 %copy-start = (s32[16]{0:T(128)S(1)}, s32[16]{0:T(128)}, u32[]{:S(2)}) copy-start(s32[16]{0:T(128)} %param.12) | copy-start | bytes 196
  1.7 5.9 %collective-permute-start.3 = (bf16[768,256]{1,0:T(8,128)(2,1)S(1)}, bf16[768,256]{1,0:T(8,128)(2,1)S(1)}, u32[]{:S(2)}, u32[]{:S(2)}) collective-permute-start(bf16[768,256]{1,0:T(8,128)(2,1)S(1)} %pad_maximum_fusion.2.refs_0_), channel_id=1, source_target_pairs={{0,1},{1,0},{2,3},{3,2},{4,5},{5,4},{6,7},{7,6},{8,9},{9,8},{10,11... | collective-permute-start | bytes 1179656 | tf_op jit(solution)/shard_map/ppermute | solution.py:38
  1.8 12.1 %collective-permute-start = (bf16[768,256]{1,0:T(8,128)(2,1)S(1)}, bf16[768,256]{1,0:T(8,128)(2,1)S(1)}, u32[]{:S(2)}, u32[]{:S(2)}) collective-permute-start(bf16[768,256]{1,0:T(8,128)(2,1)S(1)} %pad_maximum_fusion.2.refs_0_), channel_id=1, source_target_pairs={{0,6},{1,7},{2,0},{3,1},{4,2},{5,3},{6,4},{7,5},{8,14},{9,15},{10,... | collective-permute-start | bytes 1179656 | tf_op jit(solution)/shard_map/ppermute | solution.py:30
  4.9 12.4 %collective-permute-start.1 = (bf16[768,256]{1,0:T(8,128)(2,1)S(1)}, bf16[768,256]{1,0:T(8,128)(2,1)S(1)}, u32[]{:S(2)}, u32[]{:S(2)}) collective-permute-start(bf16[768,256]{1,0:T(8,128)(2,1)S(1)} %pad_maximum_fusion.2.refs_0_), channel_id=1, source_target_pairs={{0,2},{1,3},{2,4},{3,5},{4,6},{5,7},{6,0},{7,1},{8,10},{9,11},{10,... | collective-permute-start | bytes 1179656 | tf_op jit(solution)/shard_map/ppermute | solution.py:30
  4.9 12.4 %collective-permute-start.2 = (bf16[768,256]{1,0:T(8,128)(2,1)S(1)}, bf16[768,256]{1,0:T(8,128)(2,1)S(1)}, u32[]{:S(2)}, u32[]{:S(2)}) collective-permute-start(bf16[768,256]{1,0:T(8,128)(2,1)S(1)} %pad_maximum_fusion.2.refs_0_), channel_id=1, source_target_pairs={{0,8},{1,9},{2,10},{3,11},{4,12},{5,13},{6,14},{7,15},{8,0},{9,1},... | collective-permute-start | bytes 1179656 | tf_op jit(solution)/shard_map/ppermute | solution.py:34
  17.3 2.9 %collective-permute-start.7 = (bf16[768,256]{1,0:T(8,128)(2,1)S(1)}, bf16[768,256]{1,0:T(8,128)(2,1)S(1)}, u32[]{:S(2)}, u32[]{:S(2)}) collective-permute-start(bf16[768,256]{1,0:T(8,128)(2,1)S(1)} %collective-permute-done.refs_0_), channel_id=1, source_target_pairs={{0,1},{1,0},{2,3},{3,2},{4,5},{5,4},{6,7},{7,6},{8,9},{9,8},{10,11... | collective-permute-start | bytes 1179656 | tf_op jit(solution)/shard_map/ppermute | solution.py:38
  17.3 4.8 %collective-permute-start.9 = (bf16[768,256]{1,0:T(8,128)(2,1)S(1)}, bf16[768,256]{1,0:T(8,128)(2,1)S(1)}, u32[]{:S(2)}, u32[]{:S(2)}) collective-permute-start(bf16[768,256]{1,0:T(8,128)(2,1)S(1)} %collective-permute-done.2.refs_4_), channel_id=1, source_target_pairs={{0,1},{1,0},{2,3},{3,2},{4,5},{5,4},{6,7},{7,6},{8,9},{9,8},{10,11... | collective-permute-start | bytes 1179656 | tf_op jit(solution)/shard_map/ppermute | solution.py:38
  17.9 4.2 %collective-permute-start.8 = (bf16[768,256]{1,0:T(8,128)(2,1)S(1)}, bf16[768,256]{1,0:T(8,128)(2,1)S(1)}, u32[]{:S(2)}, u32[]{:S(2)}) collective-permute-start(bf16[768,256]{1,0:T(8,128)(2,1)S(1)} %collective-permute-done.1.refs_2_), channel_id=1, source_target_pairs={{0,1},{1,0},{2,3},{3,2},{4,5},{5,4},{6,7},{7,6},{8,9},{9,8},{10,11... | collective-permute-start | bytes 1179656 | tf_op jit(solution)/shard_map/ppermute | solution.py:38
  18.2 12.2 %collective-permute-start.4 = (bf16[768,256]{1,0:T(8,128)(2,1)S(1)}, bf16[768,256]{1,0:T(8,128)(2,1)S(1)}, u32[]{:S(2)}, u32[]{:S(2)}) collective-permute-start(bf16[768,256]{1,0:T(8,128)(2,1)S(1)} %get-tuple-element.96), channel_id=1, source_target_pairs={{0,6},{1,7},{2,0},{3,1},{4,2},{5,3},{6,4},{7,5},{8,14},{9,15},{10,... | collective-permute-start | bytes 1179656 | tf_op jit(solution)/shard_map/ppermute | solution.py:30
  20.1 12.4 %collective-permute-start.5 = (bf16[768,256]{1,0:T(8,128)(2,1)S(1)}, bf16[768,256]{1,0:T(8,128)(2,1)S(1)}, u32[]{:S(2)}, u32[]{:S(2)}) collective-permute-start(bf16[768,256]{1,0:T(8,128)(2,1)S(1)} %get-tuple-element.97), channel_id=1, source_target_pairs={{0,2},{1,3},{2,4},{3,5},{4,6},{5,7},{6,0},{7,1},{8,10},{9,11},{10,... | collective-permute-start | bytes 1179656 | tf_op jit(solution)/shard_map/ppermute | solution.py:30
  20.3 16.4 %copy-start.1 = (s32[2,256]{1,0:T(2,128)S(1)}, s32[2,256]{1,0:T(2,128)}, u32[]{:S(2)}) copy-start(s32[2,256]{1,0:T(2,128)} %param.11) | copy-start | bytes 6148
  20.3 12.3 %collective-permute-start.6 = (bf16[768,256]{1,0:T(8,128)(2,1)S(1)}, bf16[768,256]{1,0:T(8,128)(2,1)S(1)}, u32[]{:S(2)}, u32[]{:S(2)}) collective-permute-start(bf16[768,256]{1,0:T(8,128)(2,1)S(1)} %get-tuple-element.95), channel_id=1, source_target_pairs={{0,8},{1,9},{2,10},{3,11},{4,12},{5,13},{6,14},{7,15},{8,0},{9,1},... | collective-permute-start | bytes 1179656 | tf_op jit(solution)/shard_map/ppermute | solution.py:34
  32.6 4.2 %collective-permute-start.12 = (bf16[768,256]{1,0:T(8,128)(2,1)S(1)}, bf16[768,256]{1,0:T(8,128)(2,1)S(1)}, u32[]{:S(2)}, u32[]{:S(2)}) collective-permute-start(bf16[768,256]{1,0:T(8,128)(2,1)S(1)} %collective-permute-done.4.refs_0_), channel_id=1, source_target_pairs={{0,1},{1,0},{2,3},{3,2},{4,5},{5,4},{6,7},{7,6},{8,9},{9,8},{10,11... | collective-permute-start | bytes 1179656 | tf_op jit(solution)/shard_map/ppermute | solution.py:38
  32.6 4.2 %collective-permute-start.13 = (bf16[768,256]{1,0:T(8,128)(2,1)S(1)}, bf16[768,256]{1,0:T(8,128)(2,1)S(1)}, u32[]{:S(2)}, u32[]{:S(2)}) collective-permute-start(bf16[768,256]{1,0:T(8,128)(2,1)S(1)} %collective-permute-done.5.refs_2_), channel_id=1, source_target_pairs={{0,1},{1,0},{2,3},{3,2},{4,5},{5,4},{6,7},{7,6},{8,9},{9,8},{10,11... | collective-permute-start | bytes 1179656 | tf_op jit(solution)/shard_map/ppermute | solution.py:38
  33.1 3.8 %collective-permute-start.14 = (bf16[768,256]{1,0:T(8,128)(2,1)S(1)}, bf16[768,256]{1,0:T(8,128)(2,1)S(1)}, u32[]{:S(2)}, u32[]{:S(2)}) collective-permute-start(bf16[768,256]{1,0:T(8,128)(2,1)S(1)} %collective-permute-done.6.refs_4_), channel_id=1, source_target_pairs={{0,1},{1,0},{2,3},{3,2},{4,5},{5,4},{6,7},{7,6},{8,9},{9,8},{10,11... | collective-permute-start | bytes 1179656 | tf_op jit(solution)/shard_map/ppermute | solution.py:38
  33.1 11.9 %collective-permute-start.10 = (bf16[384,256]{1,0:T(8,128)(2,1)S(1)}, bf16[384,256]{1,0:T(8,128)(2,1)S(1)}, u32[]{:S(2)}, u32[]{:S(2)}) collective-permute-start(bf16[384,256]{1,0:T(8,128)(2,1)S(1)} %slice.93), channel_id=1, source_target_pairs={{0,6},{1,7},{2,0},{3,1},{4,2},{5,3},{6,4},{7,5},{8,14},{9,15},{10,... | collective-permute-start | bytes 589832 | tf_op jit(solution)/shard_map/ppermute | solution.py:30
  35.0 10.1 %collective-permute-start.11 = (bf16[384,256]{1,0:T(8,128)(2,1)S(1)}, bf16[384,256]{1,0:T(8,128)(2,1)S(1)}, u32[]{:S(2)}, u32[]{:S(2)}) collective-permute-start(bf16[384,256]{1,0:T(8,128)(2,1)S(1)} %slice.94), channel_id=1, source_target_pairs={{0,8},{1,9},{2,10},{3,11},{4,12},{5,13},{6,14},{7,15},{8,0},{9,1},... | collective-permute-start | bytes 589832 | tf_op jit(solution)/shard_map/ppermute | solution.py:34
  36.8 8.9 %copy-start.2 = (s32[2,128]{1,0:T(2,128)S(1)}, s32[2,128]{1,0:T(2,128)}, u32[]{:S(2)}) copy-start(s32[2,128]{1,0:T(2,128)} %param.10) | copy-start | bytes 3076
  45.1 1.5 %collective-permute-start.15 = (bf16[384,256]{1,0:T(8,128)(2,1)S(1)}, bf16[384,256]{1,0:T(8,128)(2,1)S(1)}, u32[]{:S(2)}, u32[]{:S(2)}) collective-permute-start(bf16[384,256]{1,0:T(8,128)(2,1)S(1)} %collective-permute-done.10.refs_0_), channel_id=1, source_target_pairs={{0,1},{1,0},{2,3},{3,2},{4,5},{5,4},{6,7},{7,6},{8,9},{9,8},{10,11... | collective-permute-start | bytes 589832 | tf_op jit(solution)/shard_map/ppermute | solution.py:38
  45.2 1.7 %collective-permute-start.16 = (bf16[384,256]{1,0:T(8,128)(2,1)S(1)}, bf16[384,256]{1,0:T(8,128)(2,1)S(1)}, u32[]{:S(2)}, u32[]{:S(2)}) collective-permute-start(bf16[384,256]{1,0:T(8,128)(2,1)S(1)} %collective-permute-done.11.refs_2_), channel_id=1, source_target_pairs={{0,1},{1,0},{2,3},{3,2},{4,5},{5,4},{6,7},{7,6},{8,9},{9,8},{10,11... | collective-permute-start | bytes 589832 | tf_op jit(solution)/shard_map/ppermute | solution.py:38
  53.8 4.6 %collective-permute-start.17 = (f32[4,2048]{1,0:T(4,128)S(1)}, f32[4,2048]{1,0:T(4,128)S(1)}, u32[]{:S(2)}, u32[]{:S(2)}) collective-permute-start(f32[4,2048]{1,0:T(4,128)S(1)} %get-tuple-element.54), channel_id=1, source_target_pairs={{0,96},{16,112},{32,0},{48,16},{64,32},{80,48},{96,64},{112,80},{1... | collective-permute-start | bytes 98312 | tf_op jit(solution)/shard_map/ppermute | solution.py:42
  56.6 5.4 %collective-permute-start.18 = (f32[4,2048]{1,0:T(4,128)S(1)}, f32[4,2048]{1,0:T(4,128)S(1)}, u32[]{:S(2)}, u32[]{:S(2)}) collective-permute-start(f32[4,2048]{1,0:T(4,128)S(1)} %get-tuple-element.54), channel_id=1, source_target_pairs={{0,64},{16,80},{32,96},{48,112},{64,0},{80,16},{96,32},{112,48},{1... | collective-permute-start | bytes 98312 | tf_op jit(solution)/shard_map/ppermute | solution.py:42
  57.4 5.1 %collective-permute-start.19 = (f32[4,2048]{1,0:T(4,128)S(1)}, f32[4,2048]{1,0:T(4,128)S(1)}, u32[]{:S(2)}, u32[]{:S(2)}) collective-permute-start(f32[4,2048]{1,0:T(4,128)S(1)} %get-tuple-element.54), channel_id=1, source_target_pairs={{0,32},{16,48},{32,64},{48,80},{64,96},{80,112},{96,0},{112,16},{1... | collective-permute-start | bytes 98312 | tf_op jit(solution)/shard_map/ppermute | solution.py:42
  62.6 6.6 %collective-permute-start.20 = (f32[16,2048]{1,0:T(8,128)S(1)}, f32[16,2048]{1,0:T(8,128)S(1)}, u32[]{:S(2)}, u32[]{:S(2)}) collective-permute-start(f32[16,2048]{1,0:T(8,128)S(1)} %pad_maximum_fusion.7.a.pa), channel_id=1, source_target_pairs={{0,16},{16,0},{32,48},{48,32},{64,80},{80,64},{96,112},{112,96},{1... | collective-permute-start | bytes 393224 | tf_op jit(solution)/shard_map/ppermute | solution.py:46
  70.2 9.6 %all-to-all-start = ((f32[16,8,128]{2,1,0:T(8,128)}), f32[16,8,128]{2,1,0:T(8,128)S(1)}, u32[]{:S(2)}, u32[]{:S(2)}) async-start(f32[16,8,128]{2,1,0:T(8,128)} %gram.1), calls=%async_computation | async-start | bytes 131072 | tf_op jit(solution)/shard_map/all_to_all | solution.py:454
  84.9 1.8 %collective-permute-start.21 = (bf16[768,256]{1,0:T(8,128)(2,1)S(1)}, bf16[768,256]{1,0:T(8,128)(2,1)S(1)}, u32[]{:S(2)}, u32[]{:S(2)}) collective-permute-start(bf16[768,256]{1,0:T(8,128)(2,1)S(1)} %get-tuple-element.60), channel_id=1, source_target_pairs={{0,1},{1,0},{2,3},{3,2},{4,5},{5,4},{6,7},{7,6},{8,9},{9,8},{10,11... | collective-permute-start | bytes 1179656 | tf_op jit(solution)/shard_map/ppermute | solution.py:38
  86.9 9.4 %collective-permute-start.22 = (bf16[384,256]{1,0:T(8,128)(2,1)S(1)}, bf16[384,256]{1,0:T(8,128)(2,1)S(1)}, u32[]{:S(2)}, u32[]{:S(2)}) collective-permute-start(bf16[384,256]{1,0:T(8,128)(2,1)S(1)} %get-tuple-element.92), channel_id=1, source_target_pairs={{0,2},{1,3},{2,4},{3,5},{4,6},{5,7},{6,0},{7,1},{8,10},{9,11},{10,... | collective-permute-start | bytes 589832 | tf_op jit(solution)/shard_map/ppermute | solution.py:30
  87.5 8.7 %collective-permute-start.23 = (bf16[384,256]{1,0:T(8,128)(2,1)S(1)}, bf16[384,256]{1,0:T(8,128)(2,1)S(1)}, u32[]{:S(2)}, u32[]{:S(2)}) collective-permute-start(bf16[384,256]{1,0:T(8,128)(2,1)S(1)} %get-tuple-element.91), channel_id=1, source_target_pairs={{0,8},{1,9},{2,10},{3,11},{4,12},{5,13},{6,14},{7,15},{8,0},{9,1},... | collective-permute-start | bytes 589832 | tf_op jit(solution)/shard_map/ppermute | solution.py:34
  96.1 2.9 %collective-permute-start.24 = (bf16[2304,256]{1,0:T(8,128)(2,1)S(1)}, bf16[2304,256]{1,0:T(8,128)(2,1)S(1)}, u32[]{:S(2)}, u32[]{:S(2)}) collective-permute-start(bf16[2304,256]{1,0:T(8,128)(2,1)S(1)} %get-tuple-element.63), channel_id=1, source_target_pairs={{0,1},{1,0},{2,3},{3,2},{4,5},{5,4},{6,7},{7,6},{8,9},{9,8},{10,11... | collective-permute-start | bytes 3538952 | tf_op jit(solution)/shard_map/ppermute | solution.py:38
  99.7 12.8 %collective-permute-start.25 = (bf16[768,256]{1,0:T(8,128)(2,1)S(1)}, bf16[768,256]{1,0:T(8,128)(2,1)S(1)}, u32[]{:S(2)}, u32[]{:S(2)}) collective-permute-start(bf16[768,256]{1,0:T(8,128)(2,1)S(1)} %pad_maximum_fusion.4), channel_id=1, source_target_pairs={{0,2},{1,3},{2,4},{3,5},{4,6},{5,7},{6,0},{7,1},{8,10},{9,11},{10,... | collective-permute-start | bytes 1179656 | tf_op jit(solution)/shard_map/ppermute | solution.py:30
  100.4 12.1 %collective-permute-start.26 = (bf16[768,256]{1,0:T(8,128)(2,1)S(1)}, bf16[768,256]{1,0:T(8,128)(2,1)S(1)}, u32[]{:S(2)}, u32[]{:S(2)}) collective-permute-start(bf16[768,256]{1,0:T(8,128)(2,1)S(1)} %pad_maximum_fusion.5), channel_id=1, source_target_pairs={{0,6},{1,7},{2,0},{3,1},{4,2},{5,3},{6,4},{7,5},{8,14},{9,15},{10,... | collective-permute-start | bytes 1179656 | tf_op jit(solution)/shard_map/ppermute | solution.py:30
  103.0 10.6 %collective-permute-start.27 = (bf16[768,256]{1,0:T(8,128)(2,1)S(1)}, bf16[768,256]{1,0:T(8,128)(2,1)S(1)}, u32[]{:S(2)}, u32[]{:S(2)}) collective-permute-start(bf16[768,256]{1,0:T(8,128)(2,1)S(1)} %pad_maximum_fusion.6), channel_id=1, source_target_pairs={{0,8},{1,9},{2,10},{3,11},{4,12},{5,13},{6,14},{7,15},{8,0},{9,1},... | collective-permute-start | bytes 1179656 | tf_op jit(solution)/shard_map/ppermute | solution.py:34
  112.4 2.9 %collective-permute-start.28 = (bf16[2304,256]{1,0:T(8,128)(2,1)S(1)}, bf16[2304,256]{1,0:T(8,128)(2,1)S(1)}, u32[]{:S(2)}, u32[]{:S(2)}) collective-permute-start(bf16[2304,256]{1,0:T(8,128)(2,1)S(1)} %get-tuple-element.69), channel_id=1, source_target_pairs={{0,1},{1,0},{2,3},{3,2},{4,5},{5,4},{6,7},{7,6},{8,9},{9,8},{10,11... | collective-permute-start | bytes 3538952 | tf_op jit(solution)/shard_map/ppermute | solution.py:38
  115.7 12.4 %collective-permute-start.29 = (bf16[768,256]{1,0:T(8,128)(2,1)S(1)}, bf16[768,256]{1,0:T(8,128)(2,1)S(1)}, u32[]{:S(2)}, u32[]{:S(2)}) collective-permute-start(bf16[768,256]{1,0:T(8,128)(2,1)S(1)} %get-tuple-element.72), channel_id=1, source_target_pairs={{0,2},{1,3},{2,4},{3,5},{4,6},{5,7},{6,0},{7,1},{8,10},{9,11},{10,... | collective-permute-start | bytes 1179656 | tf_op jit(solution)/shard_map/ppermute | solution.py:30
  115.8 12.4 %collective-permute-start.30 = (bf16[768,256]{1,0:T(8,128)(2,1)S(1)}, bf16[768,256]{1,0:T(8,128)(2,1)S(1)}, u32[]{:S(2)}, u32[]{:S(2)}) collective-permute-start(bf16[768,256]{1,0:T(8,128)(2,1)S(1)} %get-tuple-element.73), channel_id=1, source_target_pairs={{0,6},{1,7},{2,0},{3,1},{4,2},{5,3},{6,4},{7,5},{8,14},{9,15},{10,... | collective-permute-start | bytes 1179656 | tf_op jit(solution)/shard_map/ppermute | solution.py:30
  119.0 10.6 %collective-permute-start.31 = (bf16[768,256]{1,0:T(8,128)(2,1)S(1)}, bf16[768,256]{1,0:T(8,128)(2,1)S(1)}, u32[]{:S(2)}, u32[]{:S(2)}) collective-permute-start(bf16[768,256]{1,0:T(8,128)(2,1)S(1)} %get-tuple-element.74), channel_id=1, source_target_pairs={{0,8},{1,9},{2,10},{3,11},{4,12},{5,13},{6,14},{7,15},{8,0},{9,1},... | collective-permute-start | bytes 1179656 | tf_op jit(solution)/shard_map/ppermute | solution.py:34
  124.4 5.5 %collective-permute-start.32 = (bf16[768,256]{1,0:T(8,128)(2,1)S(1)}, bf16[768,256]{1,0:T(8,128)(2,1)S(1)}, u32[]{:S(2)}, u32[]{:S(2)}) collective-permute-start(bf16[768,256]{1,0:T(8,128)(2,1)S(1)} %get-tuple-element.75), channel_id=1, source_target_pairs={{0,1},{1,0},{2,3},{3,2},{4,5},{5,4},{6,7},{7,6},{8,9},{9,8},{10,11... | collective-permute-start | bytes 1179656 | tf_op jit(solution)/shard_map/ppermute | solution.py:38

commit v4 on v3

--- a/solution.py
+++ b/solution.py
@@ -112,7 +112,7 @@
     return pl.ds(pl.multiple_of(pl.program_id(0) * bn, bn), bn)
 
 
-def logits_kernel(copies, places, nx, bn, steps, has_acc, idx, *refs):
+def logits_kernel(copies, places, nx, bn, steps, has_acc, following, idx, *refs):
     xrefs = refs[:nx]
     w = refs[nx]
     pos = nx + 1
@@ -120,8 +120,32 @@
     if has_acc:
         acc = refs[pos]
         pos += 1
-    out, xs, ws, xsem, wsem = refs[pos:]
+    out = refs[pos]
+    if following is not None:
+        ahead, asem = refs[pos + 1], refs[-1]
+        refs = refs[:-1]
+        ahead_copies = [
+            pltpu.make_async_copy(
+                w.at[pl.ds(pl.multiple_of((idx[following] * 2 + side) * BLK, BLK), BLK), :],
+                ahead.at[pl.ds(k * BLK, BLK), :],
+                asem.at[k],
+            )
+            for k, side in enumerate((idx[8], 1 - idx[8]))
+        ]
+    xs, ws, xsem, wsem = refs[-4:]
     slot = load_operands(copies, places, bn, steps, idx, xrefs, w, xs, ws, xsem, wsem)
+    if following is not None:
+
+        @pl.when(pl.program_id(0) == 0)
+        def _():
+            for c in ahead_copies:
+                c.start()
+
+        @pl.when(pl.program_id(0) == steps - 1)
+        def _():
+            for c in ahead_copies:
+                c.wait()
+
     res = jnp.dot(xs[...], ws[slot], preferred_element_type=F32)
     cols = columns_of(bn)
     if has_acc:
@@ -129,7 +153,7 @@
     out[:, cols] = res
 
 
-def logits_part(arrays, copies, places, idx, w, acc):
+def logits_part(arrays, copies, places, idx, w, acc, following=None):
     rows = 768
     cols = w.shape[1]
     nk = 2 * len(places)
@@ -139,73 +163,84 @@
     vm = pl.BlockSpec(memory_space=pltpu.VMEM)
     ins = list(arrays) + [w] + ([acc] if acc is not None else [])
     return pl.pallas_call(
-        functools.partial(logits_kernel, copies, places, len(arrays), bn, steps, acc is not None),
+        functools.partial(logits_kernel, copies, places, len(arrays), bn, steps, acc is not None, following),
         grid_spec=pltpu.PrefetchScalarGridSpec(
             num_scalar_prefetch=1,
             grid=(steps,),
             in_specs=[any_spec] * len(arrays) + [HBM_SPEC] + ([vm] if acc is not None else []),
-            out_specs=vm,
+            out_specs=[vm] * (1 if following is None else 2),
             scratch_shapes=[
                 pltpu.VMEM((rows, nk * BLK), BF),
                 pltpu.VMEM((2, nk * BLK, bn), BF),
                 pltpu.SemaphoreType.DMA((len(copies),)),
                 pltpu.SemaphoreType.DMA((2, nk)),
-            ],
+            ]
+            + ([] if following is None else [pltpu.SemaphoreType.DMA((2,))]),
         ),
-        out_shape=jax.ShapeDtypeStruct((rows, cols), F32),
+        out_shape=[jax.ShapeDtypeStruct((rows, cols), F32)]
+        + ([] if following is None else [jax.ShapeDtypeStruct((2 * BLK, cols), BF)]),
         input_output_aliases={len(arrays) + 2: 0} if acc is not None else {},
         compiler_params=pltpu.CompilerParams(vmem_limit_bytes=(14 if nk > 2 else 12) * MIB),
         name="logits_part",
     )(idx, *ins)
 
 
-def pool_kernel(copies, places, nx, bn, steps, seqs, idx, lens, *refs):
+def pool_kernel(copies, nx, bn, seqs, lens, *refs):
     xrefs = refs[:nx]
-    w, acc, expo, stats, pooled, xs, ws, xsem, wsem = refs[nx:]
-    slot = load_operands(copies, places, bn, steps, idx, xrefs, w, xs, ws, xsem, wsem)
-    logits = jnp.dot(xs[...], ws[slot], preferred_element_type=F32) + acc[:, columns_of(bn)]
-    smooth, sums = [], []
-    for s, (start, n) in enumerate(seqs):
-        part = logits[start : start + n] * (1.0 / SHARP)
-        live = lax.broadcasted_iota(jnp.int32, (n, 1), 0) < lens[s]
-        part = jnp.where(live, part, -1e30)
-        top = jnp.max(part, axis=0, keepdims=True)
-        e = jnp.exp(part - top)
-        total = jnp.sum(e, axis=0, keepdims=True)
-        expo[pl.ds(start, n), :] = e.astype(BF)
-        smooth.append(SHARP * (top + jnp.log(total)))
-        sums.append(total)
-    both = jnp.concatenate(smooth + sums, axis=0)
-    stats[...] = both
-    pooled[...] = jnp.log1p(jnp.maximum(both[:4], 0.0))
-
-
-def logits_pool(arrays, copies, places, idx, lens, w, acc, seqs):
+    ws, acc, expo, stats, pooled, xs, es, xsem, esem = refs[nx:]
+    steps = ws.shape[1] // bn
+    loads = []
+    for i, (a, k, src, dst, n) in enumerate(copies):
+        loads.append(
+            pltpu.make_async_copy(
+                xrefs[a].at[pl.ds(src, n), :], xs.at[pl.ds(dst, n), pl.ds(k * BLK, BLK)], xsem.at[i]
+            )
+        )
+    for c in loads:
+        c.start()
+    for c in loads:
+        c.wait()
+    outs = []
+    for j in range(steps):
+        cols = pl.ds(j * bn, bn)
+        logits = jnp.dot(xs[...], ws[:, cols], preferred_element_type=F32) + acc[:, cols]
+        smooth, sums = [], []
+        for s, (start, n) in enumerate(seqs):
+            live = lax.broadcasted_iota(jnp.int32, (n, 1), 0) < lens[s]
+            part = jnp.where(live, logits[start : start + n], -1e30)
+            top = jnp.max(part, axis=0, keepdims=True)
+            e = jnp.exp((part - top) * (1.0 / SHARP))
+            total = jnp.sum(e, axis=0, keepdims=True)
+            es[pl.ds(start, n), cols] = e.astype(BF)
+            smooth.append(top + SHARP * jnp.log(total))
+            sums.append(total)
+        both = jnp.concatenate(smooth + sums, axis=0)
+        stats[:, cols] = both
+        pooled[:, cols] = jnp.log1p(jnp.maximum(both[:4], 0.0))
+        out = pltpu.make_async_copy(es.at[:, cols], expo.at[:, cols], esem.at[j])
+        out.start()
+        outs.append(out)
+    for out in outs:
+        out.wait()
+
+
+def logits_pool(arrays, copies, lens, w, acc, seqs):
     rows = 768
     cols = w.shape[1]
-    nk = 2 * len(places)
     bn = 512
-    steps = cols // bn
     any_spec = pl.BlockSpec(memory_space=pl.ANY)
-    blk = pl.BlockSpec((rows, bn), lambda j, *_: (0, j))
-    return pl.pallas_call(
-        functools.partial(pool_kernel, copies, places, len(arrays), bn, steps, seqs),
-        grid_spec=pltpu.PrefetchScalarGridSpec(
-            num_scalar_prefetch=2,
-            grid=(steps,),
-            in_specs=[any_spec] * len(arrays) + [HBM_SPEC, pl.BlockSpec(memory_space=pltpu.VMEM)],
-            out_specs=[
-                blk,
-                pl.BlockSpec((8, bn), lambda j, *_: (0, j)),
-                pl.BlockSpec((4, bn), lambda j, *_: (0, j)),
-            ],
-            scratch_shapes=[
-                pltpu.VMEM((rows, nk * BLK), BF),
-                pltpu.VMEM((2, nk * BLK, bn), BF),
-                pltpu.SemaphoreType.DMA((len(copies),)),
-                pltpu.SemaphoreType.DMA((2, nk)),
-            ],
-        ),
+    vm = pl.BlockSpec(memory_space=pltpu.VMEM)
+    sm = pl.BlockSpec(memory_space=pltpu.SMEM)
+    return pl.pallas_call(
+        functools.partial(pool_kernel, copies, len(arrays), bn, seqs),
+        in_specs=[sm] + [any_spec] * len(arrays) + [vm, vm],
+        out_specs=[HBM_SPEC, vm, vm],
+        scratch_shapes=[
+            pltpu.VMEM((rows, 2 * BLK), BF),
+            pltpu.VMEM((rows, cols), BF),
+            pltpu.SemaphoreType.DMA((len(copies),)),
+            pltpu.SemaphoreType.DMA((cols // bn,)),
+        ],
         out_shape=[
             pltpu.HBM((rows, cols), BF),
             jax.ShapeDtypeStruct((8, cols), F32),
@@ -213,7 +248,7 @@
         ],
         compiler_params=pltpu.CompilerParams(vmem_limit_bytes=16 * MIB),
         name="logits_pool",
-    )(idx, lens, *arrays, w, acc)
+    )(lens, *arrays, w, acc)
 
 
 def exact_dot(a, b, dims):
@@ -263,17 +298,20 @@
 
 
 def first_grad_kernel(
-    seqs, place, total_queries, idx, parts, pa, pb, stats, picked, expo, w, dl, loss, mine, sib, es, ws, esem, wsem
+    seqs, place, following, total_queries, idx, parts, pa, pb, stats, picked, expo, w, dl, loss, mine, sib, ahead, es, ws, esem, wsem
 ):
     e_copies = [
         pltpu.make_async_copy(expo.at[pl.ds(start, n), :], es.at[pl.ds(start, n), :], esem.at[s])
         for s, (start, n) in enumerate(seqs)
     ]
     row0 = pl.multiple_of(idx[place] * (2 * BLK), 2 * BLK)
-    w_copy = pltpu.make_async_copy(w.at[pl.ds(row0, 2 * BLK), :], ws, wsem)
+    w_copy = pltpu.make_async_copy(w.at[pl.ds(row0, 2 * BLK), :], ws, wsem.at[0])
+    row1 = pl.multiple_of(idx[following] * (2 * BLK), 2 * BLK)
+    ahead_copy = pltpu.make_async_copy(w.at[pl.ds(row1, 2 * BLK), :], ahead, wsem.at[1])
     for c in e_copies:
         c.start()
     w_copy.start()
+    ahead_copy.start()
     scores = parts[0]
     for i in range(1, parts.shape[0]):
         scores = scores + parts[i]
@@ -296,69 +334,68 @@
         dl[pl.ds(start, n), :] = (es[pl.ds(start, n), :].astype(F32) * g[s : s + 1, :]).astype(BF)
     w_copy.wait()
     store_halves(idx[8], nt_dot(dl[...], ws[...]), mine, sib)
-
-
-def first_grad(place, idx, parts, pa, pb, stats, picked, expo, w, seqs, total_queries):
+    ahead_copy.wait()
+
+
+def first_grad(place, following, idx, parts, pa, pb, stats, picked, expo, w, seqs, total_queries):
     rows, cols = expo.shape
     vm = pl.BlockSpec(memory_space=pltpu.VMEM)
     return pl.pallas_call(
-        functools.partial(first_grad_kernel, seqs, place, total_queries),
+        functools.partial(first_grad_kernel, seqs, place, following, total_queries),
         in_specs=[pl.BlockSpec(memory_space=pltpu.SMEM)] + [vm] * 5 + [HBM_SPEC] * 2,
-        out_specs=[vm] * 4,
+        out_specs=[vm] * 5,
         scratch_shapes=[
             pltpu.VMEM((rows, cols), BF),
             pltpu.VMEM((2 * BLK, cols), BF),
             pltpu.SemaphoreType.DMA((len(seqs),)),
-            pltpu.SemaphoreType.DMA,
+            pltpu.SemaphoreType.DMA((2,)),
         ],
         out_shape=[
             jax.ShapeDtypeStruct((rows, cols), BF),
             jax.ShapeDtypeStruct((8, 128), F32),
             jax.ShapeDtypeStruct((rows, BLK), F32),
             jax.ShapeDtypeStruct((rows, BLK), BF),
+            jax.ShapeDtypeStruct((2 * BLK, cols), BF),
         ],
         compiler_params=pltpu.CompilerParams(vmem_limit_bytes=18 * MIB),
         name="first_grad",
     )(idx, parts, pa, pb, stats, picked, pltpu.with_memory_space_constraint(expo, pltpu.HBM), w)
 
 
-def grad_kernel(first, n, idx, dl, w, mine, sib, ws, wsem):
-    i = pl.program_id(0)
-
-    def w_copy(step, slot):
+def grad_kernel(first, n, has_ahead, idx, dl, w, *refs):
+    ahead = refs[0] if has_ahead else None
+    mine, sib, ws, wsem = refs[has_ahead:]
+
+    def w_copy(step):
         row = pl.multiple_of(idx[first + step] * (2 * BLK), 2 * BLK)
-        return pltpu.make_async_copy(w.at[pl.ds(row, 2 * BLK), :], ws.at[slot], wsem.at[slot])
-
-    slot = lax.rem(i, 2)
-
-    @pl.when(i == 0)
-    def _():
-        w_copy(0, 0).start()
-
-    @pl.when(i + 1 < n)
-    def _():
-        w_copy(i + 1, 1 - slot).start()
-
-    w_copy(i, slot).wait()
-    store_halves(idx[8], nt_dot(dl[...], ws[slot]), mine, sib)
-
-
-def grad_part(first, n, idx, dl, w):
+        return pltpu.make_async_copy(w.at[pl.ds(row, 2 * BLK), :], ws.at[step - has_ahead], wsem.at[step - has_ahead])
+
+    for i in range(has_ahead, n):
+        w_copy(i).start()
+    rows = dl.shape[0]
+    for i in range(n):
+        here = pl.ds(i * rows, rows)
+        if i < has_ahead:
+            block = ahead[...]
+        else:
+            w_copy(i).wait()
+            block = ws[i - has_ahead]
+        store_halves(idx[8], nt_dot(dl[...], block), mine.at[here], sib.at[here])
+
+
+def grad_part(first, n, idx, dl, w, ahead=None):
     rows, cols = dl.shape
-    out = pl.BlockSpec((rows, BLK), lambda i, idx: (i, 0))
-    return pl.pallas_call(
-        functools.partial(grad_kernel, first, n),
-        grid_spec=pltpu.PrefetchScalarGridSpec(
-            num_scalar_prefetch=1,
-            grid=(n,),
-            in_specs=[pl.BlockSpec(memory_space=pltpu.VMEM), HBM_SPEC],
-            out_specs=[out, out],
-            scratch_shapes=[pltpu.VMEM((2, 2 * BLK, cols), BF), pltpu.SemaphoreType.DMA((2,))],
-        ),
+    vm = pl.BlockSpec(memory_space=pltpu.VMEM)
+    has = 0 if ahead is None else 1
+    return pl.pallas_call(
+        functools.partial(grad_kernel, first, n, has),
+        in_specs=[pl.BlockSpec(memory_space=pltpu.SMEM), vm, HBM_SPEC] + [vm] * has,
+        out_specs=[vm, vm],
+        scratch_shapes=[pltpu.VMEM((n - has, 2 * BLK, cols), BF), pltpu.SemaphoreType.DMA((n - has,))],
         out_shape=[jax.ShapeDtypeStruct((n * rows, BLK), F32), jax.ShapeDtypeStruct((n * rows, BLK), BF)],
-        compiler_params=pltpu.CompilerParams(vmem_limit_bytes=12 * MIB),
+        compiler_params=pltpu.CompilerParams(vmem_limit_bytes=16 * MIB),
         name="grad_part",
-    )(idx, dl, w)
+    )(idx, dl, w, *([ahead] if has else []))
 
 
 def add_kernel(spec, n_mine, *refs):
@@ -419,14 +456,14 @@
 
     x10, xm0, x01 = to_y(own, -1), to_y(own, 1), to_z(own)
     own_s = to_core(own)
-    acc = logits_part([own, own_s], ((0, 0, 0, 0, 768), (1, 1, 0, 0, 768)), (0,), idx, w, None)
+    acc = logits_part([own, own_s], ((0, 0, 0, 0, 768), (1, 1, 0, 0, 768)), (0,), idx, w, None)[0]
     x10, xm0, x01, acc = lax.optimization_barrier((x10, xm0, x01, acc))
     f1 = to_y(jnp.concatenate([x10[:h], x01[h:]], axis=0), -1)
     f2 = to_y(jnp.concatenate([x01[h:], xm0[h:]], axis=0), 1)
     f3 = to_z(jnp.concatenate([x10[:h], xm0[:h]], axis=0))
     near = [t for p in (x10, xm0, x01) for t in (p, to_core(p))]
     whole = tuple((i, i, 0, 0, 768) for i in range(6))
-    acc = logits_part(near, whole, (1, 2, 3), idx, w, acc)
+    acc = logits_part(near, whole, (1, 2, 3), idx, w, acc)[0]
     f1, f2, f3, acc = lax.optimization_barrier((f1, f2, f3, acc))
     g1 = to_y(f3[:h], -1)
     g2 = to_z(f2[h:])
@@ -441,13 +478,13 @@
             (4 + c, 4 + c, h, 0, h),
             (2 + c, 4 + c, 0, h, h),
         ]
-    acc = logits_part(mid, tuple(mid_copies), (4, 5, 6), idx, w, acc)
+    acc, w21 = logits_part(mid, tuple(mid_copies), (4, 5, 6), idx, w, acc, 7)
     g1, g2, acc = lax.optimization_barrier((g1, g2, acc))
     last = [t for p in (g1, g2) for t in (p, to_core(p))]
     last_copies = tuple((2 * i + c, c, 0, h * i, h) for i in range(2) for c in range(2))
     query_mask, passage_mask, positive = lax.optimization_barrier((query_mask, passage_mask, positive, x10))[:3]
     lens = jnp.concatenate([jnp.sum(query_mask > 0, axis=1), jnp.sum(passage_mask > 0, axis=1)]).astype(jnp.int32)
-    expo, stats, pooled = logits_pool(last, last_copies, (7,), idx, lens, w, acc, seqs)
+    expo, stats, pooled = logits_pool(last, last_copies, lens, w21, acc, seqs)
 
     pa = jnp.concatenate([pooled] + [to_x(pooled, -k) for k in (1, 2, 3)], axis=0)
     pb = to_zhi(pa)
@@ -457,13 +494,13 @@
     target = positive[seq]
     picked = (target[:, None] == seq[None, :]).astype(F32)
 
-    dl, loss, m21, s21 = first_grad(7, idx, parts, pa, pb, stats, picked, expo, w, seqs, positive.shape[0])
+    dl, loss, m21, s21, ahead = first_grad(7, 4, idx, parts, pa, pb, stats, picked, expo, w, seqs, positive.shape[0])
     t21 = (m21 + to_core(s21)).astype(BF)
     def rows(x, i):
         return x[768 * i : 768 * (i + 1)]
 
     r1, r2 = to_y(t21[:h], 1), to_z(t21[h:])
-    mb, sb = grad_part(4, 3, idx, after(dl, t21), w)
+    mb, sb = grad_part(4, 3, idx, after(dl, t21), w, ahead)
     sb = to_core(sb)
     (mb,) = add_arrived((mb,), (r1, r2), ((0, 0, 0, 768, h), (0, 1, 0, h, h)))
     t20, t11, tm1 = ((rows(mb, i) + rows(sb, i)).astype(BF) for i in range(3))

time: 131 us -> 129 us (0.985)
  Pallas kernels: 56.3 us -> 54.6 us
    pallas_call x5, Pallas kernels: 32 us -> 30.1 us  [the longest x3 19.8 us: grad_part(): pl.pallas_call(functools.partial(grad_kernel, first, n, has), in_specs=[p...]
where the time goes in v4:
time: 129 us
  Pallas kernels  54.6 us (42%)
  starting transfers between devices  36.6 us (28%)
  waiting for transfers between devices  31.9 us (25%)
  other arithmetic  2.51 us (2%)
  local copies, waits for them, and re-layouts  2.26 us (2%)
    pallas_call x3, Pallas kernels, logits_part(): pl.pallas_call(functools.partial(logits_kernel, copies, places, len(array...  21.9 us
    pallas_call x3, Pallas kernels, grad_part(): pl.pallas_call(functools.partial(grad_kernel, first, n, has), in_specs=[p...  19.8 us
    ppermute x10, starting transfers between devices, to_y(): return lax.ppermute(x, 'vocab', y_perm(k % 4))  14.3 us
    ppermute x10, waiting for transfers between devices, to_y(): return lax.ppermute(x, 'vocab', y_perm(k % 4))  10.4 us
    ppermute x6, starting transfers between devices, to_z(): return lax.ppermute(x, 'vocab', Z_SWAP)  8.25 us
    ppermute x13, waiting for transfers between devices, to_core(): return lax.ppermute(x, 'vocab', CORE_SWAP)  6.84 us
    all_to_all x1, waiting for transfers between devices, on_device(): parts = lax.all_to_all(gram(pa, pb, 16), 'vocab', 0, 0)  6 us
    pallas_call x1, Pallas kernels, first_grad(): pl.pallas_call(functools.partial(first_grad_kernel, seqs, place, followin...  5.15 us
  transfers between devices with their start and end apart: 34, of which 15 were waited for; matrix products, arithmetic and copies ran while one was open for 2% of the time, Pallas kernels for 33%

profile of v4, /device:TPU:0, one launch (start us, length us, event | category | flops | bytes accessed | tf_op | source)
XLA Modules:
  0.0 128.9 jit_solution(5394411318544750838)
XLA Ops:
  0.6 1.0 pad_maximum_fusion.2.refs_0_
  1.7 0.1 collective-permute-start.3
  1.8 3.2 %collective-permute-start = (bf16[768,256]{1,0:T(8,128)(2,1)S(1)}, bf16[768,256]{1,0:T(8,128)(2,1)S(1)}, u32[]{:S(2)}, u32[]{:S(2)}) collective-permute-start(bf16[768,256]{1,0:T(8,128)(2,1)S(1)} %pad_maximum_fusion.2.refs_0_), channel_id=1, source_target_pairs={{0,6},{1,7},{2,0},{3,1},{4,2},{5,3},{6,4},{7,5},{8,14},{9,15},{10,... | collective-permute-start | bytes 1179656 | tf_op jit(solution)/shard_map/ppermute | solution.py:30
  4.9 1.9 %collective-permute-start.2 = (bf16[768,256]{1,0:T(8,128)(2,1)S(1)}, bf16[768,256]{1,0:T(8,128)(2,1)S(1)}, u32[]{:S(2)}, u32[]{:S(2)}) collective-permute-start(bf16[768,256]{1,0:T(8,128)(2,1)S(1)} %pad_maximum_fusion.2.refs_0_), channel_id=1, source_target_pairs={{0,8},{1,9},{2,10},{3,11},{4,12},{5,13},{6,14},{7,15},{8,0},{9,1},... | collective-permute-start | bytes 1179656 | tf_op jit(solution)/shard_map/ppermute | solution.py:34
  6.8 0.7 constant_dynamic-slice_fusion
  7.5 5.3 %logits_part.3.refs_7_ = f32[768,2048]{1,0:T(8,128)S(1)} custom-call(s32[32]{0:T(128)S(1)} %get-tuple-element.105.idx, bf16[768,256]{1,0:T(8,128)(2,1)S(1)} %pad_maximum_fusion.2.refs_0_, bf16[768,256]{1,0:T(8,128)(2,1)S(1)} %collective-permute-done.3.refs_1_, bf16[4096,2048]{1,0:T(8,128)(2,1)} %w.7), custom_call_target="tpu_custom_call" | custom-call | tf_op jit(solution)/shard_map/logits_part/pallas_call | solution.py:165
  12.8 1.1 collective-permute-done.refs_0_
  13.9 3.4 %collective-permute-done.1.refs_2_ = bf16[768,256]{1,0:T(8,128)(2,1)S(1)} collective-permute-done((bf16[768,256]{1,0:T(8,128)(2,1)S(1)}, bf16[768,256]{1,0:T(8,128)(2,1)S(1)}, u32[]{:S(2)}, u32[]{:S(2)}) %collective-permute-start.1) | collective-permute-done | bytes 393248 | tf_op jit(solution)/shard_map/ppermute | solution.py:30
  17.3 0.6 collective-permute-start.9
  17.9 0.1 collective-permute-start.8
  18.2 2.0 %collective-permute-start.4 = (bf16[768,256]{1,0:T(8,128)(2,1)S(1)}, bf16[768,256]{1,0:T(8,128)(2,1)S(1)}, u32[]{:S(2)}, u32[]{:S(2)}) collective-permute-start(bf16[768,256]{1,0:T(8,128)(2,1)S(1)} %get-tuple-element.102), channel_id=1, source_target_pairs={{0,6},{1,7},{2,0},{3,1},{4,2},{5,3},{6,4},{7,5},{8,14},{9,15},{10,... | collective-permute-start | bytes 1179656 | tf_op jit(solution)/shard_map/ppermute | solution.py:30
  20.1 0.1 collective-permute-start.5
  20.3 1.9 %collective-permute-start.6 = (bf16[768,256]{1,0:T(8,128)(2,1)S(1)}, bf16[768,256]{1,0:T(8,128)(2,1)S(1)}, u32[]{:S(2)}, u32[]{:S(2)}) collective-permute-start(bf16[768,256]{1,0:T(8,128)(2,1)S(1)} %get-tuple-element.101), channel_id=1, source_target_pairs={{0,8},{1,9},{2,10},{3,11},{4,12},{5,13},{6,14},{7,15},{8,0},{9,1},... | collective-permute-start | bytes 1179656 | tf_op jit(solution)/shard_map/ppermute | solution.py:34
  22.2 8.2 %logits_part.4.refs_7_ = f32[768,2048]{1,0:T(8,128)S(1)} custom-call(s32[32]{0:T(128)S(1)} %get-tuple-element.105.idx, bf16[768,256]{1,0:T(8,128)(2,1)S(1)} %collective-permute-done.refs_0_, bf16[768,256]{1,0:T(8,128)(2,1)S(1)} %collective-permute-done.7.refs_1_, ...), custom_call_target="tpu_custom_call", output_to_operand_aliasing={{}: (8, {})} | custom-call | tf_op jit(solution)/shard_map/logits_part/pallas_call | solution.py:165
  30.4 2.2 %collective-permute-done.5.refs_2_ = bf16[768,256]{1,0:T(8,128)(2,1)S(1)} collective-permute-done((bf16[768,256]{1,0:T(8,128)(2,1)S(1)}, bf16[768,256]{1,0:T(8,128)(2,1)S(1)}, u32[]{:S(2)}, u32[]{:S(2)}) %collective-permute-start.5) | collective-permute-done | bytes 393248 | tf_op jit(solution)/shard_map/ppermute | solution.py:30
  32.6 0.5 collective-permute-start.13
  33.1 1.8 %collective-permute-start.10 = (bf16[384,256]{1,0:T(8,128)(2,1)S(1)}, bf16[384,256]{1,0:T(8,128)(2,1)S(1)}, u32[]{:S(2)}, u32[]{:S(2)}) collective-permute-start(bf16[384,256]{1,0:T(8,128)(2,1)S(1)} %slice.93), channel_id=1, source_target_pairs={{0,6},{1,7},{2,0},{3,1},{4,2},{5,3},{6,4},{7,5},{8,14},{9,15},{10,... | collective-permute-start | bytes 589832 | tf_op jit(solution)/shard_map/ppermute | solution.py:30
  35.0 1.7 %collective-permute-start.11 = (bf16[384,256]{1,0:T(8,128)(2,1)S(1)}, bf16[384,256]{1,0:T(8,128)(2,1)S(1)}, u32[]{:S(2)}, u32[]{:S(2)}) collective-permute-start(bf16[384,256]{1,0:T(8,128)(2,1)S(1)} %slice.94), channel_id=1, source_target_pairs={{0,8},{1,9},{2,10},{3,11},{4,12},{5,13},{6,14},{7,15},{8,0},{9,1},... | collective-permute-start | bytes 589832 | tf_op jit(solution)/shard_map/ppermute | solution.py:34
  36.7 0.1 fusion.6
  36.9 8.4 %logits_part.5 = (f32[768,2048]{1,0:T(8,128)S(1)}, bf16[512,2048]{1,0:T(8,128)(2,1)S(1)}) custom-call(s32[32]{0:T(128)S(1)} %get-tuple-element.105.idx, bf16[768,256]{1,0:T(8,128)(2,1)S(1)} %collective-permute-done.4.refs_0_, bf16[768,256]{1,0:T(8,128)(2,1)S(1)} %collective-permute-done.12.refs_1_, ...), custom_call_target="tpu_custom_call", output_to_operand_aliasing={{0}: (8, {})} | custom-call | tf_op jit(solution)/shard_map/logits_part/pallas_call | solution.py:165
  45.3 0.1 collective-permute-start.15
  45.4 0.5 collective-permute-start.16
  45.9 0.1 fusion.7
  46.1 0.7 collective-permute-done.15.refs_1_
  46.8 0.3 collective-permute-done.16.refs_3_
  47.1 5.1 %logits_pool.1 = (bf16[768,2048]{1,0:T(8,128)(2,1)}, f32[8,2048]{1,0:T(8,128)S(1)}, f32[4,2048]{1,0:T(4,128)S(1)}) custom-call(s32[4]{0:T(128)S(1)} %pad_add_fusion.lens, bf16[384,256]{1,0:T(8,128)(2,1)S(1)} %collective-permute-done.10.refs_0_, bf16[384,256]{1,0:T(8,128)(2,1)S(1)} %collective-permute-done.15.refs_1_, ...), custom_call_target="tpu_custom_call" | custom-call | tf_op jit(solution)/shard_map/logits_pool/pallas_call | solution.py:234
  52.2 2.8 %collective-permute-start.17 = (f32[4,2048]{1,0:T(4,128)S(1)}, f32[4,2048]{1,0:T(4,128)S(1)}, u32[]{:S(2)}, u32[]{:S(2)}) collective-permute-start(f32[4,2048]{1,0:T(4,128)S(1)} %get-tuple-element.59), channel_id=1, source_target_pairs={{0,96},{16,112},{32,0},{48,16},{64,32},{80,48},{96,64},{112,80},{1... | collective-permute-start | bytes 98312 | tf_op jit(solution)/shard_map/ppermute | solution.py:42
  55.1 0.8 collective-permute-start.18
  55.9 0.9 collective-permute-start.19
  56.8 3.6 %collective-permute-done.18 = f32[4,2048]{1,0:T(4,128)S(1)} collective-permute-done((f32[4,2048]{1,0:T(4,128)S(1)}, f32[4,2048]{1,0:T(4,128)S(1)}, u32[]{:S(2)}, u32[]{:S(2)}) %collective-permute-start.18) | collective-permute-done | bytes 32800 | tf_op jit(solution)/shard_map/ppermute | solution.py:42
  60.5 0.5 collective-permute-done.19
  61.0 3.7 %collective-permute-start.20 = (f32[16,2048]{1,0:T(8,128)S(1)}, f32[16,2048]{1,0:T(8,128)S(1)}, u32[]{:S(2)}, u32[]{:S(2)}) collective-permute-start(f32[16,2048]{1,0:T(8,128)S(1)} %pad_maximum_fusion.7.a.pa), channel_id=1, source_target_pairs={{0,16},{16,0},{32,48},{48,32},{64,80},{80,64},{96,112},{112,96},{1... | collective-permute-start | bytes 393224 | tf_op jit(solution)/shard_map/ppermute | solution.py:46
  64.8 0.7 gather_fusion
  65.4 2.2 %collective-permute-done.20.b.pb = f32[16,2048]{1,0:T(8,128)S(1)} collective-permute-done((f32[16,2048]{1,0:T(8,128)S(1)}, f32[16,2048]{1,0:T(8,128)S(1)}, u32[]{:S(2)}, u32[]{:S(2)}) %collective-permute-start.20) | collective-permute-done | bytes 131104 | tf_op jit(solution)/shard_map/ppermute | solution.py:46
  67.6 1.0 gram.1
  68.6 3.5 %all-to-all-start = ((f32[16,8,128]{2,1,0:T(8,128)}), f32[16,8,128]{2,1,0:T(8,128)S(1)}, u32[]{:S(2)}, u32[]{:S(2)}) async-start(f32[16,8,128]{2,1,0:T(8,128)} %gram.1), calls=%async_computation | async-start | bytes 131072 | tf_op jit(solution)/shard_map/all_to_all | solution.py:491
  72.2 6.0 %all-to-all-done.parts = f32[16,8,128]{2,1,0:T(8,128)S(1)} async-done(((f32[16,8,128]{2,1,0:T(8,128)}), f32[16,8,128]{2,1,0:T(8,128)S(1)}, u32[]{:S(2)}, u32[]{:S(2)}) %all-to-all-start) | async-done | bytes 65568 | tf_op jit(solution)/shard_map/all_to_all | solution.py:491
  78.2 5.2 %first_grad.1 = (bf16[768,2048]{1,0:T(8,128)(2,1)S(1)}, f32[8,128]{1,0:T(8,128)S(1)}, f32[768,256]{1,0:T(8,128)S(1)}, bf16[768,256]{1,0:T(8,128)(2,1)S(1)}, bf16[512,2048]{1,0:T(8,128)(2,1)S(1)}) custom-call(s32[32]{0:T(128)S(1)} %get-tuple-element.105.idx, f32[16,8,128]{2,1,0:T(8,128)S(1)} %all-to-all-done.parts, f32[16,2048]{1,0:T(8,128)S(1)} %pad_maximum_fusion.7.a.pa, ...), custom_call_target="tpu_custom_call" | custom-call | tf_op jit(solution)/shard_map/first_grad/pallas_call | solution.py:343
  83.4 0.2 collective-permute-start.21
  83.6 1.6 %collective-permute-done.21 = bf16[768,256]{1,0:T(8,128)(2,1)S(1)} collective-permute-done((bf16[768,256]{1,0:T(8,128)(2,1)S(1)}, bf16[768,256]{1,0:T(8,128)(2,1)S(1)}, u32[]{:S(2)}, u32[]{:S(2)}) %collective-permute-start.21) | collective-permute-done | bytes 393248 | tf_op jit(solution)/shard_map/ppermute | solution.py:38
  85.2 0.1 add_convert_fusion
  85.3 0.7 collective-permute-start.22
  86.0 0.7 collective-permute-start.23
  86.6 7.5 %grad_part.3 = (f32[2304,256]{1,0:T(8,128)S(1)}, bf16[2304,256]{1,0:T(8,128)(2,1)S(1)}) custom-call(s32[32]{0:T(128)S(1)} %get-tuple-element.105.idx, bf16[768,2048]{1,0:T(8,128)(2,1)S(1)} %get-tuple-element.76.dl, bf16[4096,2048]{1,0:T(8,128)(2,1)} %w.7, bf16[512,2048]{1,0:T(8,128)(2,1)S(1)} %get-tuple-element.67.refs_0_), custom_call_target="tpu_custom_call" | custom-call | tf_op jit(solution)/shard_map/grad_part/pallas_call | solution.py:390
  94.1 0.1 collective-permute-start.24
  94.2 0.2 add_arrived.3
  94.5 2.6 %collective-permute-done.24 = bf16[2304,256]{1,0:T(8,128)(2,1)S(1)} collective-permute-done((bf16[2304,256]{1,0:T(8,128)(2,1)S(1)}, bf16[2304,256]{1,0:T(8,128)(2,1)S(1)}, u32[]{:S(2)}, u32[]{:S(2)}) %collective-permute-start.24) | collective-permute-done | bytes 1179680 | tf_op jit(solution)/shard_map/ppermute | solution.py:38
  97.1 0.4 fusion.3
  97.7 0.7 collective-permute-start.25
  98.3 2.6 %collective-permute-start.26 = (bf16[768,256]{1,0:T(8,128)(2,1)S(1)}, bf16[768,256]{1,0:T(8,128)(2,1)S(1)}, u32[]{:S(2)}, u32[]{:S(2)}) collective-permute-start(bf16[768,256]{1,0:T(8,128)(2,1)S(1)} %pad_maximum_fusion.5), channel_id=1, source_target_pairs={{0,6},{1,7},{2,0},{3,1},{4,2},{5,3},{6,4},{7,5},{8,14},{9,15},{10,... | collective-permute-start | bytes 1179656 | tf_op jit(solution)/shard_map/ppermute | solution.py:30
  101.0 1.4 %collective-permute-start.27 = (bf16[768,256]{1,0:T(8,128)(2,1)S(1)}, bf16[768,256]{1,0:T(8,128)(2,1)S(1)}, u32[]{:S(2)}, u32[]{:S(2)}) collective-permute-start(bf16[768,256]{1,0:T(8,128)(2,1)S(1)} %pad_maximum_fusion.6), channel_id=1, source_target_pairs={{0,8},{1,9},{2,10},{3,11},{4,12},{5,13},{6,14},{7,15},{8,0},{9,1},... | collective-permute-start | bytes 1179656 | tf_op jit(solution)/shard_map/ppermute | solution.py:34
  102.3 8.3 %grad_part.4 = (f32[2304,256]{1,0:T(8,128)S(1)}, bf16[2304,256]{1,0:T(8,128)(2,1)S(1)}) custom-call(s32[32]{0:T(128)S(1)} %get-tuple-element.105.idx, bf16[768,2048]{1,0:T(8,128)(2,1)S(1)} %get-tuple-element.76.dl, bf16[4096,2048]{1,0:T(8,128)(2,1)} %w.7), custom_call_target="tpu_custom_call" | custom-call | tf_op jit(solution)/shard_map/grad_part/pallas_call | solution.py:390
  110.7 0.8 collective-permute-done.27.refs_3_
  111.6 0.4 add_arrived.4
  112.0 1.6 %collective-permute-done.28 = bf16[2304,256]{1,0:T(8,128)(2,1)S(1)} collective-permute-done((bf16[2304,256]{1,0:T(8,128)(2,1)S(1)}, bf16[2304,256]{1,0:T(8,128)(2,1)S(1)}, u32[]{:S(2)}, u32[]{:S(2)}) %collective-permute-start.28) | collective-permute-done | bytes 1179680 | tf_op jit(solution)/shard_map/ppermute | solution.py:38
  113.6 0.3 fusion
  114.0 3.2 %collective-permute-start.30 = (bf16[768,256]{1,0:T(8,128)(2,1)S(1)}, bf16[768,256]{1,0:T(8,128)(2,1)S(1)}, u32[]{:S(2)}, u32[]{:S(2)}) collective-permute-start(bf16[768,256]{1,0:T(8,128)(2,1)S(1)} %get-tuple-element.79), channel_id=1, source_target_pairs={{0,6},{1,7},{2,0},{3,1},{4,2},{5,3},{6,4},{7,5},{8,14},{9,15},{10,... | collective-permute-start | bytes 1179656 | tf_op jit(solution)/shard_map/ppermute | solution.py:30
  117.2 0.7 collective-permute-start.31
  117.8 0.6 slice_reduce_fusion
  118.5 4.1 %grad_part.5 = (f32[768,256]{1,0:T(8,128)S(1)}, bf16[768,256]{1,0:T(8,128)(2,1)S(1)}) custom-call(s32[32]{0:T(128)S(1)} %get-tuple-element.105.idx, bf16[768,2048]{1,0:T(8,128)(2,1)S(1)} %get-tuple-element.76.dl, bf16[4096,2048]{1,0:T(8,128)(2,1)} %w.7), custom_call_target="tpu_custom_call" | custom-call | tf_op jit(solution)/shard_map/grad_part/pallas_call | solution.py:390
  122.6 3.7 %collective-permute-done.29.refs_1_ = bf16[768,256]{1,0:T(8,128)(2,1)S(1)} collective-permute-done((bf16[768,256]{1,0:T(8,128)(2,1)S(1)}, bf16[768,256]{1,0:T(8,128)(2,1)S(1)}, u32[]{:S(2)}, u32[]{:S(2)}) %collective-permute-start.29) | collective-permute-done | bytes 393248 | tf_op jit(solution)/shard_map/ppermute | solution.py:30
  126.3 1.5 %collective-permute-done.31.refs_3_ = bf16[768,256]{1,0:T(8,128)(2,1)S(1)} collective-permute-done((bf16[768,256]{1,0:T(8,128)(2,1)S(1)}, bf16[768,256]{1,0:T(8,128)(2,1)S(1)}, u32[]{:S(2)}, u32[]{:S(2)}) %collective-permute-start.31) | collective-permute-done | bytes 393248 | tf_op jit(solution)/shard_map/ppermute | solution.py:34
  127.8 0.3 add_arrived.5.refs_0_
  128.1 0.8 add_last.1
  (52 shorter events, 1.0 us)
Async XLA Ops:
  0.6 64.1 %copy-start = (s32[16]{0:T(128)S(1)}, s32[16]{0:T(128)}, u32[]{:S(2)}) copy-start(s32[16]{0:T(128)} %param.12) | copy-start | bytes 196
  1.7 5.9 %collective-permute-start.3 = (bf16[768,256]{1,0:T(8,128)(2,1)S(1)}, bf16[768,256]{1,0:T(8,128)(2,1)S(1)}, u32[]{:S(2)}, u32[]{:S(2)}) collective-permute-start(bf16[768,256]{1,0:T(8,128)(2,1)S(1)} %pad_maximum_fusion.2.refs_0_), channel_id=1, source_target_pairs={{0,1},{1,0},{2,3},{3,2},{4,5},{5,4},{6,7},{7,6},{8,9},{9,8},{10,11... | collective-permute-start | bytes 1179656 | tf_op jit(solution)/shard_map/ppermute | solution.py:38
  1.8 12.1 %collective-permute-start = (bf16[768,256]{1,0:T(8,128)(2,1)S(1)}, bf16[768,256]{1,0:T(8,128)(2,1)S(1)}, u32[]{:S(2)}, u32[]{:S(2)}) collective-permute-start(bf16[768,256]{1,0:T(8,128)(2,1)S(1)} %pad_maximum_fusion.2.refs_0_), channel_id=1, source_target_pairs={{0,6},{1,7},{2,0},{3,1},{4,2},{5,3},{6,4},{7,5},{8,14},{9,15},{10,... | collective-permute-start | bytes 1179656 | tf_op jit(solution)/shard_map/ppermute | solution.py:30
  4.9 12.4 %collective-permute-start.1 = (bf16[768,256]{1,0:T(8,128)(2,1)S(1)}, bf16[768,256]{1,0:T(8,128)(2,1)S(1)}, u32[]{:S(2)}, u32[]{:S(2)}) collective-permute-start(bf16[768,256]{1,0:T(8,128)(2,1)S(1)} %pad_maximum_fusion.2.refs_0_), channel_id=1, source_target_pairs={{0,2},{1,3},{2,4},{3,5},{4,6},{5,7},{6,0},{7,1},{8,10},{9,11},{10,... | collective-permute-start | bytes 1179656 | tf_op jit(solution)/shard_map/ppermute | solution.py:30
  4.9 12.4 %collective-permute-start.2 = (bf16[768,256]{1,0:T(8,128)(2,1)S(1)}, bf16[768,256]{1,0:T(8,128)(2,1)S(1)}, u32[]{:S(2)}, u32[]{:S(2)}) collective-permute-start(bf16[768,256]{1,0:T(8,128)(2,1)S(1)} %pad_maximum_fusion.2.refs_0_), channel_id=1, source_target_pairs={{0,8},{1,9},{2,10},{3,11},{4,12},{5,13},{6,14},{7,15},{8,0},{9,1},... | collective-permute-start | bytes 1179656 | tf_op jit(solution)/shard_map/ppermute | solution.py:34
  17.3 2.9 %collective-permute-start.7 = (bf16[768,256]{1,0:T(8,128)(2,1)S(1)}, bf16[768,256]{1,0:T(8,128)(2,1)S(1)}, u32[]{:S(2)}, u32[]{:S(2)}) collective-permute-start(bf16[768,256]{1,0:T(8,128)(2,1)S(1)} %collective-permute-done.refs_0_), channel_id=1, source_target_pairs={{0,1},{1,0},{2,3},{3,2},{4,5},{5,4},{6,7},{7,6},{8,9},{9,8},{10,11... | collective-permute-start | bytes 1179656 | tf_op jit(solution)/shard_map/ppermute | solution.py:38
  17.3 4.8 %collective-permute-start.9 = (bf16[768,256]{1,0:T(8,128)(2,1)S(1)}, bf16[768,256]{1,0:T(8,128)(2,1)S(1)}, u32[]{:S(2)}, u32[]{:S(2)}) collective-permute-start(bf16[768,256]{1,0:T(8,128)(2,1)S(1)} %collective-permute-done.2.refs_4_), channel_id=1, source_target_pairs={{0,1},{1,0},{2,3},{3,2},{4,5},{5,4},{6,7},{7,6},{8,9},{9,8},{10,11... | collective-permute-start | bytes 1179656 | tf_op jit(solution)/shard_map/ppermute | solution.py:38
  17.9 4.2 %collective-permute-start.8 = (bf16[768,256]{1,0:T(8,128)(2,1)S(1)}, bf16[768,256]{1,0:T(8,128)(2,1)S(1)}, u32[]{:S(2)}, u32[]{:S(2)}) collective-permute-start(bf16[768,256]{1,0:T(8,128)(2,1)S(1)} %collective-permute-done.1.refs_2_), channel_id=1, source_target_pairs={{0,1},{1,0},{2,3},{3,2},{4,5},{5,4},{6,7},{7,6},{8,9},{9,8},{10,11... | collective-permute-start | bytes 1179656 | tf_op jit(solution)/shard_map/ppermute | solution.py:38
  18.2 12.2 %collective-permute-start.4 = (bf16[768,256]{1,0:T(8,128)(2,1)S(1)}, bf16[768,256]{1,0:T(8,128)(2,1)S(1)}, u32[]{:S(2)}, u32[]{:S(2)}) collective-permute-start(bf16[768,256]{1,0:T(8,128)(2,1)S(1)} %get-tuple-element.102), channel_id=1, source_target_pairs={{0,6},{1,7},{2,0},{3,1},{4,2},{5,3},{6,4},{7,5},{8,14},{9,15},{10,... | collective-permute-start | bytes 1179656 | tf_op jit(solution)/shard_map/ppermute | solution.py:30
  20.1 12.4 %collective-permute-start.5 = (bf16[768,256]{1,0:T(8,128)(2,1)S(1)}, bf16[768,256]{1,0:T(8,128)(2,1)S(1)}, u32[]{:S(2)}, u32[]{:S(2)}) collective-permute-start(bf16[768,256]{1,0:T(8,128)(2,1)S(1)} %get-tuple-element.103), channel_id=1, source_target_pairs={{0,2},{1,3},{2,4},{3,5},{4,6},{5,7},{6,0},{7,1},{8,10},{9,11},{10,... | collective-permute-start | bytes 1179656 | tf_op jit(solution)/shard_map/ppermute | solution.py:30
  20.3 16.4 %copy-start.2 = (s32[2,256]{1,0:T(2,128)S(1)}, s32[2,256]{1,0:T(2,128)}, u32[]{:S(2)}) copy-start(s32[2,256]{1,0:T(2,128)} %param.11) | copy-start | bytes 6148
  20.3 12.3 %collective-permute-start.6 = (bf16[768,256]{1,0:T(8,128)(2,1)S(1)}, bf16[768,256]{1,0:T(8,128)(2,1)S(1)}, u32[]{:S(2)}, u32[]{:S(2)}) collective-permute-start(bf16[768,256]{1,0:T(8,128)(2,1)S(1)} %get-tuple-element.101), channel_id=1, source_target_pairs={{0,8},{1,9},{2,10},{3,11},{4,12},{5,13},{6,14},{7,15},{8,0},{9,1},... | collective-permute-start | bytes 1179656 | tf_op jit(solution)/shard_map/ppermute | solution.py:34
  32.6 4.2 %collective-permute-start.12 = (bf16[768,256]{1,0:T(8,128)(2,1)S(1)}, bf16[768,256]{1,0:T(8,128)(2,1)S(1)}, u32[]{:S(2)}, u32[]{:S(2)}) collective-permute-start(bf16[768,256]{1,0:T(8,128)(2,1)S(1)} %collective-permute-done.4.refs_0_), channel_id=1, source_target_pairs={{0,1},{1,0},{2,3},{3,2},{4,5},{5,4},{6,7},{7,6},{8,9},{9,8},{10,11... | collective-permute-start | bytes 1179656 | tf_op jit(solution)/shard_map/ppermute | solution.py:38
  32.6 4.2 %collective-permute-start.13 = (bf16[768,256]{1,0:T(8,128)(2,1)S(1)}, bf16[768,256]{1,0:T(8,128)(2,1)S(1)}, u32[]{:S(2)}, u32[]{:S(2)}) collective-permute-start(bf16[768,256]{1,0:T(8,128)(2,1)S(1)} %collective-permute-done.5.refs_2_), channel_id=1, source_target_pairs={{0,1},{1,0},{2,3},{3,2},{4,5},{5,4},{6,7},{7,6},{8,9},{9,8},{10,11... | collective-permute-start | bytes 1179656 | tf_op jit(solution)/shard_map/ppermute | solution.py:38
  33.1 3.8 %collective-permute-start.14 = (bf16[768,256]{1,0:T(8,128)(2,1)S(1)}, bf16[768,256]{1,0:T(8,128)(2,1)S(1)}, u32[]{:S(2)}, u32[]{:S(2)}) collective-permute-start(bf16[768,256]{1,0:T(8,128)(2,1)S(1)} %collective-permute-done.6.refs_4_), channel_id=1, source_target_pairs={{0,1},{1,0},{2,3},{3,2},{4,5},{5,4},{6,7},{7,6},{8,9},{9,8},{10,11... | collective-permute-start | bytes 1179656 | tf_op jit(solution)/shard_map/ppermute | solution.py:38
  33.1 12.1 %collective-permute-start.10 = (bf16[384,256]{1,0:T(8,128)(2,1)S(1)}, bf16[384,256]{1,0:T(8,128)(2,1)S(1)}, u32[]{:S(2)}, u32[]{:S(2)}) collective-permute-start(bf16[384,256]{1,0:T(8,128)(2,1)S(1)} %slice.93), channel_id=1, source_target_pairs={{0,6},{1,7},{2,0},{3,1},{4,2},{5,3},{6,4},{7,5},{8,14},{9,15},{10,... | collective-permute-start | bytes 589832 | tf_op jit(solution)/shard_map/ppermute | solution.py:30
  35.0 10.3 %collective-permute-start.11 = (bf16[384,256]{1,0:T(8,128)(2,1)S(1)}, bf16[384,256]{1,0:T(8,128)(2,1)S(1)}, u32[]{:S(2)}, u32[]{:S(2)}) collective-permute-start(bf16[384,256]{1,0:T(8,128)(2,1)S(1)} %slice.94), channel_id=1, source_target_pairs={{0,8},{1,9},{2,10},{3,11},{4,12},{5,13},{6,14},{7,15},{8,0},{9,1},... | collective-permute-start | bytes 589832 | tf_op jit(solution)/shard_map/ppermute | solution.py:34
  36.8 9.1 %copy-start.3 = (s32[2,128]{1,0:T(2,128)S(1)}, s32[2,128]{1,0:T(2,128)}, u32[]{:S(2)}) copy-start(s32[2,128]{1,0:T(2,128)} %param.10) | copy-start | bytes 3076
  45.3 1.5 %collective-permute-start.15 = (bf16[384,256]{1,0:T(8,128)(2,1)S(1)}, bf16[384,256]{1,0:T(8,128)(2,1)S(1)}, u32[]{:S(2)}, u32[]{:S(2)}) collective-permute-start(bf16[384,256]{1,0:T(8,128)(2,1)S(1)} %collective-permute-done.10.refs_0_), channel_id=1, source_target_pairs={{0,1},{1,0},{2,3},{3,2},{4,5},{5,4},{6,7},{7,6},{8,9},{9,8},{10,11... | collective-permute-start | bytes 589832 | tf_op jit(solution)/shard_map/ppermute | solution.py:38
  45.4 1.7 %collective-permute-start.16 = (bf16[384,256]{1,0:T(8,128)(2,1)S(1)}, bf16[384,256]{1,0:T(8,128)(2,1)S(1)}, u32[]{:S(2)}, u32[]{:S(2)}) collective-permute-start(bf16[384,256]{1,0:T(8,128)(2,1)S(1)} %collective-permute-done.11.refs_2_), channel_id=1, source_target_pairs={{0,1},{1,0},{2,3},{3,2},{4,5},{5,4},{6,7},{7,6},{8,9},{9,8},{10,11... | collective-permute-start | bytes 589832 | tf_op jit(solution)/shard_map/ppermute | solution.py:38
  52.2 4.6 %collective-permute-start.17 = (f32[4,2048]{1,0:T(4,128)S(1)}, f32[4,2048]{1,0:T(4,128)S(1)}, u32[]{:S(2)}, u32[]{:S(2)}) collective-permute-start(f32[4,2048]{1,0:T(4,128)S(1)} %get-tuple-element.59), channel_id=1, source_target_pairs={{0,96},{16,112},{32,0},{48,16},{64,32},{80,48},{96,64},{112,80},{1... | collective-permute-start | bytes 98312 | tf_op jit(solution)/shard_map/ppermute | solution.py:42
  55.1 5.4 %collective-permute-start.18 = (f32[4,2048]{1,0:T(4,128)S(1)}, f32[4,2048]{1,0:T(4,128)S(1)}, u32[]{:S(2)}, u32[]{:S(2)}) collective-permute-start(f32[4,2048]{1,0:T(4,128)S(1)} %get-tuple-element.59), channel_id=1, source_target_pairs={{0,64},{16,80},{32,96},{48,112},{64,0},{80,16},{96,32},{112,48},{1... | collective-permute-start | bytes 98312 | tf_op jit(solution)/shard_map/ppermute | solution.py:42
  55.9 5.1 %collective-permute-start.19 = (f32[4,2048]{1,0:T(4,128)S(1)}, f32[4,2048]{1,0:T(4,128)S(1)}, u32[]{:S(2)}, u32[]{:S(2)}) collective-permute-start(f32[4,2048]{1,0:T(4,128)S(1)} %get-tuple-element.59), channel_id=1, source_target_pairs={{0,32},{16,48},{32,64},{48,80},{64,96},{80,112},{96,0},{112,16},{1... | collective-permute-start | bytes 98312 | tf_op jit(solution)/shard_map/ppermute | solution.py:42
  61.0 6.6 %collective-permute-start.20 = (f32[16,2048]{1,0:T(8,128)S(1)}, f32[16,2048]{1,0:T(8,128)S(1)}, u32[]{:S(2)}, u32[]{:S(2)}) collective-permute-start(f32[16,2048]{1,0:T(8,128)S(1)} %pad_maximum_fusion.7.a.pa), channel_id=1, source_target_pairs={{0,16},{16,0},{32,48},{48,32},{64,80},{80,64},{96,112},{112,96},{1... | collective-permute-start | bytes 393224 | tf_op jit(solution)/shard_map/ppermute | solution.py:46
  68.6 9.6 %all-to-all-start = ((f32[16,8,128]{2,1,0:T(8,128)}), f32[16,8,128]{2,1,0:T(8,128)S(1)}, u32[]{:S(2)}, u32[]{:S(2)}) async-start(f32[16,8,128]{2,1,0:T(8,128)} %gram.1), calls=%async_computation | async-start | bytes 131072 | tf_op jit(solution)/shard_map/all_to_all | solution.py:491
  83.4 1.8 %collective-permute-start.21 = (bf16[768,256]{1,0:T(8,128)(2,1)S(1)}, bf16[768,256]{1,0:T(8,128)(2,1)S(1)}, u32[]{:S(2)}, u32[]{:S(2)}) collective-permute-start(bf16[768,256]{1,0:T(8,128)(2,1)S(1)} %get-tuple-element.65), channel_id=1, source_target_pairs={{0,1},{1,0},{2,3},{3,2},{4,5},{5,4},{6,7},{7,6},{8,9},{9,8},{10,11... | collective-permute-start | bytes 1179656 | tf_op jit(solution)/shard_map/ppermute | solution.py:38
  85.3 8.9 %collective-permute-start.22 = (bf16[384,256]{1,0:T(8,128)(2,1)S(1)}, bf16[384,256]{1,0:T(8,128)(2,1)S(1)}, u32[]{:S(2)}, u32[]{:S(2)}) collective-permute-start(bf16[384,256]{1,0:T(8,128)(2,1)S(1)} %get-tuple-element.98), channel_id=1, source_target_pairs={{0,2},{1,3},{2,4},{3,5},{4,6},{5,7},{6,0},{7,1},{8,10},{9,11},{10,... | collective-permute-start | bytes 589832 | tf_op jit(solution)/shard_map/ppermute | solution.py:30
  86.0 8.3 %collective-permute-start.23 = (bf16[384,256]{1,0:T(8,128)(2,1)S(1)}, bf16[384,256]{1,0:T(8,128)(2,1)S(1)}, u32[]{:S(2)}, u32[]{:S(2)}) collective-permute-start(bf16[384,256]{1,0:T(8,128)(2,1)S(1)} %get-tuple-element.97), channel_id=1, source_target_pairs={{0,8},{1,9},{2,10},{3,11},{4,12},{5,13},{6,14},{7,15},{8,0},{9,1},... | collective-permute-start | bytes 589832 | tf_op jit(solution)/shard_map/ppermute | solution.py:34
  94.1 2.9 %collective-permute-start.24 = (bf16[2304,256]{1,0:T(8,128)(2,1)S(1)}, bf16[2304,256]{1,0:T(8,128)(2,1)S(1)}, u32[]{:S(2)}, u32[]{:S(2)}) collective-permute-start(bf16[2304,256]{1,0:T(8,128)(2,1)S(1)} %get-tuple-element.69), channel_id=1, source_target_pairs={{0,1},{1,0},{2,3},{3,2},{4,5},{5,4},{6,7},{7,6},{8,9},{9,8},{10,11... | collective-permute-start | bytes 3538952 | tf_op jit(solution)/shard_map/ppermute | solution.py:38
  97.7 13.1 %collective-permute-start.25 = (bf16[768,256]{1,0:T(8,128)(2,1)S(1)}, bf16[768,256]{1,0:T(8,128)(2,1)S(1)}, u32[]{:S(2)}, u32[]{:S(2)}) collective-permute-start(bf16[768,256]{1,0:T(8,128)(2,1)S(1)} %pad_maximum_fusion.4), channel_id=1, source_target_pairs={{0,2},{1,3},{2,4},{3,5},{4,6},{5,7},{6,0},{7,1},{8,10},{9,11},{10,... | collective-permute-start | bytes 1179656 | tf_op jit(solution)/shard_map/ppermute | solution.py:30
  98.3 12.4 %collective-permute-start.26 = (bf16[768,256]{1,0:T(8,128)(2,1)S(1)}, bf16[768,256]{1,0:T(8,128)(2,1)S(1)}, u32[]{:S(2)}, u32[]{:S(2)}) collective-permute-start(bf16[768,256]{1,0:T(8,128)(2,1)S(1)} %pad_maximum_fusion.5), channel_id=1, source_target_pairs={{0,6},{1,7},{2,0},{3,1},{4,2},{5,3},{6,4},{7,5},{8,14},{9,15},{10,... | collective-permute-start | bytes 1179656 | tf_op jit(solution)/shard_map/ppermute | solution.py:30
  101.0 10.6 %collective-permute-start.27 = (bf16[768,256]{1,0:T(8,128)(2,1)S(1)}, bf16[768,256]{1,0:T(8,128)(2,1)S(1)}, u32[]{:S(2)}, u32[]{:S(2)}) collective-permute-start(bf16[768,256]{1,0:T(8,128)(2,1)S(1)} %pad_maximum_fusion.6), channel_id=1, source_target_pairs={{0,8},{1,9},{2,10},{3,11},{4,12},{5,13},{6,14},{7,15},{8,0},{9,1},... | collective-permute-start | bytes 1179656 | tf_op jit(solution)/shard_map/ppermute | solution.py:34
  110.6 2.9 %collective-permute-start.28 = (bf16[2304,256]{1,0:T(8,128)(2,1)S(1)}, bf16[2304,256]{1,0:T(8,128)(2,1)S(1)}, u32[]{:S(2)}, u32[]{:S(2)}) collective-permute-start(bf16[2304,256]{1,0:T(8,128)(2,1)S(1)} %get-tuple-element.75), channel_id=1, source_target_pairs={{0,1},{1,0},{2,3},{3,2},{4,5},{5,4},{6,7},{7,6},{8,9},{9,8},{10,11... | collective-permute-start | bytes 3538952 | tf_op jit(solution)/shard_map/ppermute | solution.py:38
  113.9 12.4 %collective-permute-start.29 = (bf16[768,256]{1,0:T(8,128)(2,1)S(1)}, bf16[768,256]{1,0:T(8,128)(2,1)S(1)}, u32[]{:S(2)}, u32[]{:S(2)}) collective-permute-start(bf16[768,256]{1,0:T(8,128)(2,1)S(1)} %get-tuple-element.78), channel_id=1, source_target_pairs={{0,2},{1,3},{2,4},{3,5},{4,6},{5,7},{6,0},{7,1},{8,10},{9,11},{10,... | collective-permute-start | bytes 1179656 | tf_op jit(solution)/shard_map/ppermute | solution.py:30
  114.0 12.4 %collective-permute-start.30 = (bf16[768,256]{1,0:T(8,128)(2,1)S(1)}, bf16[768,256]{1,0:T(8,128)(2,1)S(1)}, u32[]{:S(2)}, u32[]{:S(2)}) collective-permute-start(bf16[768,256]{1,0:T(8,128)(2,1)S(1)} %get-tuple-element.79), channel_id=1, source_target_pairs={{0,6},{1,7},{2,0},{3,1},{4,2},{5,3},{6,4},{7,5},{8,14},{9,15},{10,... | collective-permute-start | bytes 1179656 | tf_op jit(solution)/shard_map/ppermute | solution.py:30
  117.2 10.6 %collective-permute-start.31 = (bf16[768,256]{1,0:T(8,128)(2,1)S(1)}, bf16[768,256]{1,0:T(8,128)(2,1)S(1)}, u32[]{:S(2)}, u32[]{:S(2)}) collective-permute-start(bf16[768,256]{1,0:T(8,128)(2,1)S(1)} %get-tuple-element.80), channel_id=1, source_target_pairs={{0,8},{1,9},{2,10},{3,11},{4,12},{5,13},{6,14},{7,15},{8,0},{9,1},... | collective-permute-start | bytes 1179656 | tf_op jit(solution)/shard_map/ppermute | solution.py:34
  122.5 5.5 %collective-permute-start.32 = (bf16[768,256]{1,0:T(8,128)(2,1)S(1)}, bf16[768,256]{1,0:T(8,128)(2,1)S(1)}, u32[]{:S(2)}, u32[]{:S(2)}) collective-permute-start(bf16[768,256]{1,0:T(8,128)(2,1)S(1)} %get-tuple-element.81), channel_id=1, source_target_pairs={{0,1},{1,0},{2,3},{3,2},{4,5},{5,4},{6,7},{7,6},{8,9},{9,8},{10,11... | collective-permute-start | bytes 1179656 | tf_op jit(solution)/shard_map/ppermute | solution.py:38
  127.8 1.1 copy-start.1

commit v5 on v4

--- a/solution.py
+++ b/solution.py
@@ -362,9 +362,10 @@
     )(idx, parts, pa, pb, stats, picked, pltpu.with_memory_space_constraint(expo, pltpu.HBM), w)
 
 
-def grad_kernel(first, n, has_ahead, idx, dl, w, *refs):
+def grad_kernel(first, n, has_ahead, following, idx, dl, w, *refs):
     ahead = refs[0] if has_ahead else None
-    mine, sib, ws, wsem = refs[has_ahead:]
+    mine, sib = refs[has_ahead : has_ahead + 2]
+    ws, wsem = refs[-2:]
 
     def w_copy(step):
         row = pl.multiple_of(idx[first + step] * (2 * BLK), 2 * BLK)
@@ -372,6 +373,10 @@
 
     for i in range(has_ahead, n):
         w_copy(i).start()
+    if following is not None:
+        row = pl.multiple_of(idx[following] * (2 * BLK), 2 * BLK)
+        later = pltpu.make_async_copy(w.at[pl.ds(row, 2 * BLK), :], refs[has_ahead + 2], wsem.at[n - has_ahead])
+        later.start()
     rows = dl.shape[0]
     for i in range(n):
         here = pl.ds(i * rows, rows)
@@ -381,18 +386,25 @@
             w_copy(i).wait()
             block = ws[i - has_ahead]
         store_halves(idx[8], nt_dot(dl[...], block), mine.at[here], sib.at[here])
-
-
-def grad_part(first, n, idx, dl, w, ahead=None):
+    if following is not None:
+        later.wait()
+
+
+def grad_part(first, n, idx, dl, w, ahead=None, following=None):
     rows, cols = dl.shape
     vm = pl.BlockSpec(memory_space=pltpu.VMEM)
     has = 0 if ahead is None else 1
-    return pl.pallas_call(
-        functools.partial(grad_kernel, first, n, has),
+    more = 0 if following is None else 1
+    return pl.pallas_call(
+        functools.partial(grad_kernel, first, n, has, following),
         in_specs=[pl.BlockSpec(memory_space=pltpu.SMEM), vm, HBM_SPEC] + [vm] * has,
-        out_specs=[vm, vm],
-        scratch_shapes=[pltpu.VMEM((n - has, 2 * BLK, cols), BF), pltpu.SemaphoreType.DMA((n - has,))],
-        out_shape=[jax.ShapeDtypeStruct((n * rows, BLK), F32), jax.ShapeDtypeStruct((n * rows, BLK), BF)],
+        out_specs=[vm] * (2 + more),
+        scratch_shapes=[
+            pltpu.VMEM((max(n - has, 1), 2 * BLK, cols), BF),
+            pltpu.SemaphoreType.DMA((max(n - has + more, 1),)),
+        ],
+        out_shape=[jax.ShapeDtypeStruct((n * rows, BLK), F32), jax.ShapeDtypeStruct((n * rows, BLK), BF)]
+        + [jax.ShapeDtypeStruct((2 * BLK, cols), BF)] * more,
         compiler_params=pltpu.CompilerParams(vmem_limit_bytes=16 * MIB),
         name="grad_part",
     )(idx, dl, w, *([ahead] if has else []))
@@ -500,7 +512,7 @@
         return x[768 * i : 768 * (i + 1)]
 
     r1, r2 = to_y(t21[:h], 1), to_z(t21[h:])
-    mb, sb = grad_part(4, 3, idx, after(dl, t21), w, ahead)
+    mb, sb, ahead = grad_part(4, 3, idx, after(dl, t21), w, ahead, 1)
     sb = to_core(sb)
     (mb,) = add_arrived((mb,), (r1, r2), ((0, 0, 0, 768, h), (0, 1, 0, h, h)))
     t20, t11, tm1 = ((rows(mb, i) + rows(sb, i)).astype(BF) for i in range(3))
@@ -509,7 +521,7 @@
     c3 = jnp.concatenate([t11[:h], tm1[:h]], axis=0)
     c1, c2, c3, dl = lax.optimization_barrier((c1, c2, c3, dl))
     u1, u2, u3 = to_y(c1, 1), to_y(c2, -1), to_z(c3)
-    mc, sc = grad_part(1, 3, idx, dl, w)
+    mc, sc, ahead = grad_part(1, 3, idx, dl, w, ahead, 0)
     sc = to_core(sc)
     (mc,) = add_arrived(
         (mc,),
@@ -526,7 +538,7 @@
     t10, tm0, t01 = ((rows(mc, i) + rows(sc, i)).astype(BF) for i in range(3))
     t10, tm0, t01, dl = lax.optimization_barrier((t10, tm0, t01, dl))
     v1, v2, v3 = to_y(t10, 1), to_y(tm0, -1), to_z(t01)
-    md, sd = grad_part(0, 1, idx, dl, w)
+    md, sd = grad_part(0, 1, idx, dl, w, ahead)
     (md,) = add_arrived((md,), (v1, v2, v3), tuple((0, i, 0, 0, 768) for i in range(3)))
     out_q, out_p = add_last(md, (to_core(sd),), split)
     return (

time: 129 us -> 127 us (0.984)
  Pallas kernels: 54.6 us -> 50.5 us
    pallas_call x3, Pallas kernels: 19.8 us -> 15.7 us  [grad_part(): pl.pallas_call(functools.partial(grad_kernel, first, n, has, following),...]
    ppermute x10, waiting for transfers between devices: 10.4 us -> 12.5 us  [to_y(): return lax.ppermute(x, 'vocab', y_perm(k % 4))]
    ppermute x13, waiting for transfers between devices: 6.84 us -> 5.02 us  [to_core(): return lax.ppermute(x, 'vocab', CORE_SWAP)]
  transfers between devices with their start and end apart: 34 -> 34, of which waited for: 15 -> 17; matrix products, arithmetic and copies ran while one was open for 2% -> 2% of each run, Pallas kernels for 33% -> 30%
where the time goes in v5:
time: 127 us; the launch traced here: 126 us
  Pallas kernels  50.5 us (40%)
  starting transfers between devices  37.2 us (29%)
  waiting for transfers between devices  32.9 us (26%)
  other arithmetic  2.45 us (2%)
  local copies, waits for them, and re-layouts  2.26 us (2%)
    pallas_call x3, Pallas kernels, logits_part(): pl.pallas_call(functools.partial(logits_kernel, copies, places, len(array...  21.9 us
    pallas_call x3, Pallas kernels, grad_part(): pl.pallas_call(functools.partial(grad_kernel, first, n, has, following),...  15.7 us
    ppermute x10, starting transfers between devices, to_y(): return lax.ppermute(x, 'vocab', y_perm(k % 4))  14.3 us
    ppermute x10, waiting for transfers between devices, to_y(): return lax.ppermute(x, 'vocab', y_perm(k % 4))  12.5 us
    ppermute x6, starting transfers between devices, to_z(): return lax.ppermute(x, 'vocab', Z_SWAP)  8.92 us
    all_to_all x1, waiting for transfers between devices, on_device(): parts = lax.all_to_all(gram(pa, pb, 16), 'vocab', 0, 0)  6 us
    pallas_call x1, Pallas kernels, first_grad(): pl.pallas_call(functools.partial(first_grad_kernel, seqs, place, followin...  5.19 us
    pallas_call x1, Pallas kernels, logits_pool(): pl.pallas_call(functools.partial(pool_kernel, copies, len(arrays), bn, se...  5.12 us
  transfers between devices with their start and end apart: 34, of which 17 were waited for; matrix products, arithmetic and copies ran while one was open for 2% of the time, Pallas kernels for 30%

profile of v5, /device:TPU:0, one launch (start us, length us, event | category | flops | bytes accessed | tf_op | source)
XLA Modules:
  0.0 126.3 jit_solution(9957033361557117229)
XLA Ops:
  0.6 1.0 pad_maximum_fusion.2.refs_0_
  1.7 0.1 collective-permute-start.3
  1.8 3.2 %collective-permute-start = (bf16[768,256]{1,0:T(8,128)(2,1)S(1)}, bf16[768,256]{1,0:T(8,128)(2,1)S(1)}, u32[]{:S(2)}, u32[]{:S(2)}) collective-permute-start(bf16[768,256]{1,0:T(8,128)(2,1)S(1)} %pad_maximum_fusion.2.refs_0_), channel_id=1, source_target_pairs={{0,6},{1,7},{2,0},{3,1},{4,2},{5,3},{6,4},{7,5},{8,14},{9,15},{10,... | collective-permute-start | bytes 1179656 | tf_op jit(solution)/shard_map/ppermute | solution.py:30
  4.9 1.9 %collective-permute-start.2 = (bf16[768,256]{1,0:T(8,128)(2,1)S(1)}, bf16[768,256]{1,0:T(8,128)(2,1)S(1)}, u32[]{:S(2)}, u32[]{:S(2)}) collective-permute-start(bf16[768,256]{1,0:T(8,128)(2,1)S(1)} %pad_maximum_fusion.2.refs_0_), channel_id=1, source_target_pairs={{0,8},{1,9},{2,10},{3,11},{4,12},{5,13},{6,14},{7,15},{8,0},{9,1},... | collective-permute-start | bytes 1179656 | tf_op jit(solution)/shard_map/ppermute | solution.py:34
  6.8 0.7 constant_dynamic-slice_fusion
  7.5 5.3 %logits_part.3.refs_7_ = f32[768,2048]{1,0:T(8,128)S(1)} custom-call(s32[32]{0:T(128)S(1)} %get-tuple-element.109.idx, bf16[768,256]{1,0:T(8,128)(2,1)S(1)} %pad_maximum_fusion.2.refs_0_, bf16[768,256]{1,0:T(8,128)(2,1)S(1)} %collective-permute-done.3.refs_1_, bf16[4096,2048]{1,0:T(8,128)(2,1)} %w.7), custom_call_target="tpu_custom_call" | custom-call | tf_op jit(solution)/shard_map/logits_part/pallas_call | solution.py:165
  12.8 1.1 collective-permute-done.refs_0_
  13.9 3.4 %collective-permute-done.1.refs_2_ = bf16[768,256]{1,0:T(8,128)(2,1)S(1)} collective-permute-done((bf16[768,256]{1,0:T(8,128)(2,1)S(1)}, bf16[768,256]{1,0:T(8,128)(2,1)S(1)}, u32[]{:S(2)}, u32[]{:S(2)}) %collective-permute-start.1) | collective-permute-done | bytes 393248 | tf_op jit(solution)/shard_map/ppermute | solution.py:30
  17.3 0.6 collective-permute-start.9
  17.9 0.1 collective-permute-start.8
  18.2 2.0 %collective-permute-start.4 = (bf16[768,256]{1,0:T(8,128)(2,1)S(1)}, bf16[768,256]{1,0:T(8,128)(2,1)S(1)}, u32[]{:S(2)}, u32[]{:S(2)}) collective-permute-start(bf16[768,256]{1,0:T(8,128)(2,1)S(1)} %get-tuple-element.106), channel_id=1, source_target_pairs={{0,6},{1,7},{2,0},{3,1},{4,2},{5,3},{6,4},{7,5},{8,14},{9,15},{10,... | collective-permute-start | bytes 1179656 | tf_op jit(solution)/shard_map/ppermute | solution.py:30
  20.1 0.1 collective-permute-start.5
  20.3 1.9 %collective-permute-start.6 = (bf16[768,256]{1,0:T(8,128)(2,1)S(1)}, bf16[768,256]{1,0:T(8,128)(2,1)S(1)}, u32[]{:S(2)}, u32[]{:S(2)}) collective-permute-start(bf16[768,256]{1,0:T(8,128)(2,1)S(1)} %get-tuple-element.105), channel_id=1, source_target_pairs={{0,8},{1,9},{2,10},{3,11},{4,12},{5,13},{6,14},{7,15},{8,0},{9,1},... | collective-permute-start | bytes 1179656 | tf_op jit(solution)/shard_map/ppermute | solution.py:34
  22.2 8.2 %logits_part.4.refs_7_ = f32[768,2048]{1,0:T(8,128)S(1)} custom-call(s32[32]{0:T(128)S(1)} %get-tuple-element.109.idx, bf16[768,256]{1,0:T(8,128)(2,1)S(1)} %collective-permute-done.refs_0_, bf16[768,256]{1,0:T(8,128)(2,1)S(1)} %collective-permute-done.7.refs_1_, ...), custom_call_target="tpu_custom_call", output_to_operand_aliasing={{}: (8, {})} | custom-call | tf_op jit(solution)/shard_map/logits_part/pallas_call | solution.py:165
  30.4 2.2 %collective-permute-done.5.refs_2_ = bf16[768,256]{1,0:T(8,128)(2,1)S(1)} collective-permute-done((bf16[768,256]{1,0:T(8,128)(2,1)S(1)}, bf16[768,256]{1,0:T(8,128)(2,1)S(1)}, u32[]{:S(2)}, u32[]{:S(2)}) %collective-permute-start.5) | collective-permute-done | bytes 393248 | tf_op jit(solution)/shard_map/ppermute | solution.py:30
  32.6 0.5 collective-permute-start.13
  33.1 1.8 %collective-permute-start.10 = (bf16[384,256]{1,0:T(8,128)(2,1)S(1)}, bf16[384,256]{1,0:T(8,128)(2,1)S(1)}, u32[]{:S(2)}, u32[]{:S(2)}) collective-permute-start(bf16[384,256]{1,0:T(8,128)(2,1)S(1)} %slice.93), channel_id=1, source_target_pairs={{0,6},{1,7},{2,0},{3,1},{4,2},{5,3},{6,4},{7,5},{8,14},{9,15},{10,... | collective-permute-start | bytes 589832 | tf_op jit(solution)/shard_map/ppermute | solution.py:30
  35.0 1.7 %collective-permute-start.11 = (bf16[384,256]{1,0:T(8,128)(2,1)S(1)}, bf16[384,256]{1,0:T(8,128)(2,1)S(1)}, u32[]{:S(2)}, u32[]{:S(2)}) collective-permute-start(bf16[384,256]{1,0:T(8,128)(2,1)S(1)} %slice.94), channel_id=1, source_target_pairs={{0,8},{1,9},{2,10},{3,11},{4,12},{5,13},{6,14},{7,15},{8,0},{9,1},... | collective-permute-start | bytes 589832 | tf_op jit(solution)/shard_map/ppermute | solution.py:34
  36.7 0.1 fusion.6
  36.9 8.4 %logits_part.5 = (f32[768,2048]{1,0:T(8,128)S(1)}, bf16[512,2048]{1,0:T(8,128)(2,1)S(1)}) custom-call(s32[32]{0:T(128)S(1)} %get-tuple-element.109.idx, bf16[768,256]{1,0:T(8,128)(2,1)S(1)} %collective-permute-done.4.refs_0_, bf16[768,256]{1,0:T(8,128)(2,1)S(1)} %collective-permute-done.12.refs_1_, ...), custom_call_target="tpu_custom_call", output_to_operand_aliasing={{0}: (8, {})} | custom-call | tf_op jit(solution)/shard_map/logits_part/pallas_call | solution.py:165
  45.3 0.1 collective-permute-start.15
  45.4 0.5 collective-permute-start.16
  45.9 0.1 fusion.7
  46.1 0.7 collective-permute-done.15.refs_1_
  46.8 0.3 collective-permute-done.16.refs_3_
  47.1 5.1 %logits_pool.1 = (bf16[768,2048]{1,0:T(8,128)(2,1)}, f32[8,2048]{1,0:T(8,128)S(1)}, f32[4,2048]{1,0:T(4,128)S(1)}) custom-call(s32[4]{0:T(128)S(1)} %pad_add_fusion.lens, bf16[384,256]{1,0:T(8,128)(2,1)S(1)} %collective-permute-done.10.refs_0_, bf16[384,256]{1,0:T(8,128)(2,1)S(1)} %collective-permute-done.15.refs_1_, ...), custom_call_target="tpu_custom_call" | custom-call | tf_op jit(solution)/shard_map/logits_pool/pallas_call | solution.py:234
  52.2 2.8 %collective-permute-start.17 = (f32[4,2048]{1,0:T(4,128)S(1)}, f32[4,2048]{1,0:T(4,128)S(1)}, u32[]{:S(2)}, u32[]{:S(2)}) collective-permute-start(f32[4,2048]{1,0:T(4,128)S(1)} %get-tuple-element.61), channel_id=1, source_target_pairs={{0,96},{16,112},{32,0},{48,16},{64,32},{80,48},{96,64},{112,80},{1... | collective-permute-start | bytes 98312 | tf_op jit(solution)/shard_map/ppermute | solution.py:42
  55.1 0.8 collective-permute-start.18
  55.9 0.9 collective-permute-start.19
  56.8 3.6 %collective-permute-done.18 = f32[4,2048]{1,0:T(4,128)S(1)} collective-permute-done((f32[4,2048]{1,0:T(4,128)S(1)}, f32[4,2048]{1,0:T(4,128)S(1)}, u32[]{:S(2)}, u32[]{:S(2)}) %collective-permute-start.18) | collective-permute-done | bytes 32800 | tf_op jit(solution)/shard_map/ppermute | solution.py:42
  60.5 0.5 collective-permute-done.19
  61.0 3.7 %collective-permute-start.20 = (f32[16,2048]{1,0:T(8,128)S(1)}, f32[16,2048]{1,0:T(8,128)S(1)}, u32[]{:S(2)}, u32[]{:S(2)}) collective-permute-start(f32[16,2048]{1,0:T(8,128)S(1)} %pad_maximum_fusion.7.a.pa), channel_id=1, source_target_pairs={{0,16},{16,0},{32,48},{48,32},{64,80},{80,64},{96,112},{112,96},{1... | collective-permute-start | bytes 393224 | tf_op jit(solution)/shard_map/ppermute | solution.py:46
  64.8 0.7 gather_fusion
  65.4 2.2 %collective-permute-done.20.b.pb = f32[16,2048]{1,0:T(8,128)S(1)} collective-permute-done((f32[16,2048]{1,0:T(8,128)S(1)}, f32[16,2048]{1,0:T(8,128)S(1)}, u32[]{:S(2)}, u32[]{:S(2)}) %collective-permute-start.20) | collective-permute-done | bytes 131104 | tf_op jit(solution)/shard_map/ppermute | solution.py:46
  67.6 1.0 gram.1
  68.6 3.5 %all-to-all-start = ((f32[16,8,128]{2,1,0:T(8,128)}), f32[16,8,128]{2,1,0:T(8,128)S(1)}, u32[]{:S(2)}, u32[]{:S(2)}) async-start(f32[16,8,128]{2,1,0:T(8,128)} %gram.1), calls=%async_computation | async-start | bytes 131072 | tf_op jit(solution)/shard_map/all_to_all | solution.py:503
  72.2 6.0 %all-to-all-done.parts = f32[16,8,128]{2,1,0:T(8,128)S(1)} async-done(((f32[16,8,128]{2,1,0:T(8,128)}), f32[16,8,128]{2,1,0:T(8,128)S(1)}, u32[]{:S(2)}, u32[]{:S(2)}) %all-to-all-start) | async-done | bytes 65568 | tf_op jit(solution)/shard_map/all_to_all | solution.py:503
  78.2 5.2 %first_grad.1 = (bf16[768,2048]{1,0:T(8,128)(2,1)S(1)}, f32[8,128]{1,0:T(8,128)S(1)}, f32[768,256]{1,0:T(8,128)S(1)}, bf16[768,256]{1,0:T(8,128)(2,1)S(1)}, bf16[512,2048]{1,0:T(8,128)(2,1)S(1)}) custom-call(s32[32]{0:T(128)S(1)} %get-tuple-element.109.idx, f32[16,8,128]{2,1,0:T(8,128)S(1)} %all-to-all-done.parts, f32[16,2048]{1,0:T(8,128)S(1)} %pad_maximum_fusion.7.a.pa, ...), custom_call_target="tpu_custom_call" | custom-call | tf_op jit(solution)/shard_map/first_grad/pallas_call | solution.py:343
  83.4 0.2 collective-permute-start.21
  83.6 1.6 %collective-permute-done.21 = bf16[768,256]{1,0:T(8,128)(2,1)S(1)} collective-permute-done((bf16[768,256]{1,0:T(8,128)(2,1)S(1)}, bf16[768,256]{1,0:T(8,128)(2,1)S(1)}, u32[]{:S(2)}, u32[]{:S(2)}) %collective-permute-start.21) | collective-permute-done | bytes 393248 | tf_op jit(solution)/shard_map/ppermute | solution.py:38
  85.3 0.6 collective-permute-start.22
  86.0 0.7 collective-permute-start.23
  86.6 6.5 %grad_part.3 = (f32[2304,256]{1,0:T(8,128)S(1)}, bf16[2304,256]{1,0:T(8,128)(2,1)S(1)}, bf16[512,2048]{1,0:T(8,128)(2,1)S(1)}) custom-call(s32[32]{0:T(128)S(1)} %get-tuple-element.109.idx, bf16[768,2048]{1,0:T(8,128)(2,1)S(1)} %get-tuple-element.79.dl, bf16[4096,2048]{1,0:T(8,128)(2,1)} %w.7, bf16[512,2048]{1,0:T(8,128)(2,1)S(1)} %get-tuple-element.69.refs_0_), custom_call_target="tpu_custom_call" | custom-call | tf_op jit(solution)/shard_map/grad_part/pallas_call | solution.py:398
  93.3 0.3 collective-permute-done.22.refs_1_
  93.6 0.2 add_arrived.3
  93.8 2.3 %collective-permute-done.24 = bf16[2304,256]{1,0:T(8,128)(2,1)S(1)} collective-permute-done((bf16[2304,256]{1,0:T(8,128)(2,1)S(1)}, bf16[2304,256]{1,0:T(8,128)(2,1)S(1)}, u32[]{:S(2)}, u32[]{:S(2)}) %collective-permute-start.24) | collective-permute-done | bytes 1179680 | tf_op jit(solution)/shard_map/ppermute | solution.py:38
  96.1 0.3 fusion.3
  96.6 0.7 collective-permute-start.25
  97.3 2.6 %collective-permute-start.26 = (bf16[768,256]{1,0:T(8,128)(2,1)S(1)}, bf16[768,256]{1,0:T(8,128)(2,1)S(1)}, u32[]{:S(2)}, u32[]{:S(2)}) collective-permute-start(bf16[768,256]{1,0:T(8,128)(2,1)S(1)} %pad_maximum_fusion.5), channel_id=1, source_target_pairs={{0,6},{1,7},{2,0},{3,1},{4,2},{5,3},{6,4},{7,5},{8,14},{9,15},{10,... | collective-permute-start | bytes 1179656 | tf_op jit(solution)/shard_map/ppermute | solution.py:30
  99.9 1.4 %collective-permute-start.27 = (bf16[768,256]{1,0:T(8,128)(2,1)S(1)}, bf16[768,256]{1,0:T(8,128)(2,1)S(1)}, u32[]{:S(2)}, u32[]{:S(2)}) collective-permute-start(bf16[768,256]{1,0:T(8,128)(2,1)S(1)} %pad_maximum_fusion.6), channel_id=1, source_target_pairs={{0,8},{1,9},{2,10},{3,11},{4,12},{5,13},{6,14},{7,15},{8,0},{9,1},... | collective-permute-start | bytes 1179656 | tf_op jit(solution)/shard_map/ppermute | solution.py:34
  101.3 6.7 %grad_part.4 = (f32[2304,256]{1,0:T(8,128)S(1)}, bf16[2304,256]{1,0:T(8,128)(2,1)S(1)}, bf16[512,2048]{1,0:T(8,128)(2,1)S(1)}) custom-call(s32[32]{0:T(128)S(1)} %get-tuple-element.109.idx, bf16[768,2048]{1,0:T(8,128)(2,1)S(1)} %get-tuple-element.79.dl, bf16[4096,2048]{1,0:T(8,128)(2,1)} %w.7, bf16[512,2048]{1,0:T(8,128)(2,1)S(1)} %get-tuple-element.73.refs_0_), custom_call_target="tpu_custom_call" | custom-call | tf_op jit(solution)/shard_map/grad_part/pallas_call | solution.py:398
  108.2 0.9 collective-permute-done.25.refs_1_
  109.1 1.5 %collective-permute-done.27.refs_3_ = bf16[768,256]{1,0:T(8,128)(2,1)S(1)} collective-permute-done((bf16[768,256]{1,0:T(8,128)(2,1)S(1)}, bf16[768,256]{1,0:T(8,128)(2,1)S(1)}, u32[]{:S(2)}, u32[]{:S(2)}) %collective-permute-start.27) | collective-permute-done | bytes 393248 | tf_op jit(solution)/shard_map/ppermute | solution.py:34
  110.5 0.4 add_arrived.4
  111.0 0.3 fusion
  111.4 3.2 %collective-permute-start.30 = (bf16[768,256]{1,0:T(8,128)(2,1)S(1)}, bf16[768,256]{1,0:T(8,128)(2,1)S(1)}, u32[]{:S(2)}, u32[]{:S(2)}) collective-permute-start(bf16[768,256]{1,0:T(8,128)(2,1)S(1)} %get-tuple-element.83), channel_id=1, source_target_pairs={{0,6},{1,7},{2,0},{3,1},{4,2},{5,3},{6,4},{7,5},{8,14},{9,15},{10,... | collective-permute-start | bytes 1179656 | tf_op jit(solution)/shard_map/ppermute | solution.py:30
  114.6 1.3 %collective-permute-start.31 = (bf16[768,256]{1,0:T(8,128)(2,1)S(1)}, bf16[768,256]{1,0:T(8,128)(2,1)S(1)}, u32[]{:S(2)}, u32[]{:S(2)}) collective-permute-start(bf16[768,256]{1,0:T(8,128)(2,1)S(1)} %get-tuple-element.84), channel_id=1, source_target_pairs={{0,8},{1,9},{2,10},{3,11},{4,12},{5,13},{6,14},{7,15},{8,0},{9,1},... | collective-permute-start | bytes 1179656 | tf_op jit(solution)/shard_map/ppermute | solution.py:34
  116.0 0.6 slice_reduce_fusion
  116.6 2.5 %grad_part.5 = (f32[768,256]{1,0:T(8,128)S(1)}, bf16[768,256]{1,0:T(8,128)(2,1)S(1)}) custom-call(s32[32]{0:T(128)S(1)} %get-tuple-element.109.idx, bf16[768,2048]{1,0:T(8,128)(2,1)S(1)} %get-tuple-element.79.dl, bf16[4096,2048]{1,0:T(8,128)(2,1)} %w.7, bf16[512,2048]{1,0:T(8,128)(2,1)S(1)} %get-tuple-element.80.refs_0_), custom_call_target="tpu_custom_call" | custom-call | tf_op jit(solution)/shard_map/grad_part/pallas_call | solution.py:398
  119.1 0.1 collective-permute-start.32
  119.2 4.6 %collective-permute-done.29.refs_1_ = bf16[768,256]{1,0:T(8,128)(2,1)S(1)} collective-permute-done((bf16[768,256]{1,0:T(8,128)(2,1)S(1)}, bf16[768,256]{1,0:T(8,128)(2,1)S(1)}, u32[]{:S(2)}, u32[]{:S(2)}) %collective-permute-start.29) | collective-permute-done | bytes 393248 | tf_op jit(solution)/shard_map/ppermute | solution.py:30
  123.8 1.5 %collective-permute-done.31.refs_3_ = bf16[768,256]{1,0:T(8,128)(2,1)S(1)} collective-permute-done((bf16[768,256]{1,0:T(8,128)(2,1)S(1)}, bf16[768,256]{1,0:T(8,128)(2,1)S(1)}, u32[]{:S(2)}, u32[]{:S(2)}) %collective-permute-start.31) | collective-permute-done | bytes 393248 | tf_op jit(solution)/shard_map/ppermute | solution.py:34
  125.2 0.3 add_arrived.5.refs_0_
  125.5 0.8 add_last.1
  (52 shorter events, 1.2 us)
Async XLA Ops:
  0.6 64.1 %copy-start = (s32[16]{0:T(128)S(1)}, s32[16]{0:T(128)}, u32[]{:S(2)}) copy-start(s32[16]{0:T(128)} %param.12) | copy-start | bytes 196
  1.7 5.9 %collective-permute-start.3 = (bf16[768,256]{1,0:T(8,128)(2,1)S(1)}, bf16[768,256]{1,0:T(8,128)(2,1)S(1)}, u32[]{:S(2)}, u32[]{:S(2)}) collective-permute-start(bf16[768,256]{1,0:T(8,128)(2,1)S(1)} %pad_maximum_fusion.2.refs_0_), channel_id=1, source_target_pairs={{0,1},{1,0},{2,3},{3,2},{4,5},{5,4},{6,7},{7,6},{8,9},{9,8},{10,11... | collective-permute-start | bytes 1179656 | tf_op jit(solution)/shard_map/ppermute | solution.py:38
  1.8 12.1 %collective-permute-start = (bf16[768,256]{1,0:T(8,128)(2,1)S(1)}, bf16[768,256]{1,0:T(8,128)(2,1)S(1)}, u32[]{:S(2)}, u32[]{:S(2)}) collective-permute-start(bf16[768,256]{1,0:T(8,128)(2,1)S(1)} %pad_maximum_fusion.2.refs_0_), channel_id=1, source_target_pairs={{0,6},{1,7},{2,0},{3,1},{4,2},{5,3},{6,4},{7,5},{8,14},{9,15},{10,... | collective-permute-start | bytes 1179656 | tf_op jit(solution)/shard_map/ppermute | solution.py:30
  4.9 12.4 %collective-permute-start.1 = (bf16[768,256]{1,0:T(8,128)(2,1)S(1)}, bf16[768,256]{1,0:T(8,128)(2,1)S(1)}, u32[]{:S(2)}, u32[]{:S(2)}) collective-permute-start(bf16[768,256]{1,0:T(8,128)(2,1)S(1)} %pad_maximum_fusion.2.refs_0_), channel_id=1, source_target_pairs={{0,2},{1,3},{2,4},{3,5},{4,6},{5,7},{6,0},{7,1},{8,10},{9,11},{10,... | collective-permute-start | bytes 1179656 | tf_op jit(solution)/shard_map/ppermute | solution.py:30
  4.9 12.4 %collective-permute-start.2 = (bf16[768,256]{1,0:T(8,128)(2,1)S(1)}, bf16[768,256]{1,0:T(8,128)(2,1)S(1)}, u32[]{:S(2)}, u32[]{:S(2)}) collective-permute-start(bf16[768,256]{1,0:T(8,128)(2,1)S(1)} %pad_maximum_fusion.2.refs_0_), channel_id=1, source_target_pairs={{0,8},{1,9},{2,10},{3,11},{4,12},{5,13},{6,14},{7,15},{8,0},{9,1},... | collective-permute-start | bytes 1179656 | tf_op jit(solution)/shard_map/ppermute | solution.py:34
  17.3 2.9 %collective-permute-start.7 = (bf16[768,256]{1,0:T(8,128)(2,1)S(1)}, bf16[768,256]{1,0:T(8,128)(2,1)S(1)}, u32[]{:S(2)}, u32[]{:S(2)}) collective-permute-start(bf16[768,256]{1,0:T(8,128)(2,1)S(1)} %collective-permute-done.refs_0_), channel_id=1, source_target_pairs={{0,1},{1,0},{2,3},{3,2},{4,5},{5,4},{6,7},{7,6},{8,9},{9,8},{10,11... | collective-permute-start | bytes 1179656 | tf_op jit(solution)/shard_map/ppermute | solution.py:38
  17.3 4.8 %collective-permute-start.9 = (bf16[768,256]{1,0:T(8,128)(2,1)S(1)}, bf16[768,256]{1,0:T(8,128)(2,1)S(1)}, u32[]{:S(2)}, u32[]{:S(2)}) collective-permute-start(bf16[768,256]{1,0:T(8,128)(2,1)S(1)} %collective-permute-done.2.refs_4_), channel_id=1, source_target_pairs={{0,1},{1,0},{2,3},{3,2},{4,5},{5,4},{6,7},{7,6},{8,9},{9,8},{10,11... | collective-permute-start | bytes 1179656 | tf_op jit(solution)/shard_map/ppermute | solution.py:38
  17.9 4.2 %collective-permute-start.8 = (bf16[768,256]{1,0:T(8,128)(2,1)S(1)}, bf16[768,256]{1,0:T(8,128)(2,1)S(1)}, u32[]{:S(2)}, u32[]{:S(2)}) collective-permute-start(bf16[768,256]{1,0:T(8,128)(2,1)S(1)} %collective-permute-done.1.refs_2_), channel_id=1, source_target_pairs={{0,1},{1,0},{2,3},{3,2},{4,5},{5,4},{6,7},{7,6},{8,9},{9,8},{10,11... | collective-permute-start | bytes 1179656 | tf_op jit(solution)/shard_map/ppermute | solution.py:38
  18.2 12.2 %collective-permute-start.4 = (bf16[768,256]{1,0:T(8,128)(2,1)S(1)}, bf16[768,256]{1,0:T(8,128)(2,1)S(1)}, u32[]{:S(2)}, u32[]{:S(2)}) collective-permute-start(bf16[768,256]{1,0:T(8,128)(2,1)S(1)} %get-tuple-element.106), channel_id=1, source_target_pairs={{0,6},{1,7},{2,0},{3,1},{4,2},{5,3},{6,4},{7,5},{8,14},{9,15},{10,... | collective-permute-start | bytes 1179656 | tf_op jit(solution)/shard_map/ppermute | solution.py:30
  20.1 12.4 %collective-permute-start.5 = (bf16[768,256]{1,0:T(8,128)(2,1)S(1)}, bf16[768,256]{1,0:T(8,128)(2,1)S(1)}, u32[]{:S(2)}, u32[]{:S(2)}) collective-permute-start(bf16[768,256]{1,0:T(8,128)(2,1)S(1)} %get-tuple-element.107), channel_id=1, source_target_pairs={{0,2},{1,3},{2,4},{3,5},{4,6},{5,7},{6,0},{7,1},{8,10},{9,11},{10,... | collective-permute-start | bytes 1179656 | tf_op jit(solution)/shard_map/ppermute | solution.py:30
  20.3 16.4 %copy-start.2 = (s32[2,256]{1,0:T(2,128)S(1)}, s32[2,256]{1,0:T(2,128)}, u32[]{:S(2)}) copy-start(s32[2,256]{1,0:T(2,128)} %param.11) | copy-start | bytes 6148
  20.3 12.3 %collective-permute-start.6 = (bf16[768,256]{1,0:T(8,128)(2,1)S(1)}, bf16[768,256]{1,0:T(8,128)(2,1)S(1)}, u32[]{:S(2)}, u32[]{:S(2)}) collective-permute-start(bf16[768,256]{1,0:T(8,128)(2,1)S(1)} %get-tuple-element.105), channel_id=1, source_target_pairs={{0,8},{1,9},{2,10},{3,11},{4,12},{5,13},{6,14},{7,15},{8,0},{9,1},... | collective-permute-start | bytes 1179656 | tf_op jit(solution)/shard_map/ppermute | solution.py:34
  32.6 4.2 %collective-permute-start.12 = (bf16[768,256]{1,0:T(8,128)(2,1)S(1)}, bf16[768,256]{1,0:T(8,128)(2,1)S(1)}, u32[]{:S(2)}, u32[]{:S(2)}) collective-permute-start(bf16[768,256]{1,0:T(8,128)(2,1)S(1)} %collective-permute-done.4.refs_0_), channel_id=1, source_target_pairs={{0,1},{1,0},{2,3},{3,2},{4,5},{5,4},{6,7},{7,6},{8,9},{9,8},{10,11... | collective-permute-start | bytes 1179656 | tf_op jit(solution)/shard_map/ppermute | solution.py:38
  32.6 4.2 %collective-permute-start.13 = (bf16[768,256]{1,0:T(8,128)(2,1)S(1)}, bf16[768,256]{1,0:T(8,128)(2,1)S(1)}, u32[]{:S(2)}, u32[]{:S(2)}) collective-permute-start(bf16[768,256]{1,0:T(8,128)(2,1)S(1)} %collective-permute-done.5.refs_2_), channel_id=1, source_target_pairs={{0,1},{1,0},{2,3},{3,2},{4,5},{5,4},{6,7},{7,6},{8,9},{9,8},{10,11... | collective-permute-start | bytes 1179656 | tf_op jit(solution)/shard_map/ppermute | solution.py:38
  33.1 3.8 %collective-permute-start.14 = (bf16[768,256]{1,0:T(8,128)(2,1)S(1)}, bf16[768,256]{1,0:T(8,128)(2,1)S(1)}, u32[]{:S(2)}, u32[]{:S(2)}) collective-permute-start(bf16[768,256]{1,0:T(8,128)(2,1)S(1)} %collective-permute-done.6.refs_4_), channel_id=1, source_target_pairs={{0,1},{1,0},{2,3},{3,2},{4,5},{5,4},{6,7},{7,6},{8,9},{9,8},{10,11... | collective-permute-start | bytes 1179656 | tf_op jit(solution)/shard_map/ppermute | solution.py:38
  33.1 12.1 %collective-permute-start.10 = (bf16[384,256]{1,0:T(8,128)(2,1)S(1)}, bf16[384,256]{1,0:T(8,128)(2,1)S(1)}, u32[]{:S(2)}, u32[]{:S(2)}) collective-permute-start(bf16[384,256]{1,0:T(8,128)(2,1)S(1)} %slice.93), channel_id=1, source_target_pairs={{0,6},{1,7},{2,0},{3,1},{4,2},{5,3},{6,4},{7,5},{8,14},{9,15},{10,... | collective-permute-start | bytes 589832 | tf_op jit(solution)/shard_map/ppermute | solution.py:30
  35.0 10.3 %collective-permute-start.11 = (bf16[384,256]{1,0:T(8,128)(2,1)S(1)}, bf16[384,256]{1,0:T(8,128)(2,1)S(1)}, u32[]{:S(2)}, u32[]{:S(2)}) collective-permute-start(bf16[384,256]{1,0:T(8,128)(2,1)S(1)} %slice.94), channel_id=1, source_target_pairs={{0,8},{1,9},{2,10},{3,11},{4,12},{5,13},{6,14},{7,15},{8,0},{9,1},... | collective-permute-start | bytes 589832 | tf_op jit(solution)/shard_map/ppermute | solution.py:34
  36.8 9.1 %copy-start.3 = (s32[2,128]{1,0:T(2,128)S(1)}, s32[2,128]{1,0:T(2,128)}, u32[]{:S(2)}) copy-start(s32[2,128]{1,0:T(2,128)} %param.10) | copy-start | bytes 3076
  45.3 1.5 %collective-permute-start.15 = (bf16[384,256]{1,0:T(8,128)(2,1)S(1)}, bf16[384,256]{1,0:T(8,128)(2,1)S(1)}, u32[]{:S(2)}, u32[]{:S(2)}) collective-permute-start(bf16[384,256]{1,0:T(8,128)(2,1)S(1)} %collective-permute-done.10.refs_0_), channel_id=1, source_target_pairs={{0,1},{1,0},{2,3},{3,2},{4,5},{5,4},{6,7},{7,6},{8,9},{9,8},{10,11... | collective-permute-start | bytes 589832 | tf_op jit(solution)/shard_map/ppermute | solution.py:38
  45.4 1.7 %collective-permute-start.16 = (bf16[384,256]{1,0:T(8,128)(2,1)S(1)}, bf16[384,256]{1,0:T(8,128)(2,1)S(1)}, u32[]{:S(2)}, u32[]{:S(2)}) collective-permute-start(bf16[384,256]{1,0:T(8,128)(2,1)S(1)} %collective-permute-done.11.refs_2_), channel_id=1, source_target_pairs={{0,1},{1,0},{2,3},{3,2},{4,5},{5,4},{6,7},{7,6},{8,9},{9,8},{10,11... | collective-permute-start | bytes 589832 | tf_op jit(solution)/shard_map/ppermute | solution.py:38
  52.2 4.6 %collective-permute-start.17 = (f32[4,2048]{1,0:T(4,128)S(1)}, f32[4,2048]{1,0:T(4,128)S(1)}, u32[]{:S(2)}, u32[]{:S(2)}) collective-permute-start(f32[4,2048]{1,0:T(4,128)S(1)} %get-tuple-element.61), channel_id=1, source_target_pairs={{0,96},{16,112},{32,0},{48,16},{64,32},{80,48},{96,64},{112,80},{1... | collective-permute-start | bytes 98312 | tf_op jit(solution)/shard_map/ppermute | solution.py:42
  55.1 5.4 %collective-permute-start.18 = (f32[4,2048]{1,0:T(4,128)S(1)}, f32[4,2048]{1,0:T(4,128)S(1)}, u32[]{:S(2)}, u32[]{:S(2)}) collective-permute-start(f32[4,2048]{1,0:T(4,128)S(1)} %get-tuple-element.61), channel_id=1, source_target_pairs={{0,64},{16,80},{32,96},{48,112},{64,0},{80,16},{96,32},{112,48},{1... | collective-permute-start | bytes 98312 | tf_op jit(solution)/shard_map/ppermute | solution.py:42
  55.9 5.1 %collective-permute-start.19 = (f32[4,2048]{1,0:T(4,128)S(1)}, f32[4,2048]{1,0:T(4,128)S(1)}, u32[]{:S(2)}, u32[]{:S(2)}) collective-permute-start(f32[4,2048]{1,0:T(4,128)S(1)} %get-tuple-element.61), channel_id=1, source_target_pairs={{0,32},{16,48},{32,64},{48,80},{64,96},{80,112},{96,0},{112,16},{1... | collective-permute-start | bytes 98312 | tf_op jit(solution)/shard_map/ppermute | solution.py:42
  61.0 6.6 %collective-permute-start.20 = (f32[16,2048]{1,0:T(8,128)S(1)}, f32[16,2048]{1,0:T(8,128)S(1)}, u32[]{:S(2)}, u32[]{:S(2)}) collective-permute-start(f32[16,2048]{1,0:T(8,128)S(1)} %pad_maximum_fusion.7.a.pa), channel_id=1, source_target_pairs={{0,16},{16,0},{32,48},{48,32},{64,80},{80,64},{96,112},{112,96},{1... | collective-permute-start | bytes 393224 | tf_op jit(solution)/shard_map/ppermute | solution.py:46
  68.6 9.6 %all-to-all-start = ((f32[16,8,128]{2,1,0:T(8,128)}), f32[16,8,128]{2,1,0:T(8,128)S(1)}, u32[]{:S(2)}, u32[]{:S(2)}) async-start(f32[16,8,128]{2,1,0:T(8,128)} %gram.1), calls=%async_computation | async-start | bytes 131072 | tf_op jit(solution)/shard_map/all_to_all | solution.py:503
  83.4 1.8 %collective-permute-start.21 = (bf16[768,256]{1,0:T(8,128)(2,1)S(1)}, bf16[768,256]{1,0:T(8,128)(2,1)S(1)}, u32[]{:S(2)}, u32[]{:S(2)}) collective-permute-start(bf16[768,256]{1,0:T(8,128)(2,1)S(1)} %get-tuple-element.67), channel_id=1, source_target_pairs={{0,1},{1,0},{2,3},{3,2},{4,5},{5,4},{6,7},{7,6},{8,9},{9,8},{10,11... | collective-permute-start | bytes 1179656 | tf_op jit(solution)/shard_map/ppermute | solution.py:38
  85.3 8.2 %collective-permute-start.22 = (bf16[384,256]{1,0:T(8,128)(2,1)S(1)}, bf16[384,256]{1,0:T(8,128)(2,1)S(1)}, u32[]{:S(2)}, u32[]{:S(2)}) collective-permute-start(bf16[384,256]{1,0:T(8,128)(2,1)S(1)} %get-tuple-element.102), channel_id=1, source_target_pairs={{0,2},{1,3},{2,4},{3,5},{4,6},{5,7},{6,0},{7,1},{8,10},{9,11},{10,... | collective-permute-start | bytes 589832 | tf_op jit(solution)/shard_map/ppermute | solution.py:30
  86.0 7.6 %collective-permute-start.23 = (bf16[384,256]{1,0:T(8,128)(2,1)S(1)}, bf16[384,256]{1,0:T(8,128)(2,1)S(1)}, u32[]{:S(2)}, u32[]{:S(2)}) collective-permute-start(bf16[384,256]{1,0:T(8,128)(2,1)S(1)} %get-tuple-element.101), channel_id=1, source_target_pairs={{0,8},{1,9},{2,10},{3,11},{4,12},{5,13},{6,14},{7,15},{8,0},{9,1},... | collective-permute-start | bytes 589832 | tf_op jit(solution)/shard_map/ppermute | solution.py:34
  93.2 2.9 %collective-permute-start.24 = (bf16[2304,256]{1,0:T(8,128)(2,1)S(1)}, bf16[2304,256]{1,0:T(8,128)(2,1)S(1)}, u32[]{:S(2)}, u32[]{:S(2)}) collective-permute-start(bf16[2304,256]{1,0:T(8,128)(2,1)S(1)} %get-tuple-element.71), channel_id=1, source_target_pairs={{0,1},{1,0},{2,3},{3,2},{4,5},{5,4},{6,7},{7,6},{8,9},{9,8},{10,11... | collective-permute-start | bytes 3538952 | tf_op jit(solution)/shard_map/ppermute | solution.py:38
  96.6 12.4 %collective-permute-start.25 = (bf16[768,256]{1,0:T(8,128)(2,1)S(1)}, bf16[768,256]{1,0:T(8,128)(2,1)S(1)}, u32[]{:S(2)}, u32[]{:S(2)}) collective-permute-start(bf16[768,256]{1,0:T(8,128)(2,1)S(1)} %pad_maximum_fusion.4), channel_id=1, source_target_pairs={{0,2},{1,3},{2,4},{3,5},{4,6},{5,7},{6,0},{7,1},{8,10},{9,11},{10,... | collective-permute-start | bytes 1179656 | tf_op jit(solution)/shard_map/ppermute | solution.py:30
  97.3 11.8 %collective-permute-start.26 = (bf16[768,256]{1,0:T(8,128)(2,1)S(1)}, bf16[768,256]{1,0:T(8,128)(2,1)S(1)}, u32[]{:S(2)}, u32[]{:S(2)}) collective-permute-start(bf16[768,256]{1,0:T(8,128)(2,1)S(1)} %pad_maximum_fusion.5), channel_id=1, source_target_pairs={{0,6},{1,7},{2,0},{3,1},{4,2},{5,3},{6,4},{7,5},{8,14},{9,15},{10,... | collective-permute-start | bytes 1179656 | tf_op jit(solution)/shard_map/ppermute | solution.py:30
  99.9 10.6 %collective-permute-start.27 = (bf16[768,256]{1,0:T(8,128)(2,1)S(1)}, bf16[768,256]{1,0:T(8,128)(2,1)S(1)}, u32[]{:S(2)}, u32[]{:S(2)}) collective-permute-start(bf16[768,256]{1,0:T(8,128)(2,1)S(1)} %pad_maximum_fusion.6), channel_id=1, source_target_pairs={{0,8},{1,9},{2,10},{3,11},{4,12},{5,13},{6,14},{7,15},{8,0},{9,1},... | collective-permute-start | bytes 1179656 | tf_op jit(solution)/shard_map/ppermute | solution.py:34
  108.1 2.9 %collective-permute-start.28 = (bf16[2304,256]{1,0:T(8,128)(2,1)S(1)}, bf16[2304,256]{1,0:T(8,128)(2,1)S(1)}, u32[]{:S(2)}, u32[]{:S(2)}) collective-permute-start(bf16[2304,256]{1,0:T(8,128)(2,1)S(1)} %get-tuple-element.78), channel_id=1, source_target_pairs={{0,1},{1,0},{2,3},{3,2},{4,5},{5,4},{6,7},{7,6},{8,9},{9,8},{10,11... | collective-permute-start | bytes 3538952 | tf_op jit(solution)/shard_map/ppermute | solution.py:38
  111.3 12.4 %collective-permute-start.29 = (bf16[768,256]{1,0:T(8,128)(2,1)S(1)}, bf16[768,256]{1,0:T(8,128)(2,1)S(1)}, u32[]{:S(2)}, u32[]{:S(2)}) collective-permute-start(bf16[768,256]{1,0:T(8,128)(2,1)S(1)} %get-tuple-element.82), channel_id=1, source_target_pairs={{0,2},{1,3},{2,4},{3,5},{4,6},{5,7},{6,0},{7,1},{8,10},{9,11},{10,... | collective-permute-start | bytes 1179656 | tf_op jit(solution)/shard_map/ppermute | solution.py:30
  111.4 12.4 %collective-permute-start.30 = (bf16[768,256]{1,0:T(8,128)(2,1)S(1)}, bf16[768,256]{1,0:T(8,128)(2,1)S(1)}, u32[]{:S(2)}, u32[]{:S(2)}) collective-permute-start(bf16[768,256]{1,0:T(8,128)(2,1)S(1)} %get-tuple-element.83), channel_id=1, source_target_pairs={{0,6},{1,7},{2,0},{3,1},{4,2},{5,3},{6,4},{7,5},{8,14},{9,15},{10,... | collective-permute-start | bytes 1179656 | tf_op jit(solution)/shard_map/ppermute | solution.py:30
  114.6 10.6 %collective-permute-start.31 = (bf16[768,256]{1,0:T(8,128)(2,1)S(1)}, bf16[768,256]{1,0:T(8,128)(2,1)S(1)}, u32[]{:S(2)}, u32[]{:S(2)}) collective-permute-start(bf16[768,256]{1,0:T(8,128)(2,1)S(1)} %get-tuple-element.84), channel_id=1, source_target_pairs={{0,8},{1,9},{2,10},{3,11},{4,12},{5,13},{6,14},{7,15},{8,0},{9,1},... | collective-permute-start | bytes 1179656 | tf_op jit(solution)/shard_map/ppermute | solution.py:34
  119.1 6.4 %collective-permute-start.32 = (bf16[768,256]{1,0:T(8,128)(2,1)S(1)}, bf16[768,256]{1,0:T(8,128)(2,1)S(1)}, u32[]{:S(2)}, u32[]{:S(2)}) collective-permute-start(bf16[768,256]{1,0:T(8,128)(2,1)S(1)} %get-tuple-element.85), channel_id=1, source_target_pairs={{0,1},{1,0},{2,3},{3,2},{4,5},{5,4},{6,7},{7,6},{8,9},{9,8},{10,11... | collective-permute-start | bytes 1179656 | tf_op jit(solution)/shard_map/ppermute | solution.py:38
  125.2 1.1 copy-start.1
